TPU v7x, 32 devices: a whole 2x2x4 slice. The times are simulated.
32 devices in a mesh: leaf: 32 (over z, y, x, core).
Axes of the slice: x: 2, y: 2, z: 4, core: 2. Of those that a mesh axis runs over, the one named last changes fastest.
Arguments:
- vectors: float32 [32, 512, 128], P('leaf'), may hold values from -6 to 6
- points: float32 [32, 3, 512], P('leaf')
- leaf_basis: float32 [32, 512, 128], P('leaf'), may hold values from -0.25 to 0.25
- transfer_leaf: float32 [32, 128, 128], P('leaf'), may hold values from -0.5 to 0.5
- transfer_pair: float32 [2048, 128], P('leaf'), may hold values from -0.5 to 0.5
- transfer_quad: float32 [1024, 128], P('leaf'), may hold values from -0.5 to 0.5
- skel_leaf: float32 [32, 3, 128], P('leaf')
- skel_pair: float32 [16, 3, 128], replicated
- skel_quad: float32 [8, 3, 128], replicated
- skel_top: float32 [4, 3, 128], replicated
- near_list: int32 [32, 16], P('leaf'), may hold values from -1 to 31, as said below
- far_leaf: int32 [32, 8], P('leaf'), may hold values from -1 to 31, as said below
- far_pair: int32 [16, 8], replicated, may hold values from -1 to 15, as said below
- far_quad: int32 [8, 8], replicated, may hold values from -1 to 7, as said below
- far_top: int32 [4, 8], replicated, may hold values from -1 to 3, as said below
Outputs:
- product: float32 [32, 512, 128], P('leaf')
Inputs may be any that keep to these rules, and one draw needn't show every extreme that they name: `near_list`: entry 0 of row l is l; the other entries are distinct leaves within 8 of l, or -1 for an unused slot. `far_leaf`: distinct leaves within 8 of the row's leaf, none of them in that leaf's row of near_list, or -1 for an unused slot. `far_pair`: distinct clusters within 4 of the row's cluster and other than it, or -1 for an unused slot. `far_quad`: distinct clusters within 4 of the row's cluster and other than it, or -1 for an unused slot. `far_top`: distinct top clusters other than the row's cluster, or -1 for an unused slot.
All inputs are finite; a program needn't handle non-finite values.
Results may differ from a plain program's by a relative error of at most 0.0003.
Values sent between devices are 32-bit elements; how exact they have to be, the bound alone decides.
No kernel may reach another device: no remote copies, remote signals or barrier semaphores. Data moves between devices by JAX's collectives and lax.ppermute only.
A program may use at most 64 MiB of HBM per device.

v0:
```python
import jax
import jax.numpy as jnp
from jax import lax
from jax.sharding import PartitionSpec as P

REACH = 8
FAR_REACH = 4


INV_FOUR_PI = 0.07957747154594767
DELTA_SQ = 0.01
HIGHEST = lax.Precision.HIGHEST


def from_partner(value, axis, bit):
    mask = 2**bit
    pairs = [(source, source ^ mask) for source in range(lax.axis_size(axis))]
    return lax.ppermute(value, axis, pairs)


def from_behind(block, axis, distance):
    devices = range(lax.axis_size(axis))
    route = [(i - distance, i) for i in devices if i - distance in devices]
    return lax.ppermute(block, axis, route)


def kernel_block(left_pts, right_pts):
    distance = jnp.zeros((left_pts.shape[1], right_pts.shape[1]), jnp.float32)
    for axis_id in range(3):
        offset_gap = left_pts[axis_id][:, None] - right_pts[axis_id][None, :]
        distance = distance + offset_gap * offset_gap
    return INV_FOUR_PI * lax.rsqrt(distance + DELTA_SQ)


def transposed_dot(matrix, values):
    return lax.dot_general(matrix, values, (((0,), (0,)), ((), ())), precision=HIGHEST)


def listed_sum(own_coords, entries, fetcher, width):

    def advance(running, partner):
        coords, values = fetcher(jnp.maximum(partner, 0))
        contrib = jnp.dot(kernel_block(own_coords, coords), values, precision=HIGHEST)
        return (running + jnp.where(partner >= 0, contrib, 0.0), None)

    start_value = jnp.zeros((own_coords.shape[1], width), jnp.float32)
    result, _ = lax.scan(advance, start_value, entries)
    return result


def pair_total(partial_value, levels):
    for bit_index in range(levels):
        partial_value = partial_value + from_partner(partial_value, "leaf", bit_index)
    return partial_value


def join_rows(block, levels, device):
    for bit_index in range(levels):
        other = from_partner(block, "leaf", bit_index)
        upper = device // 2**bit_index % 2
        block = jnp.where(
            upper == 0, jnp.concatenate([block, other], 0), jnp.concatenate([other, block], 0)
        )
    return block


def near_window(shipped):
    gathered = []
    for distance in range(-REACH, REACH + 1):
        if distance == 0:
            gathered.append(shipped)
        else:
            gathered.append(from_behind(shipped, "leaf", -distance))
    return jnp.stack(gathered)


def coef_window(shipped):
    gathered = []
    for distance in range(-REACH, REACH + 1):
        if distance == 0:
            gathered.append(shipped)
        else:
            gathered.append(from_behind(shipped, "leaf", -distance))
    return jnp.stack(gathered)


def partner_stack(coefs, stride):
    gathered = []
    for offset in list(range(-FAR_REACH, 0)) + list(range(1, FAR_REACH + 1)):
        gathered.append(from_behind(coefs, "leaf", -offset * stride))
    stacked = jnp.stack(gathered)

    def slot_of(distance):
        return distance + FAR_REACH - (distance > 0).astype(jnp.int32)

    return (stacked, slot_of)


def middle_level(coefs, skeletons, lists, transfer_rows, above, stride, device):
    width = coefs.shape[1]
    rank_rows = coefs.shape[0] // stride
    cluster = device // stride
    member = device % stride
    own_full = lax.dynamic_index_in_dim(skeletons, cluster, 0, keepdims=False)
    own_coords = lax.dynamic_slice_in_dim(own_full, member * rank_rows, rank_rows, 1)
    stacked, slot_of = partner_stack(coefs, stride)

    def fetcher(partner):
        coords = lax.dynamic_index_in_dim(skeletons, partner, 0, keepdims=False)
        position = jnp.clip(slot_of(partner - cluster), 0, stacked.shape[0] - 1)
        return (coords, lax.dynamic_index_in_dim(stacked, position, 0, keepdims=False))

    entries = lax.dynamic_index_in_dim(lists, cluster, 0, keepdims=False)
    rows_here = listed_sum(own_coords, entries, fetcher, width) + jnp.dot(
        transfer_rows, above, precision=HIGHEST
    )
    return join_rows(rows_here, stride.bit_length() - 1, device)


def per_device(
    vectors,
    points,
    leaf_basis,
    transfer_leaf,
    transfer_pair,
    transfer_quad,
    skel_leaf,
    skel_pair,
    skel_quad,
    skel_top,
    near_list,
    far_leaf,
    far_pair,
    far_quad,
    far_top,
):
    leaf_points = vectors.shape[1]
    width = vectors.shape[2]
    rank = leaf_basis.shape[2]
    device = lax.axis_index("leaf")
    own_points = points[0]
    shipped = jnp.concatenate(
        [vectors[0], own_points.reshape(3 * leaf_points // width, width)], axis=0
    )
    near_rim = near_window(shipped)

    def near_fetch(partner):
        position = jnp.clip(partner - device + REACH, 0, 2 * REACH)
        block = lax.dynamic_index_in_dim(near_rim, position, 0, keepdims=False)
        return (block[leaf_points:].reshape(3, leaf_points), block[:leaf_points])

    near_field = listed_sum(own_points, near_list[0], near_fetch, width)
    coef_leaf = transposed_dot(leaf_basis[0], vectors[0])
    coef_pair = pair_total(transposed_dot(transfer_leaf[0], coef_leaf), 1)
    pair_rows = lax.dynamic_slice_in_dim(coef_pair, device % 2 * (rank // 2), rank // 2, 0)
    coef_quad = pair_total(transposed_dot(transfer_pair, pair_rows), 2)
    quad_rows = lax.dynamic_slice_in_dim(coef_quad, device % 4 * (rank // 4), rank // 4, 0)
    coef_top = pair_total(transposed_dot(transfer_quad, quad_rows), 3)
    top_cluster = device // 8
    top_member = device % 8
    top_rows_own = lax.dynamic_slice_in_dim(coef_top, top_member * (rank // 8), rank // 8, 0)
    top_coords = lax.dynamic_index_in_dim(skel_top, top_cluster, 0, keepdims=False)
    top_entries = lax.dynamic_index_in_dim(far_top, top_cluster, 0, keepdims=False)
    all_top = lax.all_gather(top_rows_own, "leaf", axis=0, tiled=True).reshape(-1, rank, width)

    def top_fetch(partner):
        coords = lax.dynamic_index_in_dim(skel_top, partner, 0, keepdims=False)
        return (coords, lax.dynamic_index_in_dim(all_top, partner, 0, keepdims=False))

    local_top = listed_sum(top_coords, top_entries, top_fetch, width)
    local_quad = middle_level(coef_quad, skel_quad, far_quad, transfer_quad, local_top, 4, device)
    local_pair = middle_level(coef_pair, skel_pair, far_pair, transfer_pair, local_quad, 2, device)
    leaf_ship = jnp.concatenate([coef_leaf, skel_leaf[0]], axis=0)
    leaf_rim = coef_window(leaf_ship)

    def leaf_fetch(partner):
        position = jnp.clip(partner - device + REACH, 0, 2 * REACH)
        block = lax.dynamic_index_in_dim(leaf_rim, position, 0, keepdims=False)
        return (block[rank:], block[:rank])

    local_leaf = listed_sum(skel_leaf[0], far_leaf[0], leaf_fetch, width) + jnp.dot(
        transfer_leaf[0], local_pair, precision=HIGHEST
    )
    product = near_field + jnp.dot(leaf_basis[0], local_leaf, precision=HIGHEST)
    return product[None]


def solution(mesh):
    placed = (
        P("leaf", None, None),
        P("leaf", None, None),
        P("leaf", None, None),
        P("leaf", None, None),
        P("leaf", None),
        P("leaf", None),
        P("leaf", None, None),
        P(),
        P(),
        P(),
        P("leaf", None),
        P("leaf", None),
        P(),
        P(),
        P(),
    )
    return jax.shard_map(
        per_device, mesh=mesh, in_specs=placed, out_specs=P("leaf", None, None), check_vma=False
    )
```

profile of v0, /device:TPU:0, one launch (start us, length us, event | category | flops | bytes accessed | tf_op | source)
XLA Modules:
  0.0 455.7 jit_solution(13867952368401364163)
XLA Ops:
  1.0 1.6 fusion.136
  2.5 4.9 %collective-permute-start.16 = (f32[131,128]{1,0:T(8,128)S(1)}, f32[131,128]{1,0:T(8,128)S(1)}, u32[]{:S(2)}, u32[]{:S(2)}) collective-permute-start(f32[131,128]{1,0:T(8,128)S(1)} %pad_maximum_fusion.1), channel_id=1, source_target_pairs={{0,8},{1,9},{2,10},{3,11},{4,12},{5,13},{6,14},{7,15},{8,16},{9,17... | collective-permute-start | bytes 201224 | tf_op jit(solution)/shard_map/ppermute | solution.py:24
  7.5 3.5 collective-permute-start.17
  11.0 3.5 collective-permute-start.18
  14.5 3.7 collective-permute-start.19
  27.1 3.4 collective-permute-start.20
  31.6 1.3 collective-permute-start.21
  33.0 3.8 collective-permute-start.22
  36.8 1.9 collective-permute-start.23
  50.5 2.7 collective-permute-done.27
  53.2 8.8 %collective-permute-start = (f32[524,128]{1,0:T(8,128)S(1)}, f32[524,128]{1,0:T(8,128)S(1)}, u32[]{:S(2)}, u32[]{:S(2)}) collective-permute-start(f32[524,128]{1,0:T(8,128)S(1)} %pad_maximum_fusion), channel_id=1, source_target_pairs={{0,8},{1,9},{2,10},{3,11},{4,12},{5,13},{6,14},{7,15},{8,16},{9,17... | collective-permute-start | bytes 804872 | tf_op jit(solution)/shard_map/ppermute | solution.py:24
  62.1 4.6 %collective-permute-start.1 = (f32[524,128]{1,0:T(8,128)S(1)}, f32[524,128]{1,0:T(8,128)S(1)}, u32[]{:S(2)}, u32[]{:S(2)}) collective-permute-start(f32[524,128]{1,0:T(8,128)S(1)} %pad_maximum_fusion), channel_id=1, source_target_pairs={{0,7},{1,8},{2,9},{3,10},{4,11},{5,12},{6,13},{7,14},{8,15},{9,16}... | collective-permute-start | bytes 804872 | tf_op jit(solution)/shard_map/ppermute | solution.py:24
  66.7 4.8 %collective-permute-start.2 = (f32[524,128]{1,0:T(8,128)S(1)}, f32[524,128]{1,0:T(8,128)S(1)}, u32[]{:S(2)}, u32[]{:S(2)}) collective-permute-start(f32[524,128]{1,0:T(8,128)S(1)} %pad_maximum_fusion), channel_id=1, source_target_pairs={{0,6},{1,7},{2,8},{3,9},{4,10},{5,11},{6,12},{7,13},{8,14},{9,15},... | collective-permute-start | bytes 804872 | tf_op jit(solution)/shard_map/ppermute | solution.py:24
  71.6 3.8 collective-permute-start.33
  75.4 2.8 collective-permute-start.34
  79.3 36.3 %while.56 = (s32[]{:T(128)}, f32[128,128]{1,0:T(8,128)S(1)}, s32[8]{0:T(128)}, f32[3,128]{1,0:T(4,128)S(1)}, s32[]{:T(128)}, /*index=5*/f32[17,131,128]{2,1,0:T(...) while((s32[]{:T(128)}, f32[128,128]{1,0:T(8,128)S(1)}, ...), condition=%wide.region_3.4_spmd.clone, body=%wide.region_2.3_spmd.clone.sunk | while | flops 25378828 | bytes 206616 | solution.py:47
  115.7 4.0 collective-permute-start.35
  124.2 3.5 collective-permute-done.37
  129.0 3.0 collective-permute-done.38
  133.3 3.1 collective-permute-done.39
  137.7 3.9 collective-permute-start.3
  143.0 23.4 %while.57 = (s32[]{:T(128)}, f32[64,128]{1,0:T(8,128)S(1)}, s32[8]{0:T(128)S(1)}, f32[3,64]{1,0:T(4,128)S(1)}, f32[16,3,128]{2,0,1:T(8,128)}, /*index=5*/s32[]{:...) while((s32[]{:T(128)}, f32[64,128]{1,0:T(8,128)S(1)}, ...), condition=%wide.region_5.6_spmd.clone, body=%wide.region_4.5_spmd.clone.sunk | while | flops 12689422 | bytes 139043 | solution.py:47
  166.4 1.8 collective-permute-start.43
  168.5 1.8 collective-permute-done.43
  170.3 2.2 collective-permute-start.44
  172.6 2.4 collective-permute-done.44
  175.0 5.4 %collective-permute-start.45 = (f32[128,128]{1,0:T(8,128)S(1)}, f32[128,128]{1,0:T(8,128)S(1)}, u32[]{:S(2)}, u32[]{:S(2)}) collective-permute-start(f32[128,128]{1,0:T(8,128)S(1)} %add.194), channel_id=1, source_target_pairs={{0,8},{1,9},{2,10},{3,11},{4,12},{5,13},{6,14},{7,15},{8,16},{9,17... | collective-permute-start | bytes 196616 | tf_op jit(solution)/shard_map/ppermute | solution.py:24
  180.4 1.9 collective-permute-done.45
  182.3 2.3 collective-permute-start.46
  184.6 1.9 collective-permute-done.46
  187.8 7.6 %collective-permute-done.47 = f32[128,128]{1,0:T(8,128)S(1)} collective-permute-done((f32[128,128]{1,0:T(8,128)S(1)}, f32[128,128]{1,0:T(8,128)S(1)}, u32[]{:S(2)}, u32[]{:S(2)}) %collective-permute-start.47) | collective-permute-done | bytes 65568 | tf_op jit(solution)/shard_map/ppermute | solution.py:24
  196.7 6.6 %collective-permute-done.48 = f32[128,128]{1,0:T(8,128)S(1)} collective-permute-done((f32[128,128]{1,0:T(8,128)S(1)}, f32[128,128]{1,0:T(8,128)S(1)}, u32[]{:S(2)}, u32[]{:S(2)}) %collective-permute-start.48) | collective-permute-done | bytes 65568 | tf_op jit(solution)/shard_map/ppermute | solution.py:24
  204.6 6.4 %collective-permute-done.49 = f32[128,128]{1,0:T(8,128)S(1)} collective-permute-done((f32[128,128]{1,0:T(8,128)S(1)}, f32[128,128]{1,0:T(8,128)S(1)}, u32[]{:S(2)}, u32[]{:S(2)}) %collective-permute-start.49) | collective-permute-done | bytes 65568 | tf_op jit(solution)/shard_map/ppermute | solution.py:24
  212.4 6.5 %collective-permute-done.50 = f32[128,128]{1,0:T(8,128)S(1)} collective-permute-done((f32[128,128]{1,0:T(8,128)S(1)}, f32[128,128]{1,0:T(8,128)S(1)}, u32[]{:S(2)}, u32[]{:S(2)}) %collective-permute-start.50) | collective-permute-done | bytes 65568 | tf_op jit(solution)/shard_map/ppermute | solution.py:24
  218.8 23.3 %while.58 = (s32[]{:T(128)}, f32[32,128]{1,0:T(8,128)S(1)}, s32[8]{0:T(128)S(1)}, f32[3,32]{1,0:T(4,128)S(1)}, f32[8,3,128]{2,0,1:T(8,128)}, /*index=5*/s32[]{:T...) while((s32[]{:T(128)}, f32[32,128]{1,0:T(8,128)S(1)}, ...), condition=%wide.region_7.8_spmd.clone, body=%wide.region_6.7_spmd.clone.sunk | while | flops 6344718 | bytes 105507 | solution.py:47
  242.2 4.3 collective-permute-start.4
  246.5 2.9 collective-permute-start.5
  249.4 3.3 collective-permute-start.6
  252.8 1.6 collective-permute-start.7
  255.8 7.7 %collective-permute-done.4 = f32[524,128]{1,0:T(8,128)S(1)} collective-permute-done((f32[524,128]{1,0:T(8,128)S(1)}, f32[524,128]{1,0:T(8,128)S(1)}, u32[]{:S(2)}, u32[]{:S(2)}) %collective-permute-start.4) | collective-permute-done | bytes 268320 | tf_op jit(solution)/shard_map/ppermute | solution.py:24
  270.2 4.6 %collective-permute-done.9 = f32[524,128]{1,0:T(8,128)S(1)} collective-permute-done((f32[524,128]{1,0:T(8,128)S(1)}, f32[524,128]{1,0:T(8,128)S(1)}, u32[]{:S(2)}, u32[]{:S(2)}) %collective-permute-start.9) | collective-permute-done | bytes 268320 | tf_op jit(solution)/shard_map/ppermute | solution.py:24
  277.4 18.6 %collective-permute-done.11 = f32[524,128]{1,0:T(8,128)S(1)} collective-permute-done((f32[524,128]{1,0:T(8,128)S(1)}, f32[524,128]{1,0:T(8,128)S(1)}, u32[]{:S(2)}, u32[]{:S(2)}) %collective-permute-start.11) | collective-permute-done | bytes 268320 | tf_op jit(solution)/shard_map/ppermute | solution.py:24
  296.4 4.5 collective-permute-done.52
  301.1 4.2 collective-permute-done.53
  305.3 37.0 %all_gather.3 = f32[512,128]{1,0:T(8,128)S(1)} all-gather(f32[16,128]{1,0:T(8,128)S(1)} %dynamic-slice_add_fusion), channel_id=1, replica_groups=mesh['leaf'=32] {'leaf'}, dimensions={0}, use_global_device_ids=true | all-gather | bytes 270336 | tf_op jit(solution)/shard_map/all_gather | solution.py:164
  342.3 24.9 %while.59 = (s32[]{:T(128)}, f32[128,128]{1,0:T(8,128)S(1)}, s32[8]{0:T(128)S(1)}, f32[3,128]{1,0:T(4,128)S(1)}, f32[4,3,128]{2,0,1:T(4,128)}, /*index=5*/f32[4,...) while((s32[]{:T(128)}, f32[128,128]{1,0:T(8,128)S(1)}, ...), condition=%wide.region_9.10_spmd.clone, body=%wide.region_8.9_spmd.clone.sunk | while | flops 25378824 | bytes 206017 | solution.py:47
  368.7 2.0 collective-permute-start.55
  372.9 81.1 %while.55 = (s32[]{:T(128)}, f32[512,128]{1,0:T(8,128)S(1)}, s32[16]{0:T(128)S(1)}, f32[3,512]{1,0:T(4,128)S(1)}, s32[]{:T(128)}, /*index=5*/f32[17,524,128]{2,1...) while((s32[]{:T(128)}, f32[512,128]{1,0:T(8,128)S(1)}, ...), condition=%wide.region_1.2_spmd.clone, body=%wide.region_0.1_spmd.clone.sunk | while | flops 405471232 | bytes 824088 | solution.py:47
  375.7 2.4 fusion.189
  380.7 2.4 fusion.189
  385.8 2.4 fusion.189
  390.9 2.4 fusion.189
  395.9 2.4 fusion.189
  401.0 2.4 fusion.189
  406.1 2.4 fusion.189
  411.1 2.4 fusion.189
  416.2 2.4 fusion.189
  421.3 2.4 fusion.189
  426.3 2.4 fusion.189
  431.4 2.4 fusion.189
  436.5 2.4 fusion.189
  441.5 2.4 fusion.189
  446.6 2.4 fusion.189
  451.7 2.4 fusion.189
  (353 shorter events, 142.2 us)
Async XLA Ops:
  1.0 167.2 %copy-start.4 = (f32[32,128]{1,0:T(8,128)S(1)}, f32[32,128]{1,0:T(8,128)}, u32[]{:S(2)}) copy-start(f32[32,128]{1,0:T(8,128)} %param.30) | copy-start | bytes 49156
  2.5 29.1 %collective-permute-start.16 = (f32[131,128]{1,0:T(8,128)S(1)}, f32[131,128]{1,0:T(8,128)S(1)}, u32[]{:S(2)}, u32[]{:S(2)}) collective-permute-start(f32[131,128]{1,0:T(8,128)S(1)} %pad_maximum_fusion.1), channel_id=1, source_target_pairs={{0,8},{1,9},{2,10},{3,11},{4,12},{5,13},{6,14},{7,15},{8,16},{9,17... | collective-permute-start | bytes 201224 | tf_op jit(solution)/shard_map/ppermute | solution.py:24
  7.5 25.5 %collective-permute-start.17 = (f32[131,128]{1,0:T(8,128)S(1)}, f32[131,128]{1,0:T(8,128)S(1)}, u32[]{:S(2)}, u32[]{:S(2)}) collective-permute-start(f32[131,128]{1,0:T(8,128)S(1)} %pad_maximum_fusion.1), channel_id=1, source_target_pairs={{0,7},{1,8},{2,9},{3,10},{4,11},{5,12},{6,13},{7,14},{8,15},{9,16}... | collective-permute-start | bytes 201224 | tf_op jit(solution)/shard_map/ppermute | solution.py:24
  11.0 25.7 %collective-permute-start.18 = (f32[131,128]{1,0:T(8,128)S(1)}, f32[131,128]{1,0:T(8,128)S(1)}, u32[]{:S(2)}, u32[]{:S(2)}) collective-permute-start(f32[131,128]{1,0:T(8,128)S(1)} %pad_maximum_fusion.1), channel_id=1, source_target_pairs={{0,6},{1,7},{2,8},{3,9},{4,10},{5,11},{6,12},{7,13},{8,14},{9,15},... | collective-permute-start | bytes 201224 | tf_op jit(solution)/shard_map/ppermute | solution.py:24
  14.5 24.2 %collective-permute-start.19 = (f32[131,128]{1,0:T(8,128)S(1)}, f32[131,128]{1,0:T(8,128)S(1)}, u32[]{:S(2)}, u32[]{:S(2)}) collective-permute-start(f32[131,128]{1,0:T(8,128)S(1)} %pad_maximum_fusion.1), channel_id=1, source_target_pairs={{0,5},{1,6},{2,7},{3,8},{4,9},{5,10},{6,11},{7,12},{8,13},{9,14},{... | collective-permute-start | bytes 201224 | tf_op jit(solution)/shard_map/ppermute | solution.py:24
  19.3 7.7 %collective-permute-start.32 = (f32[128,128]{1,0:T(8,128)S(1)}, f32[128,128]{1,0:T(8,128)S(1)}, u32[]{:S(2)}, u32[]{:S(2)}) collective-permute-start(f32[128,128]{1,0:T(8,128)S(1)} %convolution_bitcast_fusion.4), channel_id=1, source_target_pairs={{0,1},{1,0},{2,3},{3,2},{4,5},{5,4},{6,7},{7,6},{8,9},{9,8},{10,11... | collective-permute-start | bytes 196616 | tf_op jit(solution)/shard_map/ppermute | solution.py:18
  27.1 12.9 %collective-permute-start.20 = (f32[131,128]{1,0:T(8,128)S(1)}, f32[131,128]{1,0:T(8,128)S(1)}, u32[]{:S(2)}, u32[]{:S(2)}) collective-permute-start(f32[131,128]{1,0:T(8,128)S(1)} %pad_maximum_fusion.1), channel_id=1, source_target_pairs={{0,4},{1,5},{2,6},{3,7},{4,8},{5,9},{6,10},{7,11},{8,12},{9,13},{1... | collective-permute-start | bytes 201224 | tf_op jit(solution)/shard_map/ppermute | solution.py:24
  31.6 9.7 %collective-permute-start.21 = (f32[131,128]{1,0:T(8,128)S(1)}, f32[131,128]{1,0:T(8,128)S(1)}, u32[]{:S(2)}, u32[]{:S(2)}) collective-permute-start(f32[131,128]{1,0:T(8,128)S(1)} %pad_maximum_fusion.1), channel_id=1, source_target_pairs={{0,3},{1,4},{2,5},{3,6},{4,7},{5,8},{6,9},{7,10},{8,11},{9,12},{10... | collective-permute-start | bytes 201224 | tf_op jit(solution)/shard_map/ppermute | solution.py:24
  33.0 9.7 %collective-permute-start.22 = (f32[131,128]{1,0:T(8,128)S(1)}, f32[131,128]{1,0:T(8,128)S(1)}, u32[]{:S(2)}, u32[]{:S(2)}) collective-permute-start(f32[131,128]{1,0:T(8,128)S(1)} %pad_maximum_fusion.1), channel_id=1, source_target_pairs={{0,2},{1,3},{2,4},{3,5},{4,6},{5,7},{6,8},{7,9},{8,10},{9,11},{10,... | collective-permute-start | bytes 201224 | tf_op jit(solution)/shard_map/ppermute | solution.py:24
  36.8 7.2 %collective-permute-start.23 = (f32[131,128]{1,0:T(8,128)S(1)}, f32[131,128]{1,0:T(8,128)S(1)}, u32[]{:S(2)}, u32[]{:S(2)}) collective-permute-start(f32[131,128]{1,0:T(8,128)S(1)} %pad_maximum_fusion.1), channel_id=1, source_target_pairs={{0,1},{1,2},{2,3},{3,4},{4,5},{5,6},{6,7},{7,8},{8,9},{9,10},{10,1... | collective-permute-start | bytes 201224 | tf_op jit(solution)/shard_map/ppermute | solution.py:24
  38.7 6.6 %collective-permute-start.24 = (f32[131,128]{1,0:T(8,128)S(1)}, f32[131,128]{1,0:T(8,128)S(1)}, u32[]{:S(2)}, u32[]{:S(2)}) collective-permute-start(f32[131,128]{1,0:T(8,128)S(1)} %pad_maximum_fusion.1), channel_id=1, source_target_pairs={{1,0},{2,1},{3,2},{4,3},{5,4},{6,5},{7,6},{8,7},{9,8},{10,9},{11,1... | collective-permute-start | bytes 201224 | tf_op jit(solution)/shard_map/ppermute | solution.py:24
  40.0 7.9 %collective-permute-start.25 = (f32[131,128]{1,0:T(8,128)S(1)}, f32[131,128]{1,0:T(8,128)S(1)}, u32[]{:S(2)}, u32[]{:S(2)}) collective-permute-start(f32[131,128]{1,0:T(8,128)S(1)} %pad_maximum_fusion.1), channel_id=1, source_target_pairs={{2,0},{3,1},{4,2},{5,3},{6,4},{7,5},{8,6},{9,7},{10,8},{11,9},{12,... | collective-permute-start | bytes 201224 | tf_op jit(solution)/shard_map/ppermute | solution.py:24
  41.3 7.8 %collective-permute-start.26 = (f32[131,128]{1,0:T(8,128)S(1)}, f32[131,128]{1,0:T(8,128)S(1)}, u32[]{:S(2)}, u32[]{:S(2)}) collective-permute-start(f32[131,128]{1,0:T(8,128)S(1)} %pad_maximum_fusion.1), channel_id=1, source_target_pairs={{3,0},{4,1},{5,2},{6,3},{7,4},{8,5},{9,6},{10,7},{11,8},{12,9},{13... | collective-permute-start | bytes 201224 | tf_op jit(solution)/shard_map/ppermute | solution.py:24
  42.7 10.6 %collective-permute-start.27 = (f32[131,128]{1,0:T(8,128)S(1)}, f32[131,128]{1,0:T(8,128)S(1)}, u32[]{:S(2)}, u32[]{:S(2)}) collective-permute-start(f32[131,128]{1,0:T(8,128)S(1)} %pad_maximum_fusion.1), channel_id=1, source_target_pairs={{4,0},{5,1},{6,2},{7,3},{8,4},{9,5},{10,6},{11,7},{12,8},{13,9},{1... | collective-permute-start | bytes 201224 | tf_op jit(solution)/shard_map/ppermute | solution.py:24
  44.0 18.1 %collective-permute-start.28 = (f32[131,128]{1,0:T(8,128)S(1)}, f32[131,128]{1,0:T(8,128)S(1)}, u32[]{:S(2)}, u32[]{:S(2)}) collective-permute-start(f32[131,128]{1,0:T(8,128)S(1)} %pad_maximum_fusion.1), channel_id=1, source_target_pairs={{5,0},{6,1},{7,2},{8,3},{9,4},{10,5},{11,6},{12,7},{13,8},{14,9},{... | collective-permute-start | bytes 201224 | tf_op jit(solution)/shard_map/ppermute | solution.py:24
  45.3 21.4 %collective-permute-start.29 = (f32[131,128]{1,0:T(8,128)S(1)}, f32[131,128]{1,0:T(8,128)S(1)}, u32[]{:S(2)}, u32[]{:S(2)}) collective-permute-start(f32[131,128]{1,0:T(8,128)S(1)} %pad_maximum_fusion.1), channel_id=1, source_target_pairs={{6,0},{7,1},{8,2},{9,3},{10,4},{11,5},{12,6},{13,7},{14,8},{15,9},... | collective-permute-start | bytes 201224 | tf_op jit(solution)/shard_map/ppermute | solution.py:24
  47.9 23.7 %collective-permute-start.30 = (f32[131,128]{1,0:T(8,128)S(1)}, f32[131,128]{1,0:T(8,128)S(1)}, u32[]{:S(2)}, u32[]{:S(2)}) collective-permute-start(f32[131,128]{1,0:T(8,128)S(1)} %pad_maximum_fusion.1), channel_id=1, source_target_pairs={{7,0},{8,1},{9,2},{10,3},{11,4},{12,5},{13,6},{14,7},{15,8},{16,9}... | collective-permute-start | bytes 201224 | tf_op jit(solution)/shard_map/ppermute | solution.py:24
  49.2 26.2 %collective-permute-start.31 = (f32[131,128]{1,0:T(8,128)S(1)}, f32[131,128]{1,0:T(8,128)S(1)}, u32[]{:S(2)}, u32[]{:S(2)}) collective-permute-start(f32[131,128]{1,0:T(8,128)S(1)} %pad_maximum_fusion.1), channel_id=1, source_target_pairs={{8,0},{9,1},{10,2},{11,3},{12,4},{13,5},{14,6},{15,7},{16,8},{17,9... | collective-permute-start | bytes 201224 | tf_op jit(solution)/shard_map/ppermute | solution.py:24
  53.2 193.3 %collective-permute-start = (f32[524,128]{1,0:T(8,128)S(1)}, f32[524,128]{1,0:T(8,128)S(1)}, u32[]{:S(2)}, u32[]{:S(2)}) collective-permute-start(f32[524,128]{1,0:T(8,128)S(1)} %pad_maximum_fusion), channel_id=1, source_target_pairs={{0,8},{1,9},{2,10},{3,11},{4,12},{5,13},{6,14},{7,15},{8,16},{9,17... | collective-permute-start | bytes 804872 | tf_op jit(solution)/shard_map/ppermute | solution.py:24
  62.1 187.3 %collective-permute-start.1 = (f32[524,128]{1,0:T(8,128)S(1)}, f32[524,128]{1,0:T(8,128)S(1)}, u32[]{:S(2)}, u32[]{:S(2)}) collective-permute-start(f32[524,128]{1,0:T(8,128)S(1)} %pad_maximum_fusion), channel_id=1, source_target_pairs={{0,7},{1,8},{2,9},{3,10},{4,11},{5,12},{6,13},{7,14},{8,15},{9,16}... | collective-permute-start | bytes 804872 | tf_op jit(solution)/shard_map/ppermute | solution.py:24
  66.7 186.1 %collective-permute-start.2 = (f32[524,128]{1,0:T(8,128)S(1)}, f32[524,128]{1,0:T(8,128)S(1)}, u32[]{:S(2)}, u32[]{:S(2)}) collective-permute-start(f32[524,128]{1,0:T(8,128)S(1)} %pad_maximum_fusion), channel_id=1, source_target_pairs={{0,6},{1,7},{2,8},{3,9},{4,10},{5,11},{6,12},{7,13},{8,14},{9,15},... | collective-permute-start | bytes 804872 | tf_op jit(solution)/shard_map/ppermute | solution.py:24
  71.6 44.1 %collective-permute-start.33 = (f32[128,128]{1,0:T(8,128)S(1)}, f32[128,128]{1,0:T(8,128)S(1)}, u32[]{:S(2)}, u32[]{:S(2)}) collective-permute-start(f32[128,128]{1,0:T(8,128)S(1)} %add.188), channel_id=1, source_target_pairs={{0,8},{1,9},{2,10},{3,11},{4,12},{5,13},{6,14},{7,15},{8,16},{9,17... | collective-permute-start | bytes 196616 | tf_op jit(solution)/shard_map/ppermute | solution.py:24
  75.4 44.3 %collective-permute-start.34 = (f32[128,128]{1,0:T(8,128)S(1)}, f32[128,128]{1,0:T(8,128)S(1)}, u32[]{:S(2)}, u32[]{:S(2)}) collective-permute-start(f32[128,128]{1,0:T(8,128)S(1)} %add.188), channel_id=1, source_target_pairs={{0,6},{1,7},{2,8},{3,9},{4,10},{5,11},{6,12},{7,13},{8,14},{9,15},... | collective-permute-start | bytes 196616 | tf_op jit(solution)/shard_map/ppermute | solution.py:24
  78.2 1.1 copy-start.6
  115.7 5.9 %collective-permute-start.35 = (f32[128,128]{1,0:T(8,128)S(1)}, f32[128,128]{1,0:T(8,128)S(1)}, u32[]{:S(2)}, u32[]{:S(2)}) collective-permute-start(f32[128,128]{1,0:T(8,128)S(1)} %add.188), channel_id=1, source_target_pairs={{0,4},{1,5},{2,6},{3,7},{4,8},{5,9},{6,10},{7,11},{8,12},{9,13},{1... | collective-permute-start | bytes 196616 | tf_op jit(solution)/shard_map/ppermute | solution.py:24
  119.7 3.2 collective-permute-start.36
  121.6 6.1 %collective-permute-start.37 = (f32[128,128]{1,0:T(8,128)S(1)}, f32[128,128]{1,0:T(8,128)S(1)}, u32[]{:S(2)}, u32[]{:S(2)}) collective-permute-start(f32[128,128]{1,0:T(8,128)S(1)} %add.188), channel_id=1, source_target_pairs={{2,0},{3,1},{4,2},{5,3},{6,4},{7,5},{8,6},{9,7},{10,8},{11,9},{12,... | collective-permute-start | bytes 196616 | tf_op jit(solution)/shard_map/ppermute | solution.py:24
  122.9 9.1 %collective-permute-start.38 = (f32[128,128]{1,0:T(8,128)S(1)}, f32[128,128]{1,0:T(8,128)S(1)}, u32[]{:S(2)}, u32[]{:S(2)}) collective-permute-start(f32[128,128]{1,0:T(8,128)S(1)} %add.188), channel_id=1, source_target_pairs={{4,0},{5,1},{6,2},{7,3},{8,4},{9,5},{10,6},{11,7},{12,8},{13,9},{1... | collective-permute-start | bytes 196616 | tf_op jit(solution)/shard_map/ppermute | solution.py:24
  127.7 8.7 %collective-permute-start.39 = (f32[128,128]{1,0:T(8,128)S(1)}, f32[128,128]{1,0:T(8,128)S(1)}, u32[]{:S(2)}, u32[]{:S(2)}) collective-permute-start(f32[128,128]{1,0:T(8,128)S(1)} %add.188), channel_id=1, source_target_pairs={{6,0},{7,1},{8,2},{9,3},{10,4},{11,5},{12,6},{13,7},{14,8},{15,9},... | collective-permute-start | bytes 196616 | tf_op jit(solution)/shard_map/ppermute | solution.py:24
  132.0 9.7 %collective-permute-start.40 = (f32[128,128]{1,0:T(8,128)S(1)}, f32[128,128]{1,0:T(8,128)S(1)}, u32[]{:S(2)}, u32[]{:S(2)}) collective-permute-start(f32[128,128]{1,0:T(8,128)S(1)} %add.188), channel_id=1, source_target_pairs={{8,0},{9,1},{10,2},{11,3},{12,4},{13,5},{14,6},{15,7},{16,8},{17,9... | collective-permute-start | bytes 196616 | tf_op jit(solution)/shard_map/ppermute | solution.py:24
  133.3 135.5 %copy-start.1 = (f32[1,512,128]{2,1,0:T(8,128)S(1)}, f32[1,512,128]{2,1,0:T(8,128)}, u32[]{:S(2)}) copy-start(f32[1,512,128]{2,1,0:T(8,128)} %param.25) | copy-start | bytes 786436
  136.5 1.3 collective-permute-start.41
  137.7 116.7 %collective-permute-start.3 = (f32[524,128]{1,0:T(8,128)S(1)}, f32[524,128]{1,0:T(8,128)S(1)}, u32[]{:S(2)}, u32[]{:S(2)}) collective-permute-start(f32[524,128]{1,0:T(8,128)S(1)} %pad_maximum_fusion), channel_id=1, source_target_pairs={{0,5},{1,6},{2,7},{3,8},{4,9},{5,10},{6,11},{7,12},{8,13},{9,14},{... | collective-permute-start | bytes 804872 | tf_op jit(solution)/shard_map/ppermute | solution.py:24
  141.7 24.7 %collective-permute-start.42 = (f32[128,128]{1,0:T(8,128)S(1)}, f32[128,128]{1,0:T(8,128)S(1)}, u32[]{:S(2)}, u32[]{:S(2)}) collective-permute-start(f32[128,128]{1,0:T(8,128)S(1)} %add.193), channel_id=1, source_target_pairs={{0,2},{1,3},{2,0},{3,1},{4,6},{5,7},{6,4},{7,5},{8,10},{9,11},{10,... | collective-permute-start | bytes 196616 | tf_op jit(solution)/shard_map/ppermute | solution.py:18
  166.4 3.9 collective-permute-start.43
  170.3 4.7 %collective-permute-start.44 = (f32[128,128]{1,0:T(8,128)S(1)}, f32[128,128]{1,0:T(8,128)S(1)}, u32[]{:S(2)}, u32[]{:S(2)}) collective-permute-start(f32[128,128]{1,0:T(8,128)S(1)} %add.194), channel_id=1, source_target_pairs={{0,12},{1,13},{2,14},{3,15},{4,16},{5,17},{6,18},{7,19},{8,20},{9,... | collective-permute-start | bytes 196616 | tf_op jit(solution)/shard_map/ppermute | solution.py:24
  175.0 7.3 %collective-permute-start.45 = (f32[128,128]{1,0:T(8,128)S(1)}, f32[128,128]{1,0:T(8,128)S(1)}, u32[]{:S(2)}, u32[]{:S(2)}) collective-permute-start(f32[128,128]{1,0:T(8,128)S(1)} %add.194), channel_id=1, source_target_pairs={{0,8},{1,9},{2,10},{3,11},{4,12},{5,13},{6,14},{7,15},{8,16},{9,17... | collective-permute-start | bytes 196616 | tf_op jit(solution)/shard_map/ppermute | solution.py:24
  182.3 4.2 collective-permute-start.46
  186.5 8.9 %collective-permute-start.47 = (f32[128,128]{1,0:T(8,128)S(1)}, f32[128,128]{1,0:T(8,128)S(1)}, u32[]{:S(2)}, u32[]{:S(2)}) collective-permute-start(f32[128,128]{1,0:T(8,128)S(1)} %add.194), channel_id=1, source_target_pairs={{4,0},{5,1},{6,2},{7,3},{8,4},{9,5},{10,6},{11,7},{12,8},{13,9},{1... | collective-permute-start | bytes 196616 | tf_op jit(solution)/shard_map/ppermute | solution.py:24
  195.4 7.9 %collective-permute-start.48 = (f32[128,128]{1,0:T(8,128)S(1)}, f32[128,128]{1,0:T(8,128)S(1)}, u32[]{:S(2)}, u32[]{:S(2)}) collective-permute-start(f32[128,128]{1,0:T(8,128)S(1)} %add.194), channel_id=1, source_target_pairs={{8,0},{9,1},{10,2},{11,3},{12,4},{13,5},{14,6},{15,7},{16,8},{17,9... | collective-permute-start | bytes 196616 | tf_op jit(solution)/shard_map/ppermute | solution.py:24
  203.3 7.7 %collective-permute-start.49 = (f32[128,128]{1,0:T(8,128)S(1)}, f32[128,128]{1,0:T(8,128)S(1)}, u32[]{:S(2)}, u32[]{:S(2)}) collective-permute-start(f32[128,128]{1,0:T(8,128)S(1)} %add.194), channel_id=1, source_target_pairs={{12,0},{13,1},{14,2},{15,3},{16,4},{17,5},{18,6},{19,7},{20,8},{21... | collective-permute-start | bytes 196616 | tf_op jit(solution)/shard_map/ppermute | solution.py:24
  211.1 7.8 %collective-permute-start.50 = (f32[128,128]{1,0:T(8,128)S(1)}, f32[128,128]{1,0:T(8,128)S(1)}, u32[]{:S(2)}, u32[]{:S(2)}) collective-permute-start(f32[128,128]{1,0:T(8,128)S(1)} %add.194), channel_id=1, source_target_pairs={{16,0},{17,1},{18,2},{19,3},{20,4},{21,5},{22,6},{23,7},{24,8},{25... | collective-permute-start | bytes 196616 | tf_op jit(solution)/shard_map/ppermute | solution.py:24
  218.8 23.3 %collective-permute-start.51 = (f32[128,128]{1,0:T(8,128)S(1)}, f32[128,128]{1,0:T(8,128)S(1)}, u32[]{:S(2)}, u32[]{:S(2)}) collective-permute-start(f32[128,128]{1,0:T(8,128)S(1)} %convolution_bitcast_fusion.2), channel_id=1, source_target_pairs={{0,1},{1,0},{2,3},{3,2},{4,5},{5,4},{6,7},{7,6},{8,9},{9,8},{10,11... | collective-permute-start | bytes 196616 | tf_op jit(solution)/shard_map/ppermute | solution.py:18
  242.2 21.3 %collective-permute-start.4 = (f32[524,128]{1,0:T(8,128)S(1)}, f32[524,128]{1,0:T(8,128)S(1)}, u32[]{:S(2)}, u32[]{:S(2)}) collective-permute-start(f32[524,128]{1,0:T(8,128)S(1)} %pad_maximum_fusion), channel_id=1, source_target_pairs={{0,4},{1,5},{2,6},{3,7},{4,8},{5,9},{6,10},{7,11},{8,12},{9,13},{1... | collective-permute-start | bytes 804872 | tf_op jit(solution)/shard_map/ppermute | solution.py:24
  246.5 18.3 %collective-permute-start.5 = (f32[524,128]{1,0:T(8,128)S(1)}, f32[524,128]{1,0:T(8,128)S(1)}, u32[]{:S(2)}, u32[]{:S(2)}) collective-permute-start(f32[524,128]{1,0:T(8,128)S(1)} %pad_maximum_fusion), channel_id=1, source_target_pairs={{0,3},{1,4},{2,5},{3,6},{4,7},{5,8},{6,9},{7,10},{8,11},{9,12},{10... | collective-permute-start | bytes 804872 | tf_op jit(solution)/shard_map/ppermute | solution.py:24
  249.4 16.7 %collective-permute-start.6 = (f32[524,128]{1,0:T(8,128)S(1)}, f32[524,128]{1,0:T(8,128)S(1)}, u32[]{:S(2)}, u32[]{:S(2)}) collective-permute-start(f32[524,128]{1,0:T(8,128)S(1)} %pad_maximum_fusion), channel_id=1, source_target_pairs={{0,2},{1,3},{2,4},{3,5},{4,6},{5,7},{6,8},{7,9},{8,10},{9,11},{10,... | collective-permute-start | bytes 804872 | tf_op jit(solution)/shard_map/ppermute | solution.py:24
  252.8 14.6 %collective-permute-start.7 = (f32[524,128]{1,0:T(8,128)S(1)}, f32[524,128]{1,0:T(8,128)S(1)}, u32[]{:S(2)}, u32[]{:S(2)}) collective-permute-start(f32[524,128]{1,0:T(8,128)S(1)} %pad_maximum_fusion), channel_id=1, source_target_pairs={{0,1},{1,2},{2,3},{3,4},{4,5},{5,6},{6,7},{7,8},{8,9},{9,10},{10,1... | collective-permute-start | bytes 804872 | tf_op jit(solution)/shard_map/ppermute | solution.py:24
  254.4 14.4 %collective-permute-start.8 = (f32[524,128]{1,0:T(8,128)S(1)}, f32[524,128]{1,0:T(8,128)S(1)}, u32[]{:S(2)}, u32[]{:S(2)}) collective-permute-start(f32[524,128]{1,0:T(8,128)S(1)} %pad_maximum_fusion), channel_id=1, source_target_pairs={{1,0},{2,1},{3,2},{4,3},{5,4},{6,5},{7,6},{8,7},{9,8},{10,9},{11,1... | collective-permute-start | bytes 804872 | tf_op jit(solution)/shard_map/ppermute | solution.py:24
  263.4 11.3 %collective-permute-start.9 = (f32[524,128]{1,0:T(8,128)S(1)}, f32[524,128]{1,0:T(8,128)S(1)}, u32[]{:S(2)}, u32[]{:S(2)}) collective-permute-start(f32[524,128]{1,0:T(8,128)S(1)} %pad_maximum_fusion), channel_id=1, source_target_pairs={{2,0},{3,1},{4,2},{5,3},{6,4},{7,5},{8,6},{9,7},{10,8},{11,9},{12,... | collective-permute-start | bytes 804872 | tf_op jit(solution)/shard_map/ppermute | solution.py:24
  264.7 107.9 %copy-start.3 = (f32[64,128]{1,0:T(8,128)S(1)}, f32[64,128]{1,0:T(8,128)}, u32[]{:S(2)}) copy-start(f32[64,128]{1,0:T(8,128)} %param.29) | copy-start | bytes 98308
  264.8 108.2 %copy-start.7 = (s32[1,16]{1,0:T(1,128)S(1)}, s32[1,16]{1,0:T(1,128)}, u32[]{:S(2)}) copy-start(s32[1,16]{1,0:T(1,128)} %param.35) | copy-start | bytes 196
  264.8 11.3 %collective-permute-start.10 = (f32[524,128]{1,0:T(8,128)S(1)}, f32[524,128]{1,0:T(8,128)S(1)}, u32[]{:S(2)}, u32[]{:S(2)}) collective-permute-start(f32[524,128]{1,0:T(8,128)S(1)} %pad_maximum_fusion), channel_id=1, source_target_pairs={{3,0},{4,1},{5,2},{6,3},{7,4},{8,5},{9,6},{10,7},{11,8},{12,9},{13... | collective-permute-start | bytes 804872 | tf_op jit(solution)/shard_map/ppermute | solution.py:24
  266.1 29.9 %collective-permute-start.11 = (f32[524,128]{1,0:T(8,128)S(1)}, f32[524,128]{1,0:T(8,128)S(1)}, u32[]{:S(2)}, u32[]{:S(2)}) collective-permute-start(f32[524,128]{1,0:T(8,128)S(1)} %pad_maximum_fusion), channel_id=1, source_target_pairs={{4,0},{5,1},{6,2},{7,3},{8,4},{9,5},{10,6},{11,7},{12,8},{13,9},{1... | collective-permute-start | bytes 804872 | tf_op jit(solution)/shard_map/ppermute | solution.py:24
  267.5 28.9 %collective-permute-start.12 = (f32[524,128]{1,0:T(8,128)S(1)}, f32[524,128]{1,0:T(8,128)S(1)}, u32[]{:S(2)}, u32[]{:S(2)}) collective-permute-start(f32[524,128]{1,0:T(8,128)S(1)} %pad_maximum_fusion), channel_id=1, source_target_pairs={{5,0},{6,1},{7,2},{8,3},{9,4},{10,5},{11,6},{12,7},{13,8},{14,9},{... | collective-permute-start | bytes 804872 | tf_op jit(solution)/shard_map/ppermute | solution.py:24
  268.8 32.2 %collective-permute-start.13 = (f32[524,128]{1,0:T(8,128)S(1)}, f32[524,128]{1,0:T(8,128)S(1)}, u32[]{:S(2)}, u32[]{:S(2)}) collective-permute-start(f32[524,128]{1,0:T(8,128)S(1)} %pad_maximum_fusion), channel_id=1, source_target_pairs={{6,0},{7,1},{8,2},{9,3},{10,4},{11,5},{12,6},{13,7},{14,8},{15,9},... | collective-permute-start | bytes 804872 | tf_op jit(solution)/shard_map/ppermute | solution.py:24
  274.7 93.1 %collective-permute-start.14 = (f32[524,128]{1,0:T(8,128)S(1)}, f32[524,128]{1,0:T(8,128)S(1)}, u32[]{:S(2)}, u32[]{:S(2)}) collective-permute-start(f32[524,128]{1,0:T(8,128)S(1)} %pad_maximum_fusion), channel_id=1, source_target_pairs={{7,0},{8,1},{9,2},{10,3},{11,4},{12,5},{13,6},{14,7},{15,8},{16,9}... | collective-permute-start | bytes 804872 | tf_op jit(solution)/shard_map/ppermute | solution.py:24
  276.1 94.6 %collective-permute-start.15 = (f32[524,128]{1,0:T(8,128)S(1)}, f32[524,128]{1,0:T(8,128)S(1)}, u32[]{:S(2)}, u32[]{:S(2)}) collective-permute-start(f32[524,128]{1,0:T(8,128)S(1)} %pad_maximum_fusion), channel_id=1, source_target_pairs={{8,0},{9,1},{10,2},{11,3},{12,4},{13,5},{14,6},{15,7},{16,8},{17,9... | collective-permute-start | bytes 804872 | tf_op jit(solution)/shard_map/ppermute | solution.py:24
  296.0 5.0 %collective-permute-start.52 = (f32[128,128]{1,0:T(8,128)S(1)}, f32[128,128]{1,0:T(8,128)S(1)}, u32[]{:S(2)}, u32[]{:S(2)}) collective-permute-start(f32[128,128]{1,0:T(8,128)S(1)} %add.196), channel_id=1, source_target_pairs={{0,2},{1,3},{2,0},{3,1},{4,6},{5,7},{6,4},{7,5},{8,10},{9,11},{10,... | collective-permute-start | bytes 196616 | tf_op jit(solution)/shard_map/ppermute | solution.py:18
  301.0 4.3 collective-permute-start.53
  301.1 41.2 %copy-start.5 = (f32[17,524,128]{2,1,0:T(8,128)}, f32[17,524,128]{2,1,0:T(8,128)S(1)}, u32[]{:S(2)}) copy-start(f32[17,524,128]{2,1,0:T(8,128)S(1)} %bitcast_dynamic-update-slice_fusion.2) | copy-start | bytes 13682692
  367.5 1.2 collective-permute-start.54
  368.7 3.9 collective-permute-start.55
  372.8 81.3 %collective-permute-start.56 = (f32[64,128]{1,0:T(8,128)S(1)}, f32[64,128]{1,0:T(8,128)S(1)}, u32[]{:S(2)}, u32[]{:S(2)}) collective-permute-start(f32[64,128]{1,0:T(8,128)S(1)} %add.202), channel_id=1, source_target_pairs={{0,1},{1,0},{2,3},{3,2},{4,5},{5,4},{6,7},{7,6},{8,9},{9,8},{10,11... | collective-permute-start | bytes 98312 | tf_op jit(solution)/shard_map/ppermute | solution.py:18
  372.9 81.2 %copy-start.2 = (f32[1,128,128]{2,1,0:T(8,128)S(1)}, f32[1,128,128]{2,1,0:T(8,128)}, u32[]{:S(2)}) copy-start(f32[1,128,128]{2,1,0:T(8,128)} %param.28) | copy-start | bytes 196612
  (1 other events, 1.0 us)
where the time goes:
time: 461 us; the launch traced here: 456 us
  starting transfers between devices  119 us (26%)
  waiting for transfers between devices  91.8 us (20%)
  local copies, waits for them, and re-layouts  82 us (18%)
  loops' own time  64.4 us (14%)
  matrix products  58 us (13%)
  blocking collectives  37 us (8%)
    ppermute x48, starting transfers between devices, from_behind(): return lax.ppermute(block, axis, route)  115 us
    ppermute x48, waiting for transfers between devices, from_behind(): return lax.ppermute(block, axis, route)  80.5 us
    another operation x5, loops' own time, listed_sum(): result, _ = lax.scan(advance, start_value, entries)  64.4 us
    dot_general x48, matrix products, advance(): jnp.dot(kernel_block(own_coords, coords), values, precision=HIGHEST)  53 us
    all_gather x1, blocking collectives, per_device(): lax.all_gather(top_rows_own, 'leaf', axis=0, tiled=True)  37 us
    sub x80, local copies, waits for them, and re-layouts, kernel_block(): offset_gap = left_pts[axis_id][:, None] - right_pts[axis_id][None, :]  36.5 us
    dynamic_slice x48, local copies, waits for them, and re-layouts, listed_sum(): result, _ = lax.scan(advance, start_value, entries)  35.2 us
    ppermute x9, waiting for transfers between devices, from_partner(): return lax.ppermute(value, axis, pairs)  11.3 us
  transfers between devices with their start and end apart: 57, of which 23 were waited for; matrix products, arithmetic and copies ran while one was open for 30% of the time, Pallas kernels for 0%

commit v1 on v0

v1 whole, which is shorter than its diff:
```python
import functools

import jax
import jax.numpy as jnp
from jax import lax
from jax.experimental import pallas as pl
from jax.experimental.pallas import tpu as pltpu
from jax.sharding import PartitionSpec as P

INV_FOUR_PI = 0.07957747154594767
DELTA_SQ = 0.01
HIGHEST = lax.Precision.HIGHEST
AXIS = "leaf"

PLANE = 8
NEAR_SLOTS = 16
FAR_SLOTS = 8

VEC = 0
META = 512
COEF = 528
CPAIR = 656
EPAIR = 720
EQUAD = 784
SHIP = 816

VMEM = pl.BlockSpec(memory_space=pltpu.VMEM)
SMEM = pl.BlockSpec(memory_space=pltpu.SMEM)


def call(body, outs, ins, n_smem=0, scratch=(), flops=0, nbytes=0):
    return pl.pallas_call(
        body,
        out_shape=outs,
        in_specs=[SMEM] * n_smem + [VMEM] * (len(ins) - n_smem),
        out_specs=jax.tree.map(lambda _: VMEM, outs),
        scratch_shapes=list(scratch),
        compiler_params=pltpu.CompilerParams(vmem_limit_bytes=32 * 1024 * 1024),
        cost_estimate=pl.CostEstimate(flops=flops, bytes_accessed=nbytes, transcendentals=0),
    )(*ins)


def f32(*shape):
    return jax.ShapeDtypeStruct(shape, jnp.float32)


def dot(a, b):
    return jnp.dot(a, b, precision=HIGHEST, preferred_element_type=jnp.float32)


def dot_t(a, b):
    return lax.dot_general(
        a, b, (((0,), (0,)), ((), ())), precision=HIGHEST, preferred_element_type=jnp.float32
    )


def columns(rows):
    pad = jnp.zeros((128 - rows.shape[0], 128), jnp.float32)
    return jnp.concatenate([rows, pad], axis=0).T


def green(cols, rows):
    dx = cols[0] - rows[0]
    dy = cols[1] - rows[1]
    dz = cols[2] - rows[2]
    return lax.rsqrt((dx * dx + dy * dy) + dz * dz + DELTA_SQ)


def green_of(cols, skel):
    return green([cols[:, a : a + 1] for a in range(3)], [skel[a : a + 1, :] for a in range(3)])


def window_bits(list_ref, row, start, count, base):
    bits = jnp.int32(0)
    for e in range(count):
        entry = list_ref[row, start + e]
        shift = jnp.clip(entry - base, 0, 31)
        bits = bits | jnp.where(entry >= 0, jnp.left_shift(jnp.int32(1), shift), 0)
    return bits


def has(bits, place):
    return (jnp.right_shift(bits, jnp.clip(place, 0, 31)) & 1) == 1


def chips_of(device):
    chip = device // 2
    place = chip % 4
    odd = (chip // 4) % 2
    out = [chip, chip ^ 1, chip ^ 2, chip ^ 3, chip ^ 4, chip + jnp.where(odd == 1, 4, -4)]
    for m in (1, 2, 3):
        other = place ^ m
        out.append((chip ^ m) + jnp.where(place < other, -4, 4))
    return out


def prepare_kernel(idx, vec, pts, skel, basis, move, epair, equad, ship, keep, send):
    core = idx[0] % 2
    ship[VEC : VEC + 512, :] = vec[0]
    zero = jnp.zeros((1, 128), jnp.float32)
    pieces = []
    for k in range(4):
        for a in range(3):
            pieces.append(pts[0, a : a + 1, 128 * k : 128 * (k + 1)])
        pieces.append(skel[0, k : k + 1, :] if k < 3 else zero)
    meta = jnp.concatenate(pieces, axis=0)
    ship[META : META + 16, :] = meta
    coef = dot_t(basis[0], vec[0])
    ship[COEF : COEF + 128, :] = coef
    up = dot_t(move[0], coef)
    ship[CPAIR : CPAIR + 64, :] = jnp.zeros((64, 128), jnp.float32)
    ship[EPAIR : EPAIR + 64, :] = epair[...]
    ship[EQUAD : EQUAD + 32, :] = equad[...]
    low, high = up[:64], up[64:]
    keep[...] = jnp.where(core == 0, low, high)
    send[0:64, :] = jnp.where(core == 0, high, low)
    send[64:80, :] = meta


def near_kernel(slots, first, idx, own_list, sib_list, meta_own, meta_sib, *refs):
    n = len(slots)
    blocks = refs[:n]
    refs = refs[n:]
    if not first:
        total_in, refs = refs[0], refs[1:]
    total, values, cols, high, low = refs
    device = idx[0]
    core = device % 2
    if first:
        total[...] = jnp.zeros_like(total)
    else:
        total[...] = total_in[...]
    chips = chips_of(device)
    bits = []
    for s, (listed, leaf) in enumerate(((own_list, device), (sib_list, device ^ 1))):
        bits.append(window_bits(listed, 0, 0, NEAR_SLOTS, leaf - 9))
    cols[0:128, :] = columns(meta_own[...])
    cols[128:256, :] = columns(meta_sib[...])
    for b, slot in enumerate(slots):
        leaf = 2 * chips[slot] + core
        block = blocks[b]
        v = block[VEC : VEC + 512, :] * INV_FOUR_PI
        vh = v.astype(jnp.bfloat16)
        values[:, 0:128] = vh
        values[:, 128:256] = (v - vh.astype(jnp.float32)).astype(jnp.bfloat16)
        for s in range(2):

            @pl.when(has(bits[s], leaf - ((device ^ s) - 9)))
            def _(block=block, s=s):
                for i in range(4):
                    col = [
                        jnp.broadcast_to(cols[128 * s : 128 * (s + 1), 4 * i + a : 4 * i + a + 1], (128, 128))
                        for a in range(3)
                    ]
                    for k in range(4):
                        row = [block[META + 4 * k + a : META + 4 * k + a + 1, :] for a in range(3)]
                        g = green(col, row)
                        gh = g.astype(jnp.bfloat16)
                        gl = (g - gh.astype(jnp.float32)).astype(jnp.bfloat16)
                        high[128 * i : 128 * (i + 1), 128 * k : 128 * (k + 1)] = gh
                        low[128 * i : 128 * (i + 1), 128 * k : 128 * (k + 1)] = gl
                both = jnp.dot(high[...], values[...], preferred_element_type=jnp.float32)
                rest = jnp.dot(low[...], values[:, 0:128], preferred_element_type=jnp.float32)
                total[512 * s : 512 * (s + 1), :] += both[:, 0:128] + (both[:, 128:256] + rest)


def near(slots, idx, own_list, sib_list, meta_own, meta_sib, blocks, total):
    first = total is None
    ins = [idx, own_list, sib_list, meta_own, meta_sib, *blocks] + ([] if first else [total])
    return call(
        functools.partial(near_kernel, slots, first),
        f32(1024, 128),
        ins,
        n_smem=3,
        scratch=[
            pltpu.VMEM((512, 256), jnp.bfloat16),
            pltpu.VMEM((256, 128), jnp.float32),
            pltpu.VMEM((512, 512), jnp.bfloat16),
            pltpu.VMEM((512, 512), jnp.bfloat16),
        ],
        flops=len(slots) * 2 * 6 * 512 * 512 * 128,
        nbytes=(1024 * 2 + 512 * len(slots)) * 512,
    )


def quad_kernel(own, bx, by, bd, out):
    part = [
        dot_t(b[EPAIR : EPAIR + 64, :], b[CPAIR : CPAIR + 64, :]) for b in (own, bx, by, bd)
    ]
    out[0:128, :] = part[0] + part[1]
    out[128:256, :] = part[2] + part[3]
    for j, b in enumerate((own, bx, by, bd)):
        out[256 + 32 * j : 288 + 32 * j, :] = b[EQUAD : EQUAD + 32, :]
    out[384:448, :] = own[EPAIR : EPAIR + 64, :]


def top_kernel(idx, mine, theirs, send, ctx, eq_own, eq_oth, coefs):
    device = idx[0]
    core = device % 2
    place = (device // 2) % 4
    for j, eq in enumerate((eq_own, eq_own, eq_oth, eq_oth)):
        parity = (place ^ j) % 2
        mine_at = pl.multiple_of((2 * parity + core) * 32, 32)
        sib_at = pl.multiple_of((2 * parity + 1 - core) * 32, 32)
        eq[pl.ds(mine_at, 32), :] = mine[256 + 32 * j : 288 + 32 * j, :]
        eq[pl.ds(sib_at, 32), :] = theirs[256 + 32 * j : 288 + 32 * j, :]
    quad_own = mine[0:128, :] + theirs[0:128, :]
    quad_oth = mine[128:256, :] + theirs[128:256, :]
    lower = place < 2
    coefs[0:128, :] = jnp.where(lower, quad_own, quad_oth)
    coefs[128:256, :] = jnp.where(lower, quad_oth, quad_own)
    coefs[256:384, :] = dot_t(eq_own[...], quad_own) + dot_t(eq_oth[...], quad_oth)
    coefs[384:512, :] = quad_oth
    half = pl.multiple_of(core * 64, 64)
    for j in range(3):
        send[64 * j : 64 * (j + 1), :] = coefs[pl.ds(128 * j + half, 64), :]
    ctx[0:128, :] = eq_own[...]
    ctx[pl.ds(128 + half, 64), :] = mine[384:448, :]
    ctx[pl.ds(128 + 64 - half, 64), :] = theirs[384:448, :]
    ctx[256:320, :] = coefs[pl.ds(384 + half, 64), :]


def upper_kernel(idx, far_quad, far_top, ctx, r1, r2, r3, skel_quad, skel_top, out, wide, values):
    device = idx[0]
    half = pl.multiple_of((device % 2) * 64, 64)
    plane = device // 8
    quad = device // 4
    received = (r1, r2, r3)
    values[...] = jnp.zeros_like(values)
    bits = window_bits(far_top, plane, 0, FAR_SLOTS, 0)
    cols = columns(skel_top[plane])
    for j, r in enumerate(received):
        other = plane ^ (j + 1)
        values[pl.ds(128 * j + half, 64), :] = r[128:192, :]
        g = green_of(cols, skel_top[other])
        wide[:, 128 * j : 128 * (j + 1)] = jnp.where(has(bits, other), g, 0.0)
    local_top = dot(wide[:, 0:384], values[0:384, :]) * INV_FOUR_PI
    bits = window_bits(far_quad, quad, 0, FAR_SLOTS, quad - 4)
    cols = columns(skel_quad[quad])
    others = [quad ^ 1] + [2 * (plane ^ (j + 1)) + k for j in range(3) for k in range(2)]
    sources = [ctx[256:320, :]] + [r[64 * k : 64 * (k + 1), :] for r in received for k in range(2)]
    for j, (other, source) in enumerate(zip(others, sources)):
        values[pl.ds(128 * j + half, 64), :] = source
        g = green_of(cols, skel_quad[other])
        ok = has(bits, other - quad + 4) & (other >= quad - 4) & (other <= quad + 4)
        wide[:, 128 * j : 128 * (j + 1)] = jnp.where(ok, g, 0.0)
    out[...] = dot(wide[...], values[...]) * INV_FOUR_PI + dot(ctx[0:128, :], local_top)


def lower_kernel(idx, own_list, sib_list, far_pair, ctx, local_quad, meta_sib, skel_pair, *refs):
    blocks = refs[:9]
    out, wide, values = refs[9:]
    device = idx[0]
    core = device % 2
    half = pl.multiple_of(core * 64, 64)
    chips = chips_of(device)
    chip = device // 2
    n_chips = skel_pair.shape[0]
    values[...] = jnp.zeros_like(values)
    bits = window_bits(far_pair, chip, 0, FAR_SLOTS, chip - 4)
    cols = columns(skel_pair[chip])
    for j in range(1, 9):
        other = chips[j]
        values[pl.ds(128 * (j - 1) + half, 64), :] = blocks[j][CPAIR : CPAIR + 64, :]
        g = green_of(cols, skel_pair[jnp.clip(other, 0, n_chips - 1)])
        wide[:, 128 * (j - 1) : 128 * j] = jnp.where(has(bits, other - chip + 4), g, 0.0)
    out[256:384, :] = dot(wide[:, 0:1024], values[0:1024, :]) * INV_FOUR_PI + dot(
        ctx[128:256, :], local_quad[...]
    )
    for j in range(9):
        values[128 * j : 128 * (j + 1), :] = blocks[j][COEF : COEF + 128, :]
    for s, (listed, meta, base) in enumerate(
        ((own_list, blocks[0], META), (sib_list, meta_sib, 64))
    ):
        leaf = device ^ s
        bits = window_bits(listed, 0, NEAR_SLOTS, FAR_SLOTS, leaf - 9)
        skel = jnp.concatenate([meta[base + 4 * a + 3 : base + 4 * a + 4, :] for a in range(3)], axis=0)
        cols = columns(skel)
        for j in range(9):
            b = blocks[j]
            rows = [b[META + 4 * a + 3 : META + 4 * a + 4, :] for a in range(3)]
            g = green([cols[:, a : a + 1] for a in range(3)], rows)
            ok = has(bits, 2 * chips[j] + core - (leaf - 9))
            wide[:, 128 * j : 128 * (j + 1)] = jnp.where(ok, g, 0.0)
        out[128 * s : 128 * (s + 1), :] = dot(wide[...], values[...]) * INV_FOUR_PI


def final_kernel(total, low, got, move, basis, out):
    local_pair = low[256:384, :] + got[640:768, :]
    local = low[0:128, :] + got[512:640, :] + dot(move[0], local_pair)
    out[0] = total[0:512, :] + got[0:512, :] + dot(basis[0], local)


def permute(value, target):
    n = lax.axis_size(AXIS)
    pairs = [(i, target(i)) for i in range(n)]
    return lax.ppermute(value, AXIS, [(i, j) for i, j in pairs if 0 <= j < n and i != j])


def swap(value, mask):
    return permute(value, lambda i: i ^ mask)


def listed_sum(own, entries, skels, coefs):
    def advance(running, partner):
        at = jnp.maximum(partner, 0)
        g = INV_FOUR_PI * green_of(own.T, skels[at])
        contrib = jnp.dot(g, coefs[at], precision=HIGHEST)
        return running + jnp.where(partner >= 0, contrib, 0.0), None

    return lax.scan(advance, jnp.zeros(coefs.shape[1:], jnp.float32), entries)[0]


def upper_anywhere(device, send, ctx, far_quad, far_top, skel_quad, skel_top):
    n = lax.axis_size(AXIS)
    rows = send.shape[0] // 4
    part = lax.dynamic_slice_in_dim(send, (device // 2 % 4) * rows, rows, 0)
    every = lax.all_gather(part, AXIS, axis=0, tiled=True)
    every = every.reshape(n // PLANE, 4, 2, rows, 128).transpose(0, 2, 1, 3, 4)
    every = every.reshape(n // PLANE, 2, 3, 64, 128).transpose(0, 2, 1, 3, 4)
    every = every.reshape(n // PLANE, 3, 128, 128)
    plane, quad = device // 8, device // 4
    local_top = listed_sum(skel_top[plane], far_top[plane], skel_top, every[:, 2])
    quads = every[:, :2].reshape(n // 4, 128, 128)
    far = listed_sum(skel_quad[quad], far_quad[quad], skel_quad, quads)
    whole = far + jnp.dot(ctx[0:128], local_top, precision=HIGHEST)
    return jnp.where(device % 2 == 0, whole, 0.0)


def per_device(
    vectors,
    points,
    leaf_basis,
    transfer_leaf,
    transfer_pair,
    transfer_quad,
    skel_leaf,
    skel_pair,
    skel_quad,
    skel_top,
    near_list,
    far_leaf,
    far_pair,
    far_quad,
    far_top,
):
    n = lax.axis_size(AXIS)
    device = lax.axis_index(AXIS)
    idx = device.reshape(1).astype(jnp.int32)
    own_list = jnp.concatenate([near_list, far_leaf], axis=1)
    sib_list = swap(own_list, 1)

    ship, keep, send = call(
        prepare_kernel,
        (f32(SHIP, 128), f32(64, 128), f32(80, 128)),
        [idx, vectors, points, skel_leaf, leaf_basis, transfer_leaf, transfer_pair, transfer_quad],
        n_smem=1,
        flops=2 * 6 * 640 * 128 * 128,
        nbytes=1 << 20,
    )
    got = swap(send, 1)
    ship = lax.dynamic_update_slice(ship, keep + got[0:64], (CPAIR, 0))

    bd = swap(ship, 6)
    bx = swap(ship, 2)
    by = swap(ship, 4)
    even = swap(ship, 8)
    odd = permute(ship, lambda i: i + 8 if i // 8 % 2 == 1 else i - 8)

    args = (idx, own_list, sib_list, ship[META : META + 16], got[64:80])
    total = near((0,), *args, [ship], None)

    plane_odd = device // 8 % 2 == 1
    place = device // 2 % 4
    crossed = []
    for m in (1, 2):
        lower = (place ^ m) < place
        crossed.append(swap(jnp.where(lower == plane_odd, even[:EPAIR], odd[:EPAIR]), 2 * m))
    cx, cy = crossed
    cd = permute(bd, lambda i: i + 8 if i // 2 % 4 < 2 else i - 8)

    half = call(quad_kernel, f32(448, 128), [ship, bx, by, bd], flops=8 * 6 * 64 * 128 * 128)
    half_got = swap(half, 1)
    up, ctx = call(
        top_kernel,
        (f32(192, 128), f32(320, 128)),
        [idx, half, half_got],
        n_smem=1,
        scratch=[
            pltpu.VMEM((128, 128), jnp.float32),
            pltpu.VMEM((128, 128), jnp.float32),
            pltpu.VMEM((512, 128), jnp.float32),
        ],
        flops=4 * 6 * 128**3,
    )
    if n == 4 * PLANE:
        r1, r2, r3 = [swap(up, PLANE * m) for m in (1, 2, 3)]
        local_quad = call(
            upper_kernel,
            f32(128, 128),
            [idx, far_quad, far_top, ctx, r1, r2, r3, skel_quad, skel_top],
            n_smem=3,
            scratch=[pltpu.VMEM((128, 896), jnp.float32), pltpu.VMEM((896, 128), jnp.float32)],
            flops=2 * 6 * 11 * 128**3,
        )
    else:
        local_quad = upper_anywhere(device, up, ctx, far_quad, far_top, skel_quad, skel_top)

    total = near((1, 2), *args, [bx, by], total)
    total = near((3,), *args, [bd], total)
    total = near((4, 5), *args, [even, odd], total)
    total = near((6, 7), *args, [cx, cy], total)
    total = near((8,), *args, [cd], total)

    low = call(
        lower_kernel,
        f32(384, 128),
        [idx, own_list, sib_list, far_pair, ctx, local_quad, got, skel_pair]
        + [ship, bx, by, bd, even, odd, cx, cy, cd],
        n_smem=4,
        scratch=[pltpu.VMEM((128, 1152), jnp.float32), pltpu.VMEM((1152, 128), jnp.float32)],
        flops=2 * 6 * 28 * 128**3,
    )
    share = swap(jnp.concatenate([total[512:], low[128:]], axis=0), 1)
    return call(
        final_kernel,
        f32(1, 512, 128),
        [total, low, share, transfer_leaf, leaf_basis],
        flops=2 * 6 * 640 * 128 * 128,
    )


def solution(mesh):
    placed = (
        P("leaf", None, None),
        P("leaf", None, None),
        P("leaf", None, None),
        P("leaf", None, None),
        P("leaf", None),
        P("leaf", None),
        P("leaf", None, None),
        P(),
        P(),
        P(),
        P("leaf", None),
        P("leaf", None),
        P(),
        P(),
        P(),
    )
    return jax.shard_map(
        per_device, mesh=mesh, in_specs=placed, out_specs=P("leaf", None, None), check_vma=False
    )
```

time: 461 us -> 77.7 us (0.17)
  the two profiles are of different devices: /device:TPU:0 before, /device:TPU:9 now
where the time goes in v1:
time: 77.7 us
  Pallas kernels  27.8 us (36%)
  waiting for transfers between devices  20.6 us (27%)
  starting transfers between devices  17.7 us (23%)
  local copies, waits for them, and re-layouts  9.73 us (13%)
  other arithmetic  1.63 us (2%)
    pallas_call x12, Pallas kernels, call(): pl.pallas_call(body, out_shape=outs, in_specs=[SMEM] * n_smem + [VMEM] *...  27.8 us
    ppermute x15, waiting for transfers between devices, permute(): lax.ppermute(value, AXIS, [(i, j) for i, j in pairs if 0 <= j < n and i !...  20.6 us
    ppermute x15, starting transfers between devices, permute(): lax.ppermute(value, AXIS, [(i, j) for i, j in pairs if 0 <= j < n and i !...  17.7 us
    unnamed x50, local copies, waits for them, and re-layouts  8.14 us
  transfers between devices with their start and end apart: 15, of which 6 were waited for; matrix products, arithmetic and copies ran while one was open for 6% of the time, Pallas kernels for 25%

profile of v1, /device:TPU:9, one launch (start us, length us, event | category | flops | bytes accessed | tf_op | source)
XLA Modules:
  0.0 77.7 jit_solution(11933282138408107860)
XLA Ops:
  0.0 0.7 copy.16.pts
  0.7 0.0 copy-start.2
  0.7 0.9 %copy-done.2 = f32[1,512,128]{2,1,0:T(8,128)S(1)} copy-done((f32[1,512,128]{2,1,0:T(8,128)S(1)}, f32[1,512,128]{2,1,0:T(8,128)}, u32[]{:S(2)}) %copy-start.2) | copy-done | bytes 262168
  1.7 0.9 %copy-done.4 = f32[1,512,128]{2,1,0:T(8,128)S(1)} copy-done((f32[1,512,128]{2,1,0:T(8,128)S(1)}, f32[1,512,128]{2,1,0:T(8,128)}, u32[]{:S(2)}) %copy-start.4) | copy-done | bytes 262168
  2.6 0.8 %copy-done.5 = f32[1,128,128]{2,1,0:T(8,128)S(1)} copy-done((f32[1,128,128]{2,1,0:T(8,128)S(1)}, f32[1,128,128]{2,1,0:T(8,128)}, u32[]{:S(2)}) %copy-start.5) | copy-done | bytes 65560
  3.5 0.8 copy-done.10
  4.2 0.7 shard_map.145
  4.9 0.7 collective-permute-start.1
  5.7 0.9 %collective-permute-done.1.meta_sib = f32[80,128]{1,0:T(8,128)S(1)} collective-permute-done((f32[80,128]{1,0:T(8,128)S(1)}, f32[80,128]{1,0:T(8,128)S(1)}, u32[]{:S(2)}, u32[]{:S(2)}) %collective-permute-start.1) | collective-permute-done | bytes 40992 | tf_op jit(solution)/shard_map/ppermute | solution.py:297
  6.5 0.6 copy-done.7
  7.2 2.2 %collective-permute-start.2 = (f32[816,128]{1,0:T(8,128)S(1)}, f32[816,128]{1,0:T(8,128)S(1)}, u32[]{:S(2)}, u32[]{:S(2)}) collective-permute-start(f32[816,128]{1,0:T(8,128)S(1)} %fusion.refs_0_.own), channel_id=1, source_target_pairs={{0,6},{1,7},{2,4},{3,5},{4,2},{5,3},{6,0},{7,1},{8,14},{9,15},{10,... | collective-permute-start | bytes 1253384 | tf_op jit(solution)/shard_map/ppermute | solution.py:297
  9.3 0.3 collective-permute-start.8
  9.6 0.2 collective-permute-start.9
  9.8 0.0 collective-permute-start.4
  9.8 4.5 %collective-permute-start.5 = (f32[816,128]{1,0:T(8,128)S(1)}, f32[816,128]{1,0:T(8,128)S(1)}, u32[]{:S(2)}, u32[]{:S(2)}) collective-permute-start(f32[816,128]{1,0:T(8,128)S(1)} %fusion.refs_0_.own), channel_id=1, source_target_pairs={{8,16},{9,17},{10,18},{11,19},{12,20},{13,21},{14,22},{15,23},{16,... | collective-permute-start | bytes 1253384 | tf_op jit(solution)/shard_map/ppermute | solution.py:297
  14.4 4.6 %collective-permute-done.2.refs_0_.bd.refs_3_ = f32[816,128]{1,0:T(8,128)S(1)} collective-permute-done((f32[816,128]{1,0:T(8,128)S(1)}, f32[816,128]{1,0:T(8,128)S(1)}, u32[]{:S(2)}, u32[]{:S(2)}) %collective-permute-start.2) | collective-permute-done | bytes 417824 | tf_op jit(solution)/shard_map/ppermute | solution.py:297
  19.0 9.0 %collective-permute-done.8.refs_0_.bx.refs_1_ = f32[816,128]{1,0:T(8,128)S(1)} collective-permute-done((f32[816,128]{1,0:T(8,128)S(1)}, f32[816,128]{1,0:T(8,128)S(1)}, u32[]{:S(2)}, u32[]{:S(2)}) %collective-permute-start.8) | collective-permute-done | bytes 417824 | tf_op jit(solution)/shard_map/ppermute | solution.py:297
  28.0 0.6 collective-permute-done.9.refs_1_.by.refs_2_
  28.6 0.4 shard_map.152.mine
  29.0 0.7 collective-permute-start.10
  29.7 0.0 collective-permute-done.4.refs_0_.refs_4_
  29.7 0.0 collective-permute-done.5.refs_1_.refs_5_
  29.7 0.0 copy-start.21
  29.7 0.0 copy-start.17
  29.7 1.0 %slice_select_fusion = (f32[720,128]{1,0:T(8,128)}, f32[720,128]{1,0:T(8,128)}) fusion(f32[816,128]{1,0:T(8,128)S(1)} %collective-permute-done.5.refs_1_.refs_5_, f32[816,128]{1,0:T(8,128)S(1)} %collective-permute-done.4.refs_0_.refs_4_, pred[]{:T(512)S(6)} %eq.14, pred[]{:T(512)S(6)} %eq.13), kind=kLoop, calls=%fused_computation.1 | loop fusion | flops 184320 | bytes 1474562 | tf_op jit(solution)/shard_map/jit(_where)/select_n | solution.py:378
  30.7 1.2 %collective-permute-start.6 = (f32[720,128]{1,0:T(8,128)}, f32[720,128]{1,0:T(8,128)S(1)}, u32[]{:S(2)}, u32[]{:S(2)}) collective-permute-start(f32[720,128]{1,0:T(8,128)} %get-tuple-element.16), channel_id=1, source_target_pairs={{0,2},{1,3},{2,0},{3,1},{4,6},{5,7},{6,4},{7,5},{8,10},{9,11},{10,... | collective-permute-start | bytes 1105928 | tf_op jit(solution)/shard_map/ppermute | solution.py:297
  31.9 1.1 %collective-permute-start.7 = (f32[720,128]{1,0:T(8,128)}, f32[720,128]{1,0:T(8,128)}, u32[]{:S(2)}, u32[]{:S(2)}) collective-permute-start(f32[720,128]{1,0:T(8,128)} %get-tuple-element.15), channel_id=1, source_target_pairs={{0,4},{1,5},{2,6},{3,7},{4,0},{5,1},{6,2},{7,3},{8,12},{9,13},{10,... | collective-permute-start | bytes 1105928 | tf_op jit(solution)/shard_map/ppermute | solution.py:297
  33.0 3.2 %collective-permute-start.3 = (f32[816,128]{1,0:T(8,128)S(1)}, f32[816,128]{1,0:T(8,128)S(1)}, u32[]{:S(2)}, u32[]{:S(2)}) collective-permute-start(f32[816,128]{1,0:T(8,128)S(1)} %collective-permute-done.2.refs_0_.bd.refs_3_), channel_id=1, source_target_pairs={{0,8},{1,9},{2,10},{3,11},{8,16},{9,17},{10,18},{11,19},{12,4},{13... | collective-permute-start | bytes 1253384 | tf_op jit(solution)/shard_map/ppermute | solution.py:297
  36.2 0.6 pad_add_fusion.own_list
  36.9 0.9 %collective-permute-start = (s32[1,24]{1,0:T(1,128)}, s32[1,24]{1,0:T(1,128)}, u32[]{:S(2)}, u32[]{:S(2)}) collective-permute-start(s32[1,24]{1,0:T(1,128)} %pad_add_fusion.own_list), channel_id=1, source_target_pairs={{0,1},{1,0},{2,3},{3,2},{4,5},{5,4},{6,7},{7,6},{8,9},{9,8},{10,11... | collective-permute-start | bytes 296 | tf_op jit(solution)/shard_map/ppermute | solution.py:297
  37.7 0.6 copy.18.skel_quad
  38.4 0.6 copy.19.skel_top
  39.0 1.4 %copy.20.far_pair = s32[16,8]{1,0:T(8,128)} copy(s32[16,8]{0,1:T(8,128)} %param.27) | data formatting | bytes 1024 | tf_op args[12]
  40.3 0.7 slice.32.meta_sib
  41.0 0.0 collective-permute-done.10.theirs
  41.0 1.3 %shard_map.153 = (f32[192,128]{1,0:T(8,128)S(1)}, f32[320,128]{1,0:T(8,128)S(1)}) custom-call(s32[1]{0:T(128)} %bitcast.idx, f32[448,128]{1,0:T(8,128)S(1)} %shard_map.152.mine, f32[448,128]{1,0:T(8,128)} %collective-permute-done.10.theirs), custom_call_target="tpu_custom_call" | custom-call | flops 50331648 | tf_op jit(solution)/shard_map/pallas_call | solution.py:32
  42.3 0.3 collective-permute-start.11
  42.6 0.0 collective-permute-done.sib_list
  42.6 2.7 %shard_map.146.refs_2_ = f32[1024,128]{1,0:T(8,128)S(1)} custom-call(s32[1]{0:T(128)} %bitcast.idx, s32[1,24]{1,0:T(1,128)} %pad_add_fusion.own_list, s32[1,24]{1,0:T(1,128)} %collective-permute-done.sib_list, f32[16,128]{1,0:T(8,128)S(1)} %slice.31.meta_own, f32[16,128]{1,0:T(8,128)S(1)} %slice.32.meta_sib, f32[816,128]{1,0:T(8,128)S(1)} %fusion.refs_0_.own), custom_call_target="tpu_custom_call" | custom-call | flops 402653184 | bytes 1310720 | tf_op jit(solution)/shard_map/pallas_call | solution.py:32
  45.3 3.7 %shard_map.147.refs_1_ = f32[1024,128]{1,0:T(8,128)S(1)} custom-call(s32[1]{0:T(128)} %bitcast.idx, s32[1,24]{1,0:T(1,128)} %pad_add_fusion.own_list, s32[1,24]{1,0:T(1,128)} %collective-permute-done.sib_list, f32[16,128]{1,0:T(8,128)S(1)} %slice.31.meta_own, f32[16,128]{1,0:T(8,128)S(1)} %slice.32.meta_sib, ...), custom_call_target="tpu_custom_call" | custom-call | flops 805306368 | bytes 1572864 | tf_op jit(solution)/shard_map/pallas_call | solution.py:32
  49.0 2.4 %collective-permute-start.12 = (f32[192,128]{1,0:T(8,128)S(1)}, f32[192,128]{1,0:T(8,128)S(1)}, u32[]{:S(2)}, u32[]{:S(2)}) collective-permute-start(f32[192,128]{1,0:T(8,128)S(1)} %get-tuple-element.14), channel_id=1, source_target_pairs={{0,16},{1,17},{2,18},{3,19},{4,20},{5,21},{6,22},{7,23},{8,24},{9,... | collective-permute-start | bytes 294920 | tf_op jit(solution)/shard_map/ppermute | solution.py:297
  51.3 0.0 collective-permute-done.11.r1
  51.3 0.0 collective-permute-start.13
  51.4 2.7 %shard_map.148.refs_2_ = f32[1024,128]{1,0:T(8,128)S(1)} custom-call(s32[1]{0:T(128)} %bitcast.idx, s32[1,24]{1,0:T(1,128)} %pad_add_fusion.own_list, s32[1,24]{1,0:T(1,128)} %collective-permute-done.sib_list, f32[16,128]{1,0:T(8,128)S(1)} %slice.31.meta_own, f32[16,128]{1,0:T(8,128)S(1)} %slice.32.meta_sib, ...), custom_call_target="tpu_custom_call" | custom-call | flops 402653184 | bytes 1310720 | tf_op jit(solution)/shard_map/pallas_call | solution.py:32
  54.1 0.0 copy-start.14
  54.1 0.0 copy-start.15
  54.1 2.2 %shard_map.149.refs_2_ = f32[1024,128]{1,0:T(8,128)S(1)} custom-call(s32[1]{0:T(128)} %bitcast.idx, s32[1,24]{1,0:T(1,128)} %pad_add_fusion.own_list, s32[1,24]{1,0:T(1,128)} %collective-permute-done.sib_list, f32[16,128]{1,0:T(8,128)S(1)} %slice.31.meta_own, f32[16,128]{1,0:T(8,128)S(1)} %slice.32.meta_sib, ...), custom_call_target="tpu_custom_call" | custom-call | flops 805306368 | bytes 1572864 | tf_op jit(solution)/shard_map/pallas_call | solution.py:32
  56.3 0.0 collective-permute-done.12.r2
  56.3 3.7 %collective-permute-done.13.r3 = f32[192,128]{1,0:T(8,128)S(1)} collective-permute-done((f32[192,128]{1,0:T(8,128)S(1)}, f32[192,128]{1,0:T(8,128)S(1)}, u32[]{:S(2)}, u32[]{:S(2)}) %collective-permute-start.13) | collective-permute-done | bytes 98336 | tf_op jit(solution)/shard_map/ppermute | solution.py:297
  60.0 1.8 %shard_map.154.local_quad = f32[128,128]{1,0:T(8,128)S(1)} custom-call(s32[1]{0:T(128)} %bitcast.idx, s32[8,8]{1,0:T(8,128)S(1)} %copy-done.14, s32[4,8]{1,0:T(4,128)S(1)} %copy-done.15, f32[320,128]{1,0:T(8,128)S(1)} %get-tuple-element.13.ctx, f32[192,128]{1,0:T(8,128)S(1)} %collective-permute-done.11.r1, f32[192,128]{1,0:T(8,128)S(1)} %collective-permute-done.12.r2, ...), custom_call_target="tpu_custom_call" | custom-call | flops 276824064 | tf_op jit(solution)/shard_map/pallas_call | solution.py:32
  61.8 0.0 copy-start.8
  61.8 0.0 collective-permute-done.6.refs_0_.refs_6_
  61.8 0.0 collective-permute-done.7.refs_1_.refs_7_
  61.8 4.9 %shard_map.150.refs_1_ = f32[1024,128]{1,0:T(8,128)S(1)} custom-call(s32[1]{0:T(128)} %bitcast.idx, s32[1,24]{1,0:T(1,128)} %pad_add_fusion.own_list, s32[1,24]{1,0:T(1,128)} %collective-permute-done.sib_list, f32[16,128]{1,0:T(8,128)S(1)} %slice.31.meta_own, f32[16,128]{1,0:T(8,128)S(1)} %slice.32.meta_sib, ...), custom_call_target="tpu_custom_call" | custom-call | flops 805306368 | bytes 1572864 | tf_op jit(solution)/shard_map/pallas_call | solution.py:32
  66.8 0.0 collective-permute-done.3.refs_0_.refs_8_
  66.8 3.4 %shard_map.155.low = f32[384,128]{1,0:T(8,128)S(1)} custom-call(s32[1]{0:T(128)} %bitcast.idx, s32[1,24]{1,0:T(1,128)} %pad_add_fusion.own_list, s32[1,24]{1,0:T(1,128)} %collective-permute-done.sib_list, s32[16,8]{1,0:T(8,128)S(1)} %copy-done.9, f32[320,128]{1,0:T(8,128)S(1)} %get-tuple-element.13.ctx, f32[128,128]{1,0:T(8,128)S(1)} %shard_map.154.local_quad, ...), custom_call_target="tpu_custom_call" | custom-call | flops 704643072 | tf_op jit(solution)/shard_map/pallas_call | solution.py:32
  70.2 0.0 copy-start
  70.3 0.7 copy-done
  70.9 2.7 %shard_map.151.total = f32[1024,128]{1,0:T(8,128)S(1)} custom-call(s32[1]{0:T(128)} %bitcast.idx, s32[1,24]{1,0:T(1,128)} %pad_add_fusion.own_list, s32[1,24]{1,0:T(1,128)} %collective-permute-done.sib_list, f32[16,128]{1,0:T(8,128)S(1)} %slice.31.meta_own, f32[16,128]{1,0:T(8,128)S(1)} %slice.32.meta_sib, ...), custom_call_target="tpu_custom_call" | custom-call | flops 402653184 | bytes 1310720 | tf_op jit(solution)/shard_map/pallas_call | solution.py:32
  73.6 0.0 slice-start
  73.6 0.9 %slice-done = f32[256,128]{1,0:T(8,128)S(1)} async-done(((f32[384,128]{1,0:T(8,128)}), f32[256,128]{1,0:T(8,128)S(1)}, s32[]{:S(2)}) %slice-start) | async-done | bytes 131096 | tf_op jit(solution)/shard_map/slice | solution.py:424
  74.5 0.1 collective-permute-start.14
  74.6 1.7 %collective-permute-done.14.got = f32[768,128]{1,0:T(8,128)S(1)} collective-permute-done((f32[768,128]{1,0:T(8,128)S(1)}, f32[768,128]{1,0:T(8,128)S(1)}, u32[]{:S(2)}, u32[]{:S(2)}) %collective-permute-start.14) | collective-permute-done | bytes 393248 | tf_op jit(solution)/shard_map/ppermute | solution.py:297
  76.3 1.4 %shard_map.156 = f32[1,512,128]{2,1,0:T(8,128)} custom-call(f32[1024,128]{1,0:T(8,128)S(1)} %shard_map.151.total, f32[384,128]{1,0:T(8,128)S(1)} %copy-done.1, f32[768,128]{1,0:T(8,128)S(1)} %collective-permute-done.14.got, f32[1,128,128]{2,1,0:T(8,128)S(1)} %copy-done.6, f32[1,512,128]{2,1,0:T(8,128)S(1)} %copy-done.3), custom_call_target="tpu_custom_call" | custom-call | flops 125829120 | tf_op jit(solution)/shard_map/pallas_call | solution.py:32
  (37 shorter events, 0.1 us)
Async XLA Ops:
  0.0 0.7 copy-start.11
  0.0 0.7 copy-start.19
  0.7 1.0 %copy-start.2 = (f32[1,512,128]{2,1,0:T(8,128)S(1)}, f32[1,512,128]{2,1,0:T(8,128)}, u32[]{:S(2)}) copy-start(f32[1,512,128]{2,1,0:T(8,128)} %basis.3) | copy-start | bytes 786436
  1.7 0.9 %copy-start.4 = (f32[1,512,128]{2,1,0:T(8,128)S(1)}, f32[1,512,128]{2,1,0:T(8,128)}, u32[]{:S(2)}) copy-start(f32[1,512,128]{2,1,0:T(8,128)} %vec.1) | copy-start | bytes 786436
  2.6 0.8 %copy-start.5 = (f32[1,128,128]{2,1,0:T(8,128)S(1)}, f32[1,128,128]{2,1,0:T(8,128)}, u32[]{:S(2)}) copy-start(f32[1,128,128]{2,1,0:T(8,128)} %move.3) | copy-start | bytes 196612
  3.5 0.8 copy-start.10
  4.9 1.6 %collective-permute-start.1 = (f32[80,128]{1,0:T(8,128)S(1)}, f32[80,128]{1,0:T(8,128)S(1)}, u32[]{:S(2)}, u32[]{:S(2)}) collective-permute-start(f32[80,128]{1,0:T(8,128)S(1)} %get-tuple-element.12), channel_id=1, source_target_pairs={{0,1},{1,0},{2,3},{3,2},{4,5},{5,4},{6,7},{7,6},{8,9},{9,8},{10,11... | collective-permute-start | bytes 122888 | tf_op jit(solution)/shard_map/ppermute | solution.py:297
  6.5 0.6 copy-start.7
  7.2 11.8 %collective-permute-start.2 = (f32[816,128]{1,0:T(8,128)S(1)}, f32[816,128]{1,0:T(8,128)S(1)}, u32[]{:S(2)}, u32[]{:S(2)}) collective-permute-start(f32[816,128]{1,0:T(8,128)S(1)} %fusion.refs_0_.own), channel_id=1, source_target_pairs={{0,6},{1,7},{2,4},{3,5},{4,2},{5,3},{6,0},{7,1},{8,14},{9,15},{10,... | collective-permute-start | bytes 1253384 | tf_op jit(solution)/shard_map/ppermute | solution.py:297
  9.3 18.7 %collective-permute-start.8 = (f32[816,128]{1,0:T(8,128)S(1)}, f32[816,128]{1,0:T(8,128)S(1)}, u32[]{:S(2)}, u32[]{:S(2)}) collective-permute-start(f32[816,128]{1,0:T(8,128)S(1)} %fusion.refs_0_.own), channel_id=1, source_target_pairs={{0,2},{1,3},{2,0},{3,1},{4,6},{5,7},{6,4},{7,5},{8,10},{9,11},{10,... | collective-permute-start | bytes 1253384 | tf_op jit(solution)/shard_map/ppermute | solution.py:297
  9.6 19.0 %collective-permute-start.9 = (f32[816,128]{1,0:T(8,128)S(1)}, f32[816,128]{1,0:T(8,128)S(1)}, u32[]{:S(2)}, u32[]{:S(2)}) collective-permute-start(f32[816,128]{1,0:T(8,128)S(1)} %fusion.refs_0_.own), channel_id=1, source_target_pairs={{0,4},{1,5},{2,6},{3,7},{4,0},{5,1},{6,2},{7,3},{8,12},{9,13},{10,... | collective-permute-start | bytes 1253384 | tf_op jit(solution)/shard_map/ppermute | solution.py:297
  9.8 19.9 %collective-permute-start.4 = (f32[816,128]{1,0:T(8,128)S(1)}, f32[816,128]{1,0:T(8,128)S(1)}, u32[]{:S(2)}, u32[]{:S(2)}) collective-permute-start(f32[816,128]{1,0:T(8,128)S(1)} %fusion.refs_0_.own), channel_id=1, source_target_pairs={{0,8},{1,9},{2,10},{3,11},{4,12},{5,13},{6,14},{7,15},{8,0},{9,1},... | collective-permute-start | bytes 1253384 | tf_op jit(solution)/shard_map/ppermute | solution.py:297
  9.8 19.9 %collective-permute-start.5 = (f32[816,128]{1,0:T(8,128)S(1)}, f32[816,128]{1,0:T(8,128)S(1)}, u32[]{:S(2)}, u32[]{:S(2)}) collective-permute-start(f32[816,128]{1,0:T(8,128)S(1)} %fusion.refs_0_.own), channel_id=1, source_target_pairs={{8,16},{9,17},{10,18},{11,19},{12,20},{13,21},{14,22},{15,23},{16,... | collective-permute-start | bytes 1253384 | tf_op jit(solution)/shard_map/ppermute | solution.py:297
  29.0 12.0 %collective-permute-start.10 = (f32[448,128]{1,0:T(8,128)S(1)}, f32[448,128]{1,0:T(8,128)}, u32[]{:S(2)}, u32[]{:S(2)}) collective-permute-start(f32[448,128]{1,0:T(8,128)S(1)} %shard_map.152.mine), channel_id=1, source_target_pairs={{0,1},{1,0},{2,3},{3,2},{4,5},{5,4},{6,7},{7,6},{8,9},{9,8},{10,11... | collective-permute-start | bytes 688136 | tf_op jit(solution)/shard_map/ppermute | solution.py:297
  29.7 6.6 %copy-start.20 = (s32[1,8]{1,0:T(1,128)S(1)}, s32[1,8]{1,0:T(1,128)}, u32[]{:S(2)}) copy-start(s32[1,8]{1,0:T(1,128)} %param.26) | copy-start | bytes 100
  29.7 6.6 %copy-start.21 = (s32[1,16]{1,0:T(1,128)S(1)}, s32[1,16]{1,0:T(1,128)}, u32[]{:S(2)}) copy-start(s32[1,16]{1,0:T(1,128)} %param.25) | copy-start | bytes 196
  29.7 8.1 %copy-start.17 = (f32[8,3,128]{2,0,1:T(8,128)S(1)}, f32[8,3,128]{2,0,1:T(8,128)}, u32[]{:S(2)}) copy-start(f32[8,3,128]{2,0,1:T(8,128)} %param.23) | copy-start | bytes 36868
  30.7 8.3 %copy-start.16 = (f32[16,3,128]{2,0,1:T(8,128)S(1)}, f32[16,3,128]{2,0,1:T(8,128)}, u32[]{:S(2)}) copy-start(f32[16,3,128]{2,0,1:T(8,128)} %param.22) | copy-start | bytes 73732
  30.7 31.1 %collective-permute-start.6 = (f32[720,128]{1,0:T(8,128)}, f32[720,128]{1,0:T(8,128)S(1)}, u32[]{:S(2)}, u32[]{:S(2)}) collective-permute-start(f32[720,128]{1,0:T(8,128)} %get-tuple-element.16), channel_id=1, source_target_pairs={{0,2},{1,3},{2,0},{3,1},{4,6},{5,7},{6,4},{7,5},{8,10},{9,11},{10,... | collective-permute-start | bytes 1105928 | tf_op jit(solution)/shard_map/ppermute | solution.py:297
  31.9 29.9 %collective-permute-start.7 = (f32[720,128]{1,0:T(8,128)}, f32[720,128]{1,0:T(8,128)}, u32[]{:S(2)}, u32[]{:S(2)}) collective-permute-start(f32[720,128]{1,0:T(8,128)} %get-tuple-element.15), channel_id=1, source_target_pairs={{0,4},{1,5},{2,6},{3,7},{4,0},{5,1},{6,2},{7,3},{8,12},{9,13},{10,... | collective-permute-start | bytes 1105928 | tf_op jit(solution)/shard_map/ppermute | solution.py:297
  33.0 33.8 %collective-permute-start.3 = (f32[816,128]{1,0:T(8,128)S(1)}, f32[816,128]{1,0:T(8,128)S(1)}, u32[]{:S(2)}, u32[]{:S(2)}) collective-permute-start(f32[816,128]{1,0:T(8,128)S(1)} %collective-permute-done.2.refs_0_.bd.refs_3_), channel_id=1, source_target_pairs={{0,8},{1,9},{2,10},{3,11},{8,16},{9,17},{10,18},{11,19},{12,4},{13... | collective-permute-start | bytes 1253384 | tf_op jit(solution)/shard_map/ppermute | solution.py:297
  36.9 1.5 %copy-start.18 = (f32[4,3,128]{2,0,1:T(4,128)S(1)}, f32[4,3,128]{2,0,1:T(4,128)}, u32[]{:S(2)}) copy-start(f32[4,3,128]{2,0,1:T(4,128)} %param.24) | copy-start | bytes 18436
  36.9 5.7 %collective-permute-start = (s32[1,24]{1,0:T(1,128)}, s32[1,24]{1,0:T(1,128)}, u32[]{:S(2)}, u32[]{:S(2)}) collective-permute-start(s32[1,24]{1,0:T(1,128)} %pad_add_fusion.own_list), channel_id=1, source_target_pairs={{0,1},{1,0},{2,3},{3,2},{4,5},{5,4},{6,7},{7,6},{8,9},{9,8},{10,11... | collective-permute-start | bytes 296 | tf_op jit(solution)/shard_map/ppermute | solution.py:297
  42.3 9.0 %collective-permute-start.11 = (f32[192,128]{1,0:T(8,128)S(1)}, f32[192,128]{1,0:T(8,128)S(1)}, u32[]{:S(2)}, u32[]{:S(2)}) collective-permute-start(f32[192,128]{1,0:T(8,128)S(1)} %get-tuple-element.14), channel_id=1, source_target_pairs={{0,8},{1,9},{2,10},{3,11},{4,12},{5,13},{6,14},{7,15},{8,0},{9,1},... | collective-permute-start | bytes 294920 | tf_op jit(solution)/shard_map/ppermute | solution.py:297
  49.0 7.3 %collective-permute-start.12 = (f32[192,128]{1,0:T(8,128)S(1)}, f32[192,128]{1,0:T(8,128)S(1)}, u32[]{:S(2)}, u32[]{:S(2)}) collective-permute-start(f32[192,128]{1,0:T(8,128)S(1)} %get-tuple-element.14), channel_id=1, source_target_pairs={{0,16},{1,17},{2,18},{3,19},{4,20},{5,21},{6,22},{7,23},{8,24},{9,... | collective-permute-start | bytes 294920 | tf_op jit(solution)/shard_map/ppermute | solution.py:297
  51.3 8.7 %collective-permute-start.13 = (f32[192,128]{1,0:T(8,128)S(1)}, f32[192,128]{1,0:T(8,128)S(1)}, u32[]{:S(2)}, u32[]{:S(2)}) collective-permute-start(f32[192,128]{1,0:T(8,128)S(1)} %get-tuple-element.14), channel_id=1, source_target_pairs={{0,24},{1,25},{2,26},{3,27},{4,28},{5,29},{6,30},{7,31},{8,16},{9,... | collective-permute-start | bytes 294920 | tf_op jit(solution)/shard_map/ppermute | solution.py:297
  54.0 6.0 %copy-start.12 = (f32[8,3,128]{2,1,0:T(4,128)S(1)}, f32[8,3,128]{2,1,0:T(4,128)}, u32[]{:S(2)}) copy-start(f32[8,3,128]{2,1,0:T(4,128)} %copy.18.skel_quad) | copy-start | bytes 36868
  54.1 6.0 %copy-start.13 = (f32[4,3,128]{2,1,0:T(4,128)S(1)}, f32[4,3,128]{2,1,0:T(4,128)}, u32[]{:S(2)}) copy-start(f32[4,3,128]{2,1,0:T(4,128)} %copy.19.skel_top) | copy-start | bytes 18436
  54.1 6.0 %copy-start.14 = (s32[8,8]{1,0:T(8,128)S(1)}, s32[8,8]{1,0:T(8,128)}, u32[]{:S(2)}) copy-start(s32[8,8]{1,0:T(8,128)} %far_quad.1) | copy-start | bytes 772
  54.1 5.9 %copy-start.15 = (s32[4,8]{1,0:T(4,128)S(1)}, s32[4,8]{1,0:T(4,128)}, u32[]{:S(2)}) copy-start(s32[4,8]{1,0:T(4,128)} %far_top.1) | copy-start | bytes 388
  61.8 5.0 %copy-start.8 = (f32[80,128]{1,0:T(8,128)S(1)}, f32[80,128]{1,0:T(8,128)}, u32[]{:S(2)}) copy-start(f32[80,128]{1,0:T(8,128)} %copy-done.7) | copy-start | bytes 122884
  61.8 5.0 %copy-start.9 = (s32[16,8]{1,0:T(8,128)S(1)}, s32[16,8]{1,0:T(8,128)}, u32[]{:S(2)}) copy-start(s32[16,8]{1,0:T(8,128)} %copy.20.far_pair) | copy-start | bytes 1540
  70.2 0.7 copy-start
  73.6 0.9 %slice-start = ((f32[384,128]{1,0:T(8,128)}), f32[256,128]{1,0:T(8,128)S(1)}, s32[]{:S(2)}) async-start(f32[384,128]{1,0:T(8,128)} %copy-done), calls=%async_computation | async-start | bytes 262144 | tf_op jit(solution)/shard_map/slice | solution.py:424
  74.5 1.8 %copy-start.1 = (f32[384,128]{1,0:T(8,128)S(1)}, f32[384,128]{1,0:T(8,128)}, u32[]{:S(2)}) copy-start(f32[384,128]{1,0:T(8,128)} %copy-done) | copy-start | bytes 589828
  74.5 1.8 %copy-start.3 = (f32[1,512,128]{2,1,0:T(8,128)S(1)}, f32[1,512,128]{2,1,0:T(8,128)}, u32[]{:S(2)}) copy-start(f32[1,512,128]{2,1,0:T(8,128)} %basis.3) | copy-start | bytes 786436
  74.5 1.8 %copy-start.6 = (f32[1,128,128]{2,1,0:T(8,128)S(1)}, f32[1,128,128]{2,1,0:T(8,128)}, u32[]{:S(2)}) copy-start(f32[1,128,128]{2,1,0:T(8,128)} %move.3) | copy-start | bytes 196612
  74.5 1.8 %collective-permute-start.14 = (f32[768,128]{1,0:T(8,128)S(1)}, f32[768,128]{1,0:T(8,128)S(1)}, u32[]{:S(2)}, u32[]{:S(2)}) collective-permute-start(f32[768,128]{1,0:T(8,128)S(1)} %pad_maximum_fusion), channel_id=1, source_target_pairs={{0,1},{1,0},{2,3},{3,2},{4,5},{5,4},{6,7},{7,6},{8,9},{9,8},{10,11... | collective-permute-start | bytes 1179656 | tf_op jit(solution)/shard_map/ppermute | solution.py:297

commit v2 on v1

v2 whole, which is shorter than its diff:
```python
import functools

import jax
import jax.numpy as jnp
from jax import lax
from jax.experimental import pallas as pl
from jax.experimental.pallas import tpu as pltpu
from jax.sharding import PartitionSpec as P

INV_FOUR_PI = 0.07957747154594767
DELTA_SQ = 0.01
HIGHEST = lax.Precision.HIGHEST
AXIS = "leaf"

PLANE = 8
NEAR_SLOTS = 16
FAR_SLOTS = 8

META = 0
COEF = 16
PART = 144
PACK = 272
LEAF = 512

VMEM = pl.BlockSpec(memory_space=pltpu.VMEM)
SMEM = pl.BlockSpec(memory_space=pltpu.SMEM)
HBM = pl.BlockSpec(memory_space=pl.ANY)


def call(body, outs, ins, n_smem=0, n_hbm=0, after=(), scratch=(), flops=0, nbytes=0, vmem=32):
    n, m = len(ins), len(after)

    def ordered(*refs):
        return body(*refs[:n], *refs[n + m :])

    return pl.pallas_call(
        ordered if after else body,
        out_shape=outs,
        in_specs=[SMEM] * n_smem + [VMEM] * (n - n_smem - n_hbm) + [HBM] * (n_hbm + m),
        out_specs=jax.tree.map(lambda _: VMEM, outs),
        scratch_shapes=list(scratch),
        compiler_params=pltpu.CompilerParams(vmem_limit_bytes=vmem * 1024 * 1024),
        cost_estimate=pl.CostEstimate(flops=flops, bytes_accessed=nbytes, transcendentals=0),
    )(*ins, *after)


def f32(*shape):
    return jax.ShapeDtypeStruct(shape, jnp.float32)


def dot(a, b):
    return jnp.dot(a, b, precision=HIGHEST, preferred_element_type=jnp.float32)


def dot_t(a, b):
    return lax.dot_general(
        a, b, (((0,), (0,)), ((), ())), precision=HIGHEST, preferred_element_type=jnp.float32
    )


def columns(rows):
    pad = jnp.zeros((128 - rows.shape[0], 128), jnp.float32)
    return jnp.concatenate([rows, pad], axis=0).T


def green(cols, rows):
    dx = cols[0] - rows[0]
    dy = cols[1] - rows[1]
    dz = cols[2] - rows[2]
    return lax.rsqrt((dx * dx + dy * dy) + dz * dz + DELTA_SQ)


def skeleton(skel, cluster):
    return [skel[a, pl.ds(cluster, 1), :] for a in range(3)]


def own_columns(rows):
    cols = columns(jnp.concatenate(rows, axis=0))
    return [cols[:, a : a + 1] for a in range(3)]


def meta_skeleton(ref, at):
    return [ref[at + 4 * a + 3 : at + 4 * a + 4, :] for a in range(3)]


def window_bits(entry_at, count, base):
    bits = jnp.int32(0)
    for e in range(count):
        entry = entry_at(e)
        shift = jnp.clip(entry - base, 0, 31)
        bits = bits | jnp.where(entry >= 0, jnp.left_shift(jnp.int32(1), shift), 0)
    return bits


def leaf_bits(ref, at, start, count, leaf):
    row = ref[at + 15 : at + 16, :].astype(jnp.int32)
    lane = lax.broadcasted_iota(jnp.int32, (1, 128), 1)
    valid = (lane >= start) & (lane < start + count) & (row >= 0)
    shift = jnp.clip(row - (leaf - 9), 0, 23)
    one = jnp.where(valid, jnp.left_shift(jnp.ones_like(row), shift), 0)
    return jnp.sum(one.astype(jnp.float32)).astype(jnp.int32)


def has(bits, place):
    return (jnp.right_shift(bits, jnp.clip(place, 0, 31)) & 1) == 1


def chips_of(device):
    chip = device // 2
    place = chip % 4
    odd = (chip // 4) % 2
    out = [chip, chip ^ 1, chip ^ 2, chip ^ 3, chip ^ 4, chip + jnp.where(odd == 1, 4, -4)]
    for m in (1, 2, 3):
        other = place ^ m
        out.append((chip ^ m) + jnp.where(place < other, -4, 4))
    return out


def prepare_kernel(idx, *refs):
    names = 7
    ins, (ship, keep, send), bufs, sems = refs[:names], refs[names : names + 3], refs[names + 3 : -1], refs[-1]
    copies = [pltpu.make_async_copy(a, b, sems.at[k]) for k, (a, b) in enumerate(zip(ins, bufs))]
    for c in copies:
        c.start()
    for c in copies:
        c.wait()
    vec, basis, move, pts, skel, near_list, far_list = bufs
    core = idx[0] % 2
    pieces = []
    for k in range(4):
        for a in range(3):
            pieces.append(pts[a, :, 128 * k : 128 * (k + 1)])
        if k < 3:
            pieces.append(skel[k])
    rest = jnp.zeros((1, 128 - NEAR_SLOTS - FAR_SLOTS), jnp.float32)
    lists = [near_list[...].astype(jnp.float32), far_list[...].astype(jnp.float32), rest]
    pieces.append(jnp.concatenate(lists, axis=1))
    meta = jnp.concatenate(pieces, axis=0)
    coef = dot_t(basis[0], vec[0])
    up = dot_t(move[0], coef)
    ship[0:LEAF, :] = vec[0]
    ship[LEAF : LEAF + PACK, :] = jnp.concatenate([meta, coef, up], axis=0)
    low, high = up[:64], up[64:]
    keep[...] = jnp.where(core == 0, low, high)
    send[0:64, :] = jnp.where(core == 0, high, low)
    send[64:80, :] = meta


def add_near(device, slots, blocks, metas, total, scratch):
    values, cols, high, low = scratch
    core = device % 2
    chips = chips_of(device)
    bits = []
    for s, (ref, at) in enumerate(metas):
        bits.append(leaf_bits(ref, at, 0, NEAR_SLOTS, device ^ s))
        cols[128 * s : 128 * (s + 1), :] = columns(ref[at : at + 16, :])
    for slot, (vec, pack, at) in zip(slots, blocks):
        leaf = 2 * chips[slot] + core
        v = vec[0:LEAF, :] * INV_FOUR_PI
        vh = v.astype(jnp.bfloat16)
        values[:, 0:128] = vh
        values[:, 128:256] = (v - vh.astype(jnp.float32)).astype(jnp.bfloat16)
        for s in range(2):

            @pl.when(has(bits[s], leaf - ((device ^ s) - 9)))
            def _(pack=pack, at=at, s=s):
                for i in range(4):
                    col = [
                        jnp.broadcast_to(cols[128 * s : 128 * (s + 1), 4 * i + a : 4 * i + a + 1], (128, 128))
                        for a in range(3)
                    ]
                    for k in range(4):
                        row = [pack[at + 4 * k + a : at + 4 * k + a + 1, :] for a in range(3)]
                        g = green(col, row)
                        gh = g.astype(jnp.bfloat16)
                        gl = (g - gh.astype(jnp.float32)).astype(jnp.bfloat16)
                        high[128 * i : 128 * (i + 1), 128 * k : 128 * (k + 1)] = gh
                        low[128 * i : 128 * (i + 1), 128 * k : 128 * (k + 1)] = gl
                both = jnp.dot(high[...], values[...], preferred_element_type=jnp.float32)
                rest = jnp.dot(low[...], values[:, 0:128], preferred_element_type=jnp.float32)
                total[512 * s : 512 * (s + 1), :] += both[:, 0:128] + (both[:, 128:256] + rest)


def add_far(device, slots, blocks, metas, far_pair, skel_pair, out, scratch):
    wide, values = scratch
    n = len(slots)
    core = device % 2
    chips = chips_of(device)
    chip = device // 2
    n_chips = skel_pair.shape[1]
    bits = window_bits(lambda e: far_pair[e, chip], FAR_SLOTS, chip - 4)
    cols = own_columns(skeleton(skel_pair, chip))
    for j, (slot, (_, pack, at)) in enumerate(zip(slots, blocks)):
        other = chips[slot]
        span = slice(128 * j, 128 * (j + 1))
        values[span, :] = pack[at + PART : at + PART + 128, :]
        g = green(cols, skeleton(skel_pair, jnp.clip(other, 0, n_chips - 1)))
        wide[:, span] = jnp.where(has(bits, other - chip + 4), g, 0.0)
    out[256:384, :] += dot(wide[:, 0 : 128 * n], values[0 : 128 * n, :]) * INV_FOUR_PI
    for j, (_, pack, at) in enumerate(blocks):
        values[128 * j : 128 * (j + 1), :] = pack[at + COEF : at + COEF + 128, :]
    for s, (ref, base) in enumerate(metas):
        leaf = device ^ s
        bits = leaf_bits(ref, base, NEAR_SLOTS, FAR_SLOTS, leaf)
        cols = own_columns(meta_skeleton(ref, base))
        for j, (slot, (_, pack, at)) in enumerate(zip(slots, blocks)):
            g = green(cols, meta_skeleton(pack, at))
            ok = has(bits, 2 * chips[slot] + core - (leaf - 9))
            wide[:, 128 * j : 128 * (j + 1)] = jnp.where(ok, g, 0.0)
        out[128 * s : 128 * (s + 1), :] += dot(wide[:, 0 : 128 * n], values[0 : 128 * n, :]) * INV_FOUR_PI


def near_kernel(slots, idx, got, own, *refs):
    n = len(slots)
    if slots == (0,):
        blocks = [(own, own, LEAF)]
        total, *scratch = refs
        total[...] = jnp.zeros_like(total)
    else:
        blocks = [(b, b, LEAF) for b in refs[:n]]
        total_in, total, *scratch = refs[n:]
        total[...] = total_in[...]
    add_near(idx[0], slots, blocks, ((own, LEAF), (got, 64)), total, scratch)


def way_kernel(idx, bx, by, out):
    out[...] = jnp.where(idx[0] % 2 == 0, bx[...], by[...])


def middle_kernel(idx, far_pair, got, own, skel_pair, total_in, bx, by, bd, be, bo, cx, cy, total, low, *scratch):
    total[...] = total_in[...]
    low[...] = jnp.zeros_like(low)
    device = idx[0]
    metas = ((own, LEAF), (got, 64))
    blocks = [(b, b, LEAF) for b in (own, bx, by, bd, be, bo, cx, cy)]
    add_far(device, range(8), blocks, metas, far_pair, skel_pair, low, scratch[4:])
    slots = (3, 6, 7)
    add_near(device, slots, [blocks[j] for j in slots], metas, total, scratch[:4])


def tail_kernel(slots, idx, far_pair, got, own, skel_pair, total_in, low_in, ctx, local_quad, *refs):
    n = len(slots)
    wholes = refs[:n]
    keep, share, *scratch = refs[n:]
    total, low = scratch[6:]
    total[...] = total_in[...]
    low[...] = low_in[...]
    device = idx[0]
    metas = ((own, LEAF), (got, 64))
    blocks = [(b, b, LEAF) for b in wholes]
    add_far(device, slots, blocks, metas, far_pair, skel_pair, low, scratch[4:6])
    low[256:384, :] += dot(ctx[128:256, :], local_quad[...])
    keep[512:640, :] = low[0:128, :]
    keep[640:768, :] = low[256:384, :]
    share[512:768, :] = low[128:384, :]
    add_near(device, slots, blocks, metas, total, scratch[:4])
    keep[0:512, :] = total[0:512, :]
    share[0:512, :] = total[512:1024, :]


def rise_kernel(keep, got, epair, equad, out):
    out[0:128, :] = dot_t(epair[...], keep[...] + got[0:64, :])
    out[128:160, :] = equad[...]


def quad_kernel(own, bx, epair, out):
    out[0:128, :] = own[0:128, :] + bx[0:128, :]
    out[128:160, :] = own[128:160, :]
    out[160:192, :] = bx[128:160, :]
    out[192:256, :] = epair[...]


def top_kernel(idx, mine, theirs, send, ctx, quad, top):
    device = idx[0]
    core = device % 2
    half = pl.multiple_of(core * 64, 64)
    for j in range(2):
        member = 2 * (((device // 2) ^ j) % 2)
        mine_at = pl.multiple_of((member + core) * 32, 32)
        sib_at = pl.multiple_of((member + 1 - core) * 32, 32)
        ctx[pl.ds(mine_at, 32), :] = mine[128 + 32 * j : 160 + 32 * j, :]
        ctx[pl.ds(sib_at, 32), :] = theirs[128 + 32 * j : 160 + 32 * j, :]
    ctx[pl.ds(128 + half, 64), :] = mine[192:256, :]
    ctx[pl.ds(192 - half, 64), :] = theirs[192:256, :]
    quad[...] = mine[0:128, :] + theirs[0:128, :]
    top[...] = dot_t(ctx[0:128, :], quad[...])
    send[0:64, :] = quad[pl.ds(half, 64), :]
    send[64:128, :] = top[pl.ds(half, 64), :]


def join_kernel(mine, theirs, out):
    out[0:64, :] = mine[0:64, :]
    out[64:128, :] = theirs[0:64, :]
    out[128:192, :] = mine[64:128, :] + theirs[64:128, :]


def upper_kernel(idx, far_quad, far_top, ctx, up, r1, r2, r3, skel_quad, skel_top, out, wide, values):
    device = idx[0]
    half = pl.multiple_of((device % 2) * 64, 64)
    plane = device // 8
    quad = device // 4
    received = (r1, r2, r3)
    values[...] = jnp.zeros_like(values)
    bits = window_bits(lambda e: far_top[plane, e], FAR_SLOTS, 0)
    cols = own_columns(skeleton(skel_top, plane))
    for j, r in enumerate(received):
        other = plane ^ (j + 1)
        values[pl.ds(128 * j + half, 64), :] = r[128:192, :]
        g = green(cols, skeleton(skel_top, other))
        wide[:, 128 * j : 128 * (j + 1)] = jnp.where(has(bits, other), g, 0.0)
    local_top = dot(wide[:, 0:384], values[0:384, :]) * INV_FOUR_PI
    bits = window_bits(lambda e: far_quad[quad, e], FAR_SLOTS, quad - 4)
    cols = own_columns(skeleton(skel_quad, quad))
    others = [quad ^ 1] + [(quad ^ (2 * (j + 1))) ^ k for j in range(3) for k in range(2)]
    sources = [up[64:128, :]] + [r[64 * k : 64 * (k + 1), :] for r in received for k in range(2)]
    for j, (other, source) in enumerate(zip(others, sources)):
        values[pl.ds(128 * j + half, 64), :] = source
        g = green(cols, skeleton(skel_quad, other))
        ok = has(bits, other - quad + 4) & (other >= quad - 4) & (other <= quad + 4)
        wide[:, 128 * j : 128 * (j + 1)] = jnp.where(ok, g, 0.0)
    out[...] = dot(wide[...], values[...]) * INV_FOUR_PI + dot(ctx[0:128, :], local_top)


def final_kernel(keep, got, move, basis, out):
    local_pair = keep[640:768, :] + got[640:768, :]
    local = keep[512:640, :] + got[512:640, :] + dot(move[0], local_pair)
    out[0] = keep[0:512, :] + got[0:512, :] + dot(basis[0], local)


def near_scratch():
    return [
        pltpu.VMEM((512, 256), jnp.bfloat16),
        pltpu.VMEM((256, 128), jnp.float32),
        pltpu.VMEM((512, 512), jnp.bfloat16),
        pltpu.VMEM((512, 512), jnp.bfloat16),
    ]


def far_scratch(n):
    return [pltpu.VMEM((128, 128 * n), jnp.float32), pltpu.VMEM((128 * n, 128), jnp.float32)]


NEAR_FLOPS = 2 * 6 * 512 * 512 * 128


def permute(value, target):
    n = lax.axis_size(AXIS)
    pairs = [(i, target(i)) for i in range(n)]
    return lax.ppermute(value, AXIS, [(i, j) for i, j in pairs if 0 <= j < n and i != j])


def swap(value, mask):
    return permute(value, lambda i: i ^ mask)


def listed_sum(own, entries, skels, coefs):
    def advance(running, partner):
        at = jnp.maximum(partner, 0)
        rows = skels[at]
        g = green([own[a][:, None] for a in range(3)], [rows[a][None, :] for a in range(3)]) * INV_FOUR_PI
        contrib = jnp.dot(g, coefs[at], precision=HIGHEST)
        return running + jnp.where(partner >= 0, contrib, 0.0), None

    return lax.scan(advance, jnp.zeros(coefs.shape[1:], jnp.float32), entries)[0]


def upper_anywhere(device, send, ctx, far_quad, far_top, skel_quad, skel_top):
    n = lax.axis_size(AXIS)
    first = jnp.where(device // 4 % 2 == 0, send[0:64], send[64:128])
    second = jnp.where(device // 4 % 2 == 0, send[64:128], send[0:64])
    send = jnp.concatenate([first, second, send[128:192]], axis=0)
    rows = send.shape[0] // 4
    part = lax.dynamic_slice_in_dim(send, (device // 2 % 4) * rows, rows, 0)
    every = lax.all_gather(part, AXIS, axis=0, tiled=True)
    every = every.reshape(n // PLANE, 4, 2, rows, 128).transpose(0, 2, 1, 3, 4)
    every = every.reshape(n // PLANE, 2, 3, 64, 128).transpose(0, 2, 1, 3, 4)
    every = every.reshape(n // PLANE, 3, 128, 128)
    plane, quad = device // 8, device // 4
    local_top = listed_sum(skel_top[plane], far_top[plane], skel_top, every[:, 2])
    quads = every[:, :2].reshape(n // 4, 128, 128)
    far = listed_sum(skel_quad[quad], far_quad[quad], skel_quad, quads)
    whole = far + jnp.dot(ctx[0:128], local_top, precision=HIGHEST)
    return jnp.where(device % 2 == 0, whole, 0.0)


def per_device(
    vectors,
    points,
    leaf_basis,
    transfer_leaf,
    transfer_pair,
    transfer_quad,
    skel_leaf,
    skel_pair,
    skel_quad,
    skel_top,
    near_list,
    far_leaf,
    far_pair,
    far_quad,
    far_top,
):
    n = lax.axis_size(AXIS)
    device = lax.axis_index(AXIS)
    idx = device.reshape(1).astype(jnp.int32)
    def before(i):
        return i + 8 if i // 8 % 2 == 1 else i - 8

    ins = [vectors, leaf_basis, transfer_leaf]
    ins += [points.transpose(1, 0, 2), skel_leaf.transpose(1, 0, 2)]
    ins += [near_list, far_leaf]
    ship, keep, send = call(
        prepare_kernel,
        (f32(LEAF + PACK, 128), f32(64, 128), f32(80, 128)),
        [idx, *ins],
        n_smem=1,
        n_hbm=len(ins),
        scratch=[pltpu.VMEM(a.shape, a.dtype) for a in ins] + [pltpu.SemaphoreType.DMA((len(ins),))],
        flops=2 * 6 * 640 * 128 * 128,
        nbytes=1 << 20,
        vmem=60,
    )
    got = swap(send, 1)
    def near(slots, blocks, total, after):
        return call(
            functools.partial(near_kernel, slots),
            f32(1024, 128),
            [idx, got, ship] + blocks + ([total] if blocks else []),
            n_smem=1,
            after=after,
            scratch=near_scratch(),
            flops=2 * len(slots) * NEAR_FLOPS,
        )

    bx, by, be = [swap(ship, m) for m in (2, 4, 8)]
    bo = permute(ship, before)
    rise = call(rise_kernel, f32(160, 128), [keep, got, transfer_pair, transfer_quad], flops=2 * 6 * 64 * 128 * 128)
    rise_x = swap(rise, 2)
    total = near((0,), [], None, [rise])
    way = call(way_kernel, f32(LEAF + PACK, 128), [idx, bx, by], n_smem=1, after=[total])
    bd = permute(way, lambda i: i ^ 4 if i % 2 == 0 else i ^ 2)

    plane_odd = device // 8 % 2 == 1
    place = device // 2 % 4
    picks = [((place ^ m) < place) == plane_odd for m in (1, 2)]
    cx, cy = [
        swap(jnp.where(pick, be, bo), 2 * m) for m, pick in zip((1, 2), picks)
    ]
    cd = permute(bd, lambda i: i + 8 if i // 2 % 4 < 2 else i - 8)

    half = call(quad_kernel, f32(256, 128), [rise, rise_x, transfer_pair], after=[total])
    half_got = swap(half, 1)
    shared, ctx = call(
        top_kernel,
        (f32(128, 128), f32(256, 128)),
        [idx, half, half_got],
        n_smem=1,
        after=[way],
        scratch=[pltpu.VMEM((128, 128), jnp.float32), pltpu.VMEM((128, 128), jnp.float32)],
        flops=2 * 6 * 128**3,
    )
    total = near((1, 2, 4, 5), [bx, by, be, bo], total, [shared])
    up = call(join_kernel, f32(192, 128), [shared, swap(shared, 4)], after=[total])
    far_pair_t, skel_pair_t = far_pair.T, skel_pair.transpose(1, 0, 2)
    total, low = call(
        middle_kernel,
        (f32(1024, 128), f32(384, 128)),
        [idx, far_pair_t, got, ship, skel_pair_t, total, bx, by, bd, be, bo, cx, cy],
        n_smem=2,
        after=[up],
        scratch=near_scratch() + far_scratch(8),
        flops=6 * NEAR_FLOPS,
    )
    if n == 4 * PLANE:
        received = [swap(up, PLANE * m) for m in (3, 2, 1)]
        skels = [skel_quad.transpose(1, 0, 2), skel_top.transpose(1, 0, 2)]
        local_quad = call(
            upper_kernel,
            f32(128, 128),
            [idx, far_quad, far_top, ctx, up, *received[::-1], *skels],
            n_smem=3,
            after=[low],
            scratch=far_scratch(7),
            flops=2 * 6 * 11 * 128**3,
        )
    else:
        local_quad = upper_anywhere(device, up, ctx, far_quad, far_top, skel_quad, skel_top)

    keep, share = call(
        functools.partial(tail_kernel, (8,)),
        (f32(768, 128), f32(768, 128)),
        [idx, far_pair_t, got, ship, skel_pair_t, total, low, ctx, local_quad, cd],
        n_smem=2,
        scratch=near_scratch()
        + far_scratch(1)
        + [pltpu.VMEM((1024, 128), jnp.float32), pltpu.VMEM((384, 128), jnp.float32)],
        flops=2 * NEAR_FLOPS,
    )
    return call(
        final_kernel,
        f32(1, 512, 128),
        [keep, swap(share, 1), transfer_leaf, leaf_basis],
        flops=2 * 6 * 640 * 128 * 128,
    )


def solution(mesh):
    placed = (
        P("leaf", None, None),
        P("leaf", None, None),
        P("leaf", None, None),
        P("leaf", None, None),
        P("leaf", None),
        P("leaf", None),
        P("leaf", None, None),
        P(),
        P(),
        P(),
        P("leaf", None),
        P("leaf", None),
        P(),
        P(),
        P(),
    )
    return jax.shard_map(
        per_device, mesh=mesh, in_specs=placed, out_specs=P("leaf", None, None), check_vma=False
    )
```

time: 77.7 us -> 56.9 us (0.73)
  the two profiles are of different devices: /device:TPU:9 before, /device:TPU:15 now
where the time goes in v2:
time: 56.9 us; the launch traced here: 58 us
  Pallas kernels  24.5 us (43%)
  starting transfers between devices  22.1 us (39%)
  waiting for transfers between devices  9.17 us (16%)
  local copies, waits for them, and re-layouts  1.82 us (3%)
    pallas_call x12, Pallas kernels, call(): pl.pallas_call(ordered if after else body, out_shape=outs, in_specs=[SMEM...  24.5 us
    ppermute x16, starting transfers between devices, permute(): lax.ppermute(value, AXIS, [(i, j) for i, j in pairs if 0 <= j < n and i !...  22.1 us
    ppermute x16, waiting for transfers between devices, permute(): lax.ppermute(value, AXIS, [(i, j) for i, j in pairs if 0 <= j < n and i !...  9.17 us
    unnamed x26, local copies, waits for them, and re-layouts  1.82 us
  transfers between devices with their start and end apart: 16, of which 4 were waited for; matrix products, arithmetic and copies ran while one was open for 0% of the time, Pallas kernels for 30%

profile of v2, /device:TPU:15, one launch (start us, length us, event | category | flops | bytes accessed | tf_op | source)
XLA Modules:
  0.0 58.0 jit_solution(11328596560000628828)
XLA Ops:
  0.0 2.6 %shard_map.145 = (f32[784,128]{1,0:T(8,128)}, f32[64,128]{1,0:T(8,128)}, f32[80,128]{1,0:T(8,128)}) custom-call(s32[1]{0:T(128)} %bitcast.idx.refs_0_, f32[1,512,128]{2,1,0:T(8,128)} %refs_0_.1, f32[1,512,128]{2,1,0:T(8,128)} %basis.1, f32[1,128,128]{2,1,0:T(8,128)} %move.1, f32[3,1,512]{2,1,0:T(1,128)} %bitcast.13, f32[3,1,128]{2,1,0:T(1,128)} %bitcast.14, ...), custom_call_target="tpu_custom_call" | custom-call | flops 125829120 | bytes 1048576 | tf_op jit(solution)/shard_map/pallas_call | solution.py:36
  2.6 0.3 collective-permute-start.1
  2.9 0.2 collective-permute-start.2
  3.1 0.0 collective-permute-start.3
  3.1 4.5 %collective-permute-start.4 = (f32[784,128]{1,0:T(8,128)}, f32[784,128]{1,0:T(8,128)S(1)}, u32[]{:S(2)}, u32[]{:S(2)}) collective-permute-start(f32[784,128]{1,0:T(8,128)} %get-tuple-element.15.refs_2_.refs_3_.own), channel_id=1, source_target_pairs={{8,16},{9,17},{10,18},{11,19},{12,20},{13,21},{14,22},{15,23},{16,... | collective-permute-start | bytes 1204232 | tf_op jit(solution)/shard_map/ppermute | solution.py:349
  7.6 1.9 %collective-permute-start = (f32[80,128]{1,0:T(8,128)}, f32[80,128]{1,0:T(8,128)S(1)}, u32[]{:S(2)}, u32[]{:S(2)}) collective-permute-start(f32[80,128]{1,0:T(8,128)} %get-tuple-element.14), channel_id=1, source_target_pairs={{0,1},{1,0},{2,3},{3,2},{4,5},{5,4},{6,7},{7,6},{8,9},{9,8},{10,11... | collective-permute-start | bytes 122888 | tf_op jit(solution)/shard_map/ppermute | solution.py:349
  9.5 1.1 %collective-permute-done.got.refs_1_.refs_2_ = f32[80,128]{1,0:T(8,128)S(1)} collective-permute-done((f32[80,128]{1,0:T(8,128)}, f32[80,128]{1,0:T(8,128)S(1)}, u32[]{:S(2)}, u32[]{:S(2)}) %collective-permute-start) | collective-permute-done | bytes 40992 | tf_op jit(solution)/shard_map/ppermute | solution.py:349
  10.6 0.0 copy-done.2
  10.6 0.0 copy-done.4
  10.6 0.8 %copy-done.3 = f32[64,128]{1,0:T(8,128)S(1)} copy-done((f32[64,128]{1,0:T(8,128)S(1)}, f32[64,128]{1,0:T(8,128)}, u32[]{:S(2)}) %copy-start.3) | copy-done | bytes 32792
  11.3 0.3 shard_map.146.refs_3_.refs_0_
  11.6 1.3 %collective-permute-start.5 = (f32[160,128]{1,0:T(8,128)S(1)}, f32[160,128]{1,0:T(8,128)S(1)}, u32[]{:S(2)}, u32[]{:S(2)}) collective-permute-start(f32[160,128]{1,0:T(8,128)S(1)} %shard_map.146.refs_3_.refs_0_), channel_id=1, source_target_pairs={{0,2},{1,3},{2,0},{3,1},{4,6},{5,7},{6,4},{7,5},{8,10},{9,11},{10,... | collective-permute-start | bytes 245768 | tf_op jit(solution)/shard_map/ppermute | solution.py:349
  12.9 1.0 %copy-done.5 = f32[784,128]{1,0:T(8,128)S(1)} copy-done((f32[784,128]{1,0:T(8,128)S(1)}, f32[784,128]{1,0:T(8,128)}, u32[]{:S(2)}) %copy-start.5) | copy-done | bytes 401432
  13.9 2.1 %shard_map.147.refs_3_.refs_7_ = f32[1024,128]{1,0:T(8,128)S(1)} custom-call(s32[1]{0:T(128)} %bitcast.idx.refs_0_, f32[80,128]{1,0:T(8,128)S(1)} %collective-permute-done.got.refs_1_.refs_2_, f32[784,128]{1,0:T(8,128)S(1)} %copy-done.5, f32[160,128]{1,0:T(8,128)S(1)} %shard_map.146.refs_3_.refs_0_), custom_call_target="tpu_custom_call" | custom-call | flops 805306368 | tf_op jit(solution)/shard_map/pallas_call | solution.py:36
  16.0 0.0 collective-permute-done.1.refs_1_.refs_3_.refs_6_
  16.0 0.0 collective-permute-done.2.refs_2_.refs_4_.refs_7_
  16.0 0.1 shard_map.149.refs_3_
  16.0 0.3 collective-permute-start.7
  16.3 0.0 collective-permute-done.5.refs_1_
  16.4 1.0 %collective-permute-start.6 = (f32[256,128]{1,0:T(8,128)S(1)}, f32[256,128]{1,0:T(8,128)S(1)}, u32[]{:S(2)}, u32[]{:S(2)}) collective-permute-start(f32[256,128]{1,0:T(8,128)S(1)} %shard_map.148.refs_1_), channel_id=1, source_target_pairs={{0,1},{1,0},{2,3},{3,2},{4,5},{5,4},{6,7},{7,6},{8,9},{9,8},{10,11... | collective-permute-start | bytes 393224 | tf_op jit(solution)/shard_map/ppermute | solution.py:349
  17.4 0.0 collective-permute-done.3.refs_5_.refs_9_
  17.4 0.0 collective-permute-done.4.refs_6_.refs_10_
  17.4 0.1 broadcast_select_fusion
  17.5 0.0 copy-start.6
  17.5 0.5 collective-permute-start.8
  17.9 1.2 %collective-permute-start.9 = (f32[784,128]{1,0:T(8,128)S(1)}, f32[784,128]{1,0:T(8,128)S(1)}, u32[]{:S(2)}, u32[]{:S(2)}) collective-permute-start(f32[784,128]{1,0:T(8,128)S(1)} %get-tuple-element.23), channel_id=1, source_target_pairs={{0,4},{1,5},{2,6},{3,7},{4,0},{5,1},{6,2},{7,3},{8,12},{9,13},{10,... | collective-permute-start | bytes 1204232 | tf_op jit(solution)/shard_map/ppermute | solution.py:349
  19.2 0.0 collective-permute-done.6.refs_2_
  19.2 0.3 shard_map.150
  19.5 0.4 collective-permute-start.10
  19.9 4.9 %collective-permute-done.7.refs_8_ = f32[784,128]{1,0:T(8,128)S(1)} collective-permute-done((f32[784,128]{1,0:T(8,128)S(1)}, f32[784,128]{1,0:T(8,128)S(1)}, u32[]{:S(2)}, u32[]{:S(2)}) %collective-permute-start.7) | collective-permute-done | bytes 401440 | tf_op jit(solution)/shard_map/ppermute | solution.py:349
  24.8 1.9 %collective-permute-start.14 = (f32[784,128]{1,0:T(8,128)S(1)}, f32[784,128]{1,0:T(8,128)S(1)}, u32[]{:S(2)}, u32[]{:S(2)}) collective-permute-start(f32[784,128]{1,0:T(8,128)S(1)} %collective-permute-done.7.refs_8_), channel_id=1, source_target_pairs={{0,8},{1,9},{2,10},{3,11},{8,16},{9,17},{10,18},{11,19},{12,4},{13... | collective-permute-start | bytes 1204232 | tf_op jit(solution)/shard_map/ppermute | solution.py:349
  26.7 0.0 copy-done.6
  26.7 5.3 %shard_map.151.refs_2_.refs_5_ = f32[1024,128]{1,0:T(8,128)S(1)} custom-call(s32[1]{0:T(128)} %bitcast.idx.refs_0_, f32[80,128]{1,0:T(8,128)S(1)} %collective-permute-done.got.refs_1_.refs_2_, f32[784,128]{1,0:T(8,128)S(1)} %copy-done.6, f32[784,128]{1,0:T(8,128)S(1)} %collective-permute-done.1.refs_1_.refs_3_.refs_6_, ...), custom_call_target="tpu_custom_call" | custom-call | flops 3221225472 | tf_op jit(solution)/shard_map/pallas_call | solution.py:36
  32.0 0.0 copy-start.7
  32.0 0.0 copy-start.11
  32.0 0.0 collective-permute-done.10.refs_1_
  32.0 0.1 collective-permute-start.11
  32.1 1.7 %collective-permute-start.12 = (f32[192,128]{1,0:T(8,128)S(1)}, f32[192,128]{1,0:T(8,128)S(1)}, u32[]{:S(2)}, u32[]{:S(2)}) collective-permute-start(f32[192,128]{1,0:T(8,128)S(1)} %shard_map.152.refs_13_.refs_4_), channel_id=1, source_target_pairs={{0,16},{1,17},{2,18},{3,19},{4,20},{5,21},{6,22},{7,23},{8,24},{9,... | collective-permute-start | bytes 294920 | tf_op jit(solution)/shard_map/ppermute | solution.py:349
  33.8 0.0 collective-permute-done.8.refs_11_
  33.8 0.9 %collective-permute-start.13 = (f32[192,128]{1,0:T(8,128)S(1)}, f32[192,128]{1,0:T(8,128)S(1)}, u32[]{:S(2)}, u32[]{:S(2)}) collective-permute-start(f32[192,128]{1,0:T(8,128)S(1)} %shard_map.152.refs_13_.refs_4_), channel_id=1, source_target_pairs={{0,24},{1,25},{2,26},{3,27},{4,28},{5,29},{6,30},{7,31},{8,16},{9,... | collective-permute-start | bytes 294920 | tf_op jit(solution)/shard_map/ppermute | solution.py:349
  34.8 0.0 collective-permute-done.9.refs_12_
  34.8 0.0 copy-done.7
  34.8 0.0 copy-done.11
  34.8 0.0 copy-start.8
  34.8 0.0 copy-start.10
  34.8 0.0 copy-start.12
  34.8 7.6 %shard_map.153 = (f32[1024,128]{1,0:T(8,128)S(1)}, f32[384,128]{1,0:T(8,128)S(1)}) custom-call(s32[1]{0:T(128)} %bitcast.idx.refs_0_, s32[8,16]{1,0:T(8,128)S(1)} %bitcast.11, f32[80,128]{1,0:T(8,128)S(1)} %collective-permute-done.got.refs_1_.refs_2_, f32[784,128]{1,0:T(8,128)S(1)} %copy-done.6, f32[3,16,128]{2,1,0:T(8,128)S(1)} %bitcast.7, ...), custom_call_target="tpu_custom_call" | custom-call | flops 2415919104 | tf_op jit(solution)/shard_map/pallas_call | solution.py:36
  42.4 0.0 copy-start.9
  42.4 0.0 collective-permute-done.11.refs_5_
  42.4 0.0 collective-permute-done.12.refs_6_
  42.4 1.8 %collective-permute-done.13.refs_7_ = f32[192,128]{1,0:T(8,128)S(1)} collective-permute-done((f32[192,128]{1,0:T(8,128)S(1)}, f32[192,128]{1,0:T(8,128)S(1)}, u32[]{:S(2)}, u32[]{:S(2)}) %collective-permute-start.13) | collective-permute-done | bytes 98336 | tf_op jit(solution)/shard_map/ppermute | solution.py:349
  44.2 0.0 copy-done.8
  44.2 0.0 copy-done.10
  44.2 0.0 copy-done.12
  44.2 0.0 copy-done.9
  44.3 1.8 %shard_map.154.local_quad = f32[128,128]{1,0:T(8,128)S(1)} custom-call(s32[1]{0:T(128)} %bitcast.idx.refs_0_, s32[8,8]{1,0:T(8,128)S(1)} %copy-done.10, s32[4,8]{1,0:T(4,128)S(1)} %copy-done.12, f32[256,128]{1,0:T(8,128)S(1)} %get-tuple-element.20.refs_3_.ctx, f32[192,128]{1,0:T(8,128)S(1)} %shard_map.152.refs_13_.refs_4_, ...), custom_call_target="tpu_custom_call" | custom-call | flops 276824064 | tf_op jit(solution)/shard_map/pallas_call | solution.py:36
  46.0 0.0 collective-permute-done.14.refs_0_
  46.0 0.0 copy-start
  46.1 0.0 copy-start.1
  46.1 3.3 %shard_map.155 = (f32[768,128]{1,0:T(8,128)S(1)}, f32[768,128]{1,0:T(8,128)S(1)}) custom-call(s32[1]{0:T(128)} %bitcast.idx.refs_0_, s32[8,16]{1,0:T(8,128)S(1)} %bitcast.12, f32[80,128]{1,0:T(8,128)S(1)} %collective-permute-done.got.refs_1_.refs_2_, f32[784,128]{1,0:T(8,128)S(1)} %copy-done.6, f32[3,16,128]{2,1,0:T(8,128)S(1)} %bitcast.8, ...), custom_call_target="tpu_custom_call" | custom-call | flops 805306368 | tf_op jit(solution)/shard_map/pallas_call | solution.py:36
  49.4 5.9 %collective-permute-start.15 = (f32[768,128]{1,0:T(8,128)S(1)}, f32[768,128]{1,0:T(8,128)S(1)}, u32[]{:S(2)}, u32[]{:S(2)}) collective-permute-start(f32[768,128]{1,0:T(8,128)S(1)} %get-tuple-element.22), channel_id=1, source_target_pairs={{0,1},{1,0},{2,3},{3,2},{4,5},{5,4},{6,7},{7,6},{8,9},{9,8},{10,11... | collective-permute-start | bytes 1179656 | tf_op jit(solution)/shard_map/ppermute | solution.py:349
  55.3 1.3 %collective-permute-done.15.got = f32[768,128]{1,0:T(8,128)S(1)} collective-permute-done((f32[768,128]{1,0:T(8,128)S(1)}, f32[768,128]{1,0:T(8,128)S(1)}, u32[]{:S(2)}, u32[]{:S(2)}) %collective-permute-start.15) | collective-permute-done | bytes 393248 | tf_op jit(solution)/shard_map/ppermute | solution.py:349
  56.6 0.0 copy-done.1
  56.6 1.3 %shard_map.156 = f32[1,512,128]{2,1,0:T(8,128)} custom-call(f32[768,128]{1,0:T(8,128)S(1)} %get-tuple-element.21.keep, f32[768,128]{1,0:T(8,128)S(1)} %collective-permute-done.15.got, f32[1,128,128]{2,1,0:T(8,128)S(1)} %copy-done.1, f32[1,512,128]{2,1,0:T(8,128)S(1)} %copy-done), custom_call_target="tpu_custom_call" | custom-call | flops 125829120 | tf_op jit(solution)/shard_map/pallas_call | solution.py:36
  (7 shorter events, 0.0 us)
Async XLA Ops:
  0.0 10.6 %copy-start.2 = (f32[64,128]{1,0:T(8,128)S(1)}, f32[64,128]{1,0:T(8,128)}, u32[]{:S(2)}) copy-start(f32[64,128]{1,0:T(8,128)} %refs_2_.4) | copy-start | bytes 98308
  0.0 10.6 %copy-start.4 = (f32[32,128]{1,0:T(8,128)S(1)}, f32[32,128]{1,0:T(8,128)}, u32[]{:S(2)}) copy-start(f32[32,128]{1,0:T(8,128)} %equad.1) | copy-start | bytes 49156
  2.6 13.4 %collective-permute-start.1 = (f32[784,128]{1,0:T(8,128)}, f32[784,128]{1,0:T(8,128)S(1)}, u32[]{:S(2)}, u32[]{:S(2)}) collective-permute-start(f32[784,128]{1,0:T(8,128)} %get-tuple-element.15.refs_2_.refs_3_.own), channel_id=1, source_target_pairs={{0,2},{1,3},{2,0},{3,1},{4,6},{5,7},{6,4},{7,5},{8,10},{9,11},{10,... | collective-permute-start | bytes 1204232 | tf_op jit(solution)/shard_map/ppermute | solution.py:349
  2.9 13.1 %collective-permute-start.2 = (f32[784,128]{1,0:T(8,128)}, f32[784,128]{1,0:T(8,128)S(1)}, u32[]{:S(2)}, u32[]{:S(2)}) collective-permute-start(f32[784,128]{1,0:T(8,128)} %get-tuple-element.15.refs_2_.refs_3_.own), channel_id=1, source_target_pairs={{0,4},{1,5},{2,6},{3,7},{4,0},{5,1},{6,2},{7,3},{8,12},{9,13},{10,... | collective-permute-start | bytes 1204232 | tf_op jit(solution)/shard_map/ppermute | solution.py:349
  3.1 14.3 %collective-permute-start.3 = (f32[784,128]{1,0:T(8,128)}, f32[784,128]{1,0:T(8,128)S(1)}, u32[]{:S(2)}, u32[]{:S(2)}) collective-permute-start(f32[784,128]{1,0:T(8,128)} %get-tuple-element.15.refs_2_.refs_3_.own), channel_id=1, source_target_pairs={{0,8},{1,9},{2,10},{3,11},{4,12},{5,13},{6,14},{7,15},{8,0},{9,1},... | collective-permute-start | bytes 1204232 | tf_op jit(solution)/shard_map/ppermute | solution.py:349
  3.1 14.3 %collective-permute-start.4 = (f32[784,128]{1,0:T(8,128)}, f32[784,128]{1,0:T(8,128)S(1)}, u32[]{:S(2)}, u32[]{:S(2)}) collective-permute-start(f32[784,128]{1,0:T(8,128)} %get-tuple-element.15.refs_2_.refs_3_.own), channel_id=1, source_target_pairs={{8,16},{9,17},{10,18},{11,19},{12,20},{13,21},{14,22},{15,23},{16,... | collective-permute-start | bytes 1204232 | tf_op jit(solution)/shard_map/ppermute | solution.py:349
  7.6 2.9 %collective-permute-start = (f32[80,128]{1,0:T(8,128)}, f32[80,128]{1,0:T(8,128)S(1)}, u32[]{:S(2)}, u32[]{:S(2)}) collective-permute-start(f32[80,128]{1,0:T(8,128)} %get-tuple-element.14), channel_id=1, source_target_pairs={{0,1},{1,0},{2,3},{3,2},{4,5},{5,4},{6,7},{7,6},{8,9},{9,8},{10,11... | collective-permute-start | bytes 122888 | tf_op jit(solution)/shard_map/ppermute | solution.py:349
  10.6 0.8 %copy-start.3 = (f32[64,128]{1,0:T(8,128)S(1)}, f32[64,128]{1,0:T(8,128)}, u32[]{:S(2)}) copy-start(f32[64,128]{1,0:T(8,128)} %get-tuple-element.16.keep) | copy-start | bytes 98308
  11.6 4.8 %collective-permute-start.5 = (f32[160,128]{1,0:T(8,128)S(1)}, f32[160,128]{1,0:T(8,128)S(1)}, u32[]{:S(2)}, u32[]{:S(2)}) collective-permute-start(f32[160,128]{1,0:T(8,128)S(1)} %shard_map.146.refs_3_.refs_0_), channel_id=1, source_target_pairs={{0,2},{1,3},{2,0},{3,1},{4,6},{5,7},{6,4},{7,5},{8,10},{9,11},{10,... | collective-permute-start | bytes 245768 | tf_op jit(solution)/shard_map/ppermute | solution.py:349
  12.9 1.0 %copy-start.5 = (f32[784,128]{1,0:T(8,128)S(1)}, f32[784,128]{1,0:T(8,128)}, u32[]{:S(2)}) copy-start(f32[784,128]{1,0:T(8,128)} %get-tuple-element.15.refs_2_.refs_3_.own) | copy-start | bytes 1204228
  16.0 8.8 %collective-permute-start.7 = (f32[784,128]{1,0:T(8,128)S(1)}, f32[784,128]{1,0:T(8,128)S(1)}, u32[]{:S(2)}, u32[]{:S(2)}) collective-permute-start(f32[784,128]{1,0:T(8,128)S(1)} %shard_map.149.refs_3_), channel_id=1, source_target_pairs={{0,4},{1,3},{2,6},{3,1},{4,0},{5,7},{6,2},{7,5},{8,12},{9,11},{10,... | collective-permute-start | bytes 1204232 | tf_op jit(solution)/shard_map/ppermute | solution.py:349
  16.4 2.8 %collective-permute-start.6 = (f32[256,128]{1,0:T(8,128)S(1)}, f32[256,128]{1,0:T(8,128)S(1)}, u32[]{:S(2)}, u32[]{:S(2)}) collective-permute-start(f32[256,128]{1,0:T(8,128)S(1)} %shard_map.148.refs_1_), channel_id=1, source_target_pairs={{0,1},{1,0},{2,3},{3,2},{4,5},{5,4},{6,7},{7,6},{8,9},{9,8},{10,11... | collective-permute-start | bytes 393224 | tf_op jit(solution)/shard_map/ppermute | solution.py:349
  17.5 9.2 %copy-start.6 = (f32[784,128]{1,0:T(8,128)S(1)}, f32[784,128]{1,0:T(8,128)}, u32[]{:S(2)}) copy-start(f32[784,128]{1,0:T(8,128)} %get-tuple-element.15.refs_2_.refs_3_.own) | copy-start | bytes 1204228
  17.5 16.3 %collective-permute-start.8 = (f32[784,128]{1,0:T(8,128)S(1)}, f32[784,128]{1,0:T(8,128)S(1)}, u32[]{:S(2)}, u32[]{:S(2)}) collective-permute-start(f32[784,128]{1,0:T(8,128)S(1)} %get-tuple-element.24), channel_id=1, source_target_pairs={{0,2},{1,3},{2,0},{3,1},{4,6},{5,7},{6,4},{7,5},{8,10},{9,11},{10,... | collective-permute-start | bytes 1204232 | tf_op jit(solution)/shard_map/ppermute | solution.py:349
  17.9 16.8 %collective-permute-start.9 = (f32[784,128]{1,0:T(8,128)S(1)}, f32[784,128]{1,0:T(8,128)S(1)}, u32[]{:S(2)}, u32[]{:S(2)}) collective-permute-start(f32[784,128]{1,0:T(8,128)S(1)} %get-tuple-element.23), channel_id=1, source_target_pairs={{0,4},{1,5},{2,6},{3,7},{4,0},{5,1},{6,2},{7,3},{8,12},{9,13},{10,... | collective-permute-start | bytes 1204232 | tf_op jit(solution)/shard_map/ppermute | solution.py:349
  19.5 12.5 %collective-permute-start.10 = (f32[128,128]{1,0:T(8,128)S(1)}, f32[128,128]{1,0:T(8,128)S(1)}, u32[]{:S(2)}, u32[]{:S(2)}) collective-permute-start(f32[128,128]{1,0:T(8,128)S(1)} %get-tuple-element.17.refs_8_.refs_0_), channel_id=1, source_target_pairs={{0,4},{1,5},{2,6},{3,7},{4,0},{5,1},{6,2},{7,3},{8,12},{9,13},{10,... | collective-permute-start | bytes 196616 | tf_op jit(solution)/shard_map/ppermute | solution.py:349
  24.8 21.3 %collective-permute-start.14 = (f32[784,128]{1,0:T(8,128)S(1)}, f32[784,128]{1,0:T(8,128)S(1)}, u32[]{:S(2)}, u32[]{:S(2)}) collective-permute-start(f32[784,128]{1,0:T(8,128)S(1)} %collective-permute-done.7.refs_8_), channel_id=1, source_target_pairs={{0,8},{1,9},{2,10},{3,11},{8,16},{9,17},{10,18},{11,19},{12,4},{13... | collective-permute-start | bytes 1204232 | tf_op jit(solution)/shard_map/ppermute | solution.py:349
  32.0 2.8 %copy-start.7 = (f32[16,3,128]{2,0,1:T(8,128)S(1)}, f32[16,3,128]{2,0,1:T(8,128)}, u32[]{:S(2)}) copy-start(f32[16,3,128]{2,0,1:T(8,128)} %param.22) | copy-start | bytes 73732
  32.0 2.8 %copy-start.11 = (s32[16,8]{0,1:T(8,128)S(1)}, s32[16,8]{0,1:T(8,128)}, u32[]{:S(2)}) copy-start(s32[16,8]{0,1:T(8,128)} %param.27) | copy-start | bytes 1540
  32.0 10.3 %collective-permute-start.11 = (f32[192,128]{1,0:T(8,128)S(1)}, f32[192,128]{1,0:T(8,128)S(1)}, u32[]{:S(2)}, u32[]{:S(2)}) collective-permute-start(f32[192,128]{1,0:T(8,128)S(1)} %shard_map.152.refs_13_.refs_4_), channel_id=1, source_target_pairs={{0,8},{1,9},{2,10},{3,11},{4,12},{5,13},{6,14},{7,15},{8,0},{9,1},... | collective-permute-start | bytes 294920 | tf_op jit(solution)/shard_map/ppermute | solution.py:349
  32.1 10.3 %collective-permute-start.12 = (f32[192,128]{1,0:T(8,128)S(1)}, f32[192,128]{1,0:T(8,128)S(1)}, u32[]{:S(2)}, u32[]{:S(2)}) collective-permute-start(f32[192,128]{1,0:T(8,128)S(1)} %shard_map.152.refs_13_.refs_4_), channel_id=1, source_target_pairs={{0,16},{1,17},{2,18},{3,19},{4,20},{5,21},{6,22},{7,23},{8,24},{9,... | collective-permute-start | bytes 294920 | tf_op jit(solution)/shard_map/ppermute | solution.py:349
  33.8 10.4 %collective-permute-start.13 = (f32[192,128]{1,0:T(8,128)S(1)}, f32[192,128]{1,0:T(8,128)S(1)}, u32[]{:S(2)}, u32[]{:S(2)}) collective-permute-start(f32[192,128]{1,0:T(8,128)S(1)} %shard_map.152.refs_13_.refs_4_), channel_id=1, source_target_pairs={{0,24},{1,25},{2,26},{3,27},{4,28},{5,29},{6,30},{7,31},{8,16},{9,... | collective-permute-start | bytes 294920 | tf_op jit(solution)/shard_map/ppermute | solution.py:349
  34.8 9.5 %copy-start.8 = (f32[8,3,128]{2,0,1:T(8,128)S(1)}, f32[8,3,128]{2,0,1:T(8,128)}, u32[]{:S(2)}) copy-start(f32[8,3,128]{2,0,1:T(8,128)} %param.23) | copy-start | bytes 36868
  34.8 9.5 %copy-start.10 = (s32[8,8]{1,0:T(8,128)S(1)}, s32[8,8]{1,0:T(8,128)}, u32[]{:S(2)}) copy-start(s32[8,8]{1,0:T(8,128)} %refs_1_.3) | copy-start | bytes 772
  34.8 9.5 %copy-start.12 = (s32[4,8]{1,0:T(4,128)S(1)}, s32[4,8]{1,0:T(4,128)}, u32[]{:S(2)}) copy-start(s32[4,8]{1,0:T(4,128)} %refs_2_.5) | copy-start | bytes 388
  42.4 1.9 %copy-start.9 = (f32[4,3,128]{2,0,1:T(4,128)S(1)}, f32[4,3,128]{2,0,1:T(4,128)}, u32[]{:S(2)}) copy-start(f32[4,3,128]{2,0,1:T(4,128)} %param.24) | copy-start | bytes 18436
  46.0 10.6 %copy-start = (f32[1,512,128]{2,1,0:T(8,128)S(1)}, f32[1,512,128]{2,1,0:T(8,128)}, u32[]{:S(2)}) copy-start(f32[1,512,128]{2,1,0:T(8,128)} %basis.1) | copy-start | bytes 786436
  46.1 10.6 %copy-start.1 = (f32[1,128,128]{2,1,0:T(8,128)S(1)}, f32[1,128,128]{2,1,0:T(8,128)}, u32[]{:S(2)}) copy-start(f32[1,128,128]{2,1,0:T(8,128)} %move.1) | copy-start | bytes 196612
  49.4 7.2 %collective-permute-start.15 = (f32[768,128]{1,0:T(8,128)S(1)}, f32[768,128]{1,0:T(8,128)S(1)}, u32[]{:S(2)}, u32[]{:S(2)}) collective-permute-start(f32[768,128]{1,0:T(8,128)S(1)} %get-tuple-element.22), channel_id=1, source_target_pairs={{0,1},{1,0},{2,3},{3,2},{4,5},{5,4},{6,7},{7,6},{8,9},{9,8},{10,11... | collective-permute-start | bytes 1179656 | tf_op jit(solution)/shard_map/ppermute | solution.py:349

commit v3 on v2

v3 whole, which is shorter than its diff:
```python
import functools

import jax
import jax.numpy as jnp
from jax import lax
from jax.experimental import pallas as pl
from jax.experimental.pallas import tpu as pltpu
from jax.sharding import PartitionSpec as P

INV_FOUR_PI = 0.07957747154594767
DELTA_SQ = 0.01
HIGHEST = lax.Precision.HIGHEST
AXIS = "leaf"

PLANE = 8
NEAR_SLOTS = 16
FAR_SLOTS = 8

META = 0
COEF = 16
PART = 144
PACK = 272
LEAF = 512
STRIP = 16

VMEM = pl.BlockSpec(memory_space=pltpu.VMEM)
SMEM = pl.BlockSpec(memory_space=pltpu.SMEM)
HBM = pl.BlockSpec(memory_space=pl.ANY)


def call(body, outs, ins, n_smem=0, n_hbm=0, after=(), scratch=(), flops=0, nbytes=0, vmem=32):
    n, m = len(ins), len(after)

    def ordered(*refs):
        return body(*refs[:n], *refs[n + m :])

    return pl.pallas_call(
        ordered if after else body,
        out_shape=outs,
        in_specs=[SMEM] * n_smem + [VMEM] * (n - n_smem - n_hbm) + [HBM] * (n_hbm + m),
        out_specs=jax.tree.map(lambda _: VMEM, outs),
        scratch_shapes=list(scratch),
        compiler_params=pltpu.CompilerParams(vmem_limit_bytes=vmem * 1024 * 1024),
        cost_estimate=pl.CostEstimate(flops=flops, bytes_accessed=nbytes, transcendentals=0),
    )(*ins, *after)


def f32(*shape):
    return jax.ShapeDtypeStruct(shape, jnp.float32)


def dot(a, b):
    return jnp.dot(a, b, precision=HIGHEST, preferred_element_type=jnp.float32)


def dot_t(a, b):
    return lax.dot_general(
        a, b, (((0,), (0,)), ((), ())), precision=HIGHEST, preferred_element_type=jnp.float32
    )


def split(x):
    high = x.astype(jnp.bfloat16)
    return high, (x - high.astype(jnp.float32)).astype(jnp.bfloat16)


def put_values(values, span, x):
    values[span, 0:128], values[span, 128:256] = split(x)


def split_dot(high, low, values):
    both = jnp.dot(high, values, preferred_element_type=jnp.float32)
    rest = jnp.dot(low, values[:, 0:128], preferred_element_type=jnp.float32)
    return both[:, 0:128] + (both[:, 128:256] + rest)


def columns(rows):
    pad = jnp.zeros((128 - rows.shape[0], 128), jnp.float32)
    return jnp.concatenate([rows, pad], axis=0).T


def green(cols, rows):
    dx = cols[0] - rows[0]
    dy = cols[1] - rows[1]
    dz = cols[2] - rows[2]
    return lax.rsqrt((dx * dx + dy * dy) + dz * dz + DELTA_SQ)


def skeleton(skel, cluster):
    return [skel[a, pl.ds(cluster, 1), :] for a in range(3)]


def own_columns(rows):
    cols = columns(jnp.concatenate(rows, axis=0))
    return [cols[:, a : a + 1] for a in range(3)]


def meta_skeleton(ref, at):
    return [ref[at + 4 * a + 3 : at + 4 * a + 4, :] for a in range(3)]


def window_bits(entry_at, count, base):
    bits = jnp.int32(0)
    for e in range(count):
        entry = entry_at(e)
        shift = jnp.clip(entry - base, 0, 31)
        bits = bits | jnp.where(entry >= 0, jnp.left_shift(jnp.int32(1), shift), 0)
    return bits


def leaf_bits(ref, at, start, count, leaf):
    row = ref[at + 15 : at + 16, :].astype(jnp.int32)
    lane = lax.broadcasted_iota(jnp.int32, (1, 128), 1)
    valid = (lane >= start) & (lane < start + count) & (row >= 0)
    shift = jnp.clip(row - (leaf - 9), 0, 23)
    one = jnp.where(valid, jnp.left_shift(jnp.ones_like(row), shift), 0)
    return jnp.sum(one.astype(jnp.float32)).astype(jnp.int32)


def has(bits, place):
    return (jnp.right_shift(bits, jnp.clip(place, 0, 31)) & 1) == 1


def chips_of(device):
    chip = device // 2
    place = chip % 4
    odd = (chip // 4) % 2
    out = [chip, chip ^ 1, chip ^ 2, chip ^ 3, chip ^ 4, chip + jnp.where(odd == 1, 4, -4)]
    for m in (1, 2, 3):
        other = place ^ m
        out.append((chip ^ m) + jnp.where(place < other, -4, 4))
    return out


def prepare_kernel(idx, *refs):
    names = 7
    ins, (ship, keep, send), bufs, sems = refs[:names], refs[names : names + 3], refs[names + 3 : -1], refs[-1]
    copies = [pltpu.make_async_copy(a, b, sems.at[k]) for k, (a, b) in enumerate(zip(ins, bufs))]
    for c in copies:
        c.start()
    for c in copies:
        c.wait()
    vec, basis, move, pts, skel, near_list, far_list = bufs
    core = idx[0] % 2
    pieces = []
    for k in range(4):
        for a in range(3):
            pieces.append(pts[a, :, 128 * k : 128 * (k + 1)])
        if k < 3:
            pieces.append(skel[k])
    rest = jnp.zeros((1, 128 - NEAR_SLOTS - FAR_SLOTS), jnp.float32)
    lists = [near_list[...].astype(jnp.float32), far_list[...].astype(jnp.float32), rest]
    pieces.append(jnp.concatenate(lists, axis=1))
    meta = jnp.concatenate(pieces, axis=0)
    coef = dot_t(basis[0], vec[0])
    up = dot_t(move[0], coef)
    ship[0:LEAF, :] = vec[0]
    ship[LEAF : LEAF + PACK, :] = jnp.concatenate([meta, coef, up], axis=0)
    low, high = up[:64], up[64:]
    keep[...] = jnp.where(core == 0, low, high)
    send[0:64, :] = jnp.where(core == 0, high, low)
    send[64:80, :] = meta


def add_near(device, slots, blocks, metas, total, scratch):
    values, cols = scratch
    core = device % 2
    chips = chips_of(device)
    bits = []
    for s, (ref, at) in enumerate(metas):
        bits.append(leaf_bits(ref, at, 0, NEAR_SLOTS, device ^ s))
        cols[128 * s : 128 * (s + 1), :] = columns(ref[at : at + 16, :])

    def with_sums(*sums):
        for slot, (vec, pack, at) in zip(slots, blocks):
            leaf = 2 * chips[slot] + core
            put_values(values, slice(0, LEAF), vec[0:LEAF, :] * INV_FOUR_PI)
            for s in range(2):
                listed = has(bits[s], leaf - ((device ^ s) - 9))
                for m in range(2):
                    half = values[256 * m : 256 * (m + 1), :]
                    pltpu.matmul_push_rhs(jnp.where(listed, half, jnp.zeros_like(half)), 0, m)
                for i in range(LEAF // STRIP):
                    start, piece = 128 * s + STRIP * i % 128, STRIP * i // 128
                    col = [
                        jnp.broadcast_to(cols[start : start + STRIP, 4 * piece + a : 4 * piece + a + 1], (STRIP, 128))
                        for a in range(3)
                    ]
                    for m in range(2):
                        parts = []
                        for k in (2 * m, 2 * m + 1):
                            row = [pack[at + 4 * k + a : at + 4 * k + a + 1, :] for a in range(3)]
                            parts.append(split(green(col, row)))
                        strip = sums[(s * (LEAF // STRIP) + i) * 2 + m]
                        for j in range(2):
                            side = jnp.concatenate([part[j] for part in parts], axis=1)
                            pltpu.matmul_acc_lhs(strip, side, 0 if i == 0 and j == 0 else None)
        for i in range(2 * LEAF // STRIP):
            both = pltpu.matmul_pop(sums[2 * i]) + pltpu.matmul_pop(sums[2 * i + 1])
            total[STRIP * i : STRIP * (i + 1), :] += both[:, 0:128] + both[:, 128:256]

    shape = (STRIP, 256)
    pl.run_scoped(with_sums, *[pltpu.ACC(m)(shape, jnp.float32) for _ in range(2 * LEAF // STRIP) for m in range(2)])


def add_far(device, slots, blocks, metas, far_pair, skel_pair, out, scratch):
    high, low, values = scratch
    n = len(slots)
    core = device % 2
    chips = chips_of(device)
    chip = device // 2
    n_chips = skel_pair.shape[1]
    depth = slice(0, 128 * n)
    bits = window_bits(lambda e: far_pair[e, chip], FAR_SLOTS, chip - 4)
    cols = own_columns(skeleton(skel_pair, chip))
    for j, (slot, (_, pack, at)) in enumerate(zip(slots, blocks)):
        other = chips[slot]
        span = slice(128 * j, 128 * (j + 1))
        put_values(values, span, pack[at + PART : at + PART + 128, :])
        g = green(cols, skeleton(skel_pair, jnp.clip(other, 0, n_chips - 1)))
        high[0:128, span], low[0:128, span] = split(jnp.where(has(bits, other - chip + 4), g, 0.0))
    out[256:384, :] += split_dot(high[0:128, depth], low[0:128, depth], values[depth, :]) * INV_FOUR_PI
    for j, (_, pack, at) in enumerate(blocks):
        put_values(values, slice(128 * j, 128 * (j + 1)), pack[at + COEF : at + COEF + 128, :])
    for s, (ref, base) in enumerate(metas):
        leaf = device ^ s
        bits = leaf_bits(ref, base, NEAR_SLOTS, FAR_SLOTS, leaf)
        cols = own_columns(meta_skeleton(ref, base))
        for j, (slot, (_, pack, at)) in enumerate(zip(slots, blocks)):
            g = green(cols, meta_skeleton(pack, at))
            ok = has(bits, 2 * chips[slot] + core - (leaf - 9))
            here = (slice(128 * s, 128 * (s + 1)), slice(128 * j, 128 * (j + 1)))
            high[here], low[here] = split(jnp.where(ok, g, 0.0))
    out[0:256, :] += split_dot(high[:, depth], low[:, depth], values[depth, :]) * INV_FOUR_PI


def own_kernel(idx, got, ship, total, own, *scratch):
    copy = pltpu.make_async_copy(ship, own, scratch[-1])
    copy.start()
    total[...] = jnp.zeros_like(total)
    copy.wait()
    add_near(idx[0], (0,), [(own, own, LEAF)], ((own, LEAF), (got, 64)), total, scratch[:-1])


def near_kernel(slots, idx, got, own, *refs):
    n = len(slots)
    blocks = [(b, b, LEAF) for b in refs[:n]]
    total_in, total, *scratch = refs[n:]
    total[...] = total_in[...]
    add_near(idx[0], slots, blocks, ((own, LEAF), (got, 64)), total, scratch)


def stack_kernel(*refs):
    out = refs[-1]
    for j, r in enumerate(refs[:-1]):
        out[128 * j : 128 * (j + 1), :] = r[...]


def cross_kernel(idx, even, odd, *outs):
    plane_odd = idx[0] // 8 % 2 == 1
    place = idx[0] // 2 % 4
    for m, out in zip((1, 2), outs):
        out[...] = jnp.where(((place ^ m) < place) == plane_odd, even[...], odd[...])


def way_kernel(idx, bx, by, out):
    out[...] = jnp.where(idx[0] % 2 == 0, bx[...], by[...])


def close_kernel(idx, far_pair, got, own, skel_pair, total, ctx, quad_own, quad_got, *refs):
    blocks = [(b, b, LEAF) for b in (own,) + refs[:8]]
    keep, share, low, *scratch = refs[8:]
    low[...] = jnp.zeros_like(low)
    add_far(idx[0], range(9), blocks, ((own, LEAF), (got, 64)), far_pair, skel_pair, low, scratch)
    local_top = quad_own[128:256, :] + quad_got[128:256, :]
    local_quad = quad_own[0:128, :] + quad_got[0:128, :] + dot(ctx[0:128, :], local_top)
    low[256:384, :] += dot(ctx[128:256, :], local_quad)
    keep[0:512, :] = total[0:512, :]
    keep[512:640, :] = low[0:128, :]
    keep[640:768, :] = low[256:384, :]
    share[0:512, :] = total[512:1024, :]
    share[512:768, :] = low[128:384, :]


def rise_kernel(keep, got, epair, equad, out, moved):
    moved[...] = epair[...]
    out[0:128, :] = dot_t(epair[...], keep[...] + got[0:64, :])
    out[128:160, :] = equad[...]


def quad_kernel(own, bx, epair, out):
    out[0:128, :] = own[0:128, :] + bx[0:128, :]
    out[128:160, :] = own[128:160, :]
    out[160:192, :] = bx[128:160, :]
    out[192:256, :] = epair[...]


def top_kernel(idx, mine, theirs, send, ctx, quad, top):
    device = idx[0]
    core = device % 2
    half = pl.multiple_of(core * 64, 64)
    for j in range(2):
        member = 2 * (((device // 2) ^ j) % 2)
        mine_at = pl.multiple_of((member + core) * 32, 32)
        sib_at = pl.multiple_of((member + 1 - core) * 32, 32)
        ctx[pl.ds(mine_at, 32), :] = mine[128 + 32 * j : 160 + 32 * j, :]
        ctx[pl.ds(sib_at, 32), :] = theirs[128 + 32 * j : 160 + 32 * j, :]
    ctx[pl.ds(128 + half, 64), :] = mine[192:256, :]
    ctx[pl.ds(192 - half, 64), :] = theirs[192:256, :]
    quad[...] = mine[0:128, :] + theirs[0:128, :]
    top[...] = dot_t(ctx[0:128, :], quad[...])
    send[0:64, :] = quad[pl.ds(half, 64), :]
    send[64:128, :] = top[pl.ds(half, 64), :]


def upper_kernel(idx, far_quad, far_top, planes, skel_quad, skel_top, mine, send, high, low, values, rows):
    device = idx[0]
    half = pl.multiple_of((device % 2) * 64, 64)
    plane = device // 8
    quad = device // 4
    rows[...] = jnp.zeros_like(rows)
    for j in range(4):
        rows[pl.ds(128 * j + half, 64), :] = planes[128 * j + 64 : 128 * (j + 1), :]
    put_values(values, slice(0, 512), rows[...])
    bits = window_bits(lambda e: far_top[plane, e], FAR_SLOTS, 0)
    cols = own_columns(skeleton(skel_top, plane))
    for j in range(4):
        other = plane ^ j
        span = slice(128 * j, 128 * (j + 1))
        g = jnp.where(has(bits, other), green(cols, skeleton(skel_top, other)), 0.0)
        high[0:128, span], low[0:128, span] = split(g)
    top = split_dot(high[0:128, :], low[0:128, :], values[...]) * INV_FOUR_PI
    mine[128:256, :] = top
    send[128:256, :] = top
    for j in range(4):
        rows[pl.ds(128 * j + half, 64), :] = planes[128 * j : 128 * j + 64, :]
    put_values(values, slice(0, 512), rows[...])
    for s in range(2):
        target = quad ^ s
        bits = window_bits(lambda e: far_quad[target, e], FAR_SLOTS, target - 4)
        cols = own_columns(skeleton(skel_quad, target))
        for j in range(4):
            other = quad ^ (2 * j)
            here = (slice(128 * s, 128 * (s + 1)), slice(128 * j, 128 * (j + 1)))
            ok = has(bits, other - target + 4) & (other >= target - 4) & (other <= target + 4)
            high[here], low[here] = split(jnp.where(ok, green(cols, skeleton(skel_quad, other)), 0.0))
    far = split_dot(high[...], low[...], values[...]) * INV_FOUR_PI
    mine[0:128, :] = far[0:128]
    send[0:128, :] = far[128:256]


def final_kernel(keep, got, move, basis, out):
    local_pair = keep[640:768, :] + got[640:768, :]
    local = keep[512:640, :] + got[512:640, :] + dot(move[0], local_pair)
    out[0] = keep[0:512, :] + got[0:512, :] + dot(basis[0], local)


def near_scratch():
    return [
        pltpu.VMEM((512, 256), jnp.bfloat16),
        pltpu.VMEM((256, 128), jnp.float32),
    ]


def far_scratch(rows, n):
    wide = pltpu.VMEM((rows, 128 * n), jnp.bfloat16)
    return [wide, wide, pltpu.VMEM((128 * n, 256), jnp.bfloat16)]


NEAR_FLOPS = 2 * 6 * 512 * 512 * 128


def permute(value, target):
    n = lax.axis_size(AXIS)
    pairs = [(i, target(i)) for i in range(n)]
    return lax.ppermute(value, AXIS, [(i, j) for i, j in pairs if 0 <= j < n and i != j])


def swap(value, mask):
    return permute(value, lambda i: i ^ mask)


def listed_sum(own, entries, skels, coefs):
    def advance(running, partner):
        at = jnp.maximum(partner, 0)
        rows = skels[at]
        g = green([own[a][:, None] for a in range(3)], [rows[a][None, :] for a in range(3)]) * INV_FOUR_PI
        contrib = jnp.dot(g, coefs[at], precision=HIGHEST)
        return running + jnp.where(partner >= 0, contrib, 0.0), None

    return lax.scan(advance, jnp.zeros(coefs.shape[1:], jnp.float32), entries)[0]


def upper_anywhere(device, send, ctx, far_quad, far_top, skel_quad, skel_top):
    n = lax.axis_size(AXIS)
    part = lax.dynamic_slice_in_dim(send, device // 2 % 2 * 64, 64, 0)
    every = lax.all_gather(part, AXIS, axis=0, tiled=True).reshape(n // 4, 2, 2, 64, 128)
    quads = every[:, 0].reshape(n // 4, 128, 128)
    tops = every[:, 1].reshape(n // PLANE, 2, 128, 128).sum(axis=1)
    plane, quad = device // 8, device // 4
    local_top = listed_sum(skel_top[plane], far_top[plane], skel_top, tops)
    far = listed_sum(skel_quad[quad], far_quad[quad], skel_quad, quads)
    whole = jnp.concatenate([far, local_top], axis=0)
    return jnp.where(device % 2 == 0, whole, 0.0)


def per_device(
    vectors,
    points,
    leaf_basis,
    transfer_leaf,
    transfer_pair,
    transfer_quad,
    skel_leaf,
    skel_pair,
    skel_quad,
    skel_top,
    near_list,
    far_leaf,
    far_pair,
    far_quad,
    far_top,
):
    n = lax.axis_size(AXIS)
    device = lax.axis_index(AXIS)
    idx = device.reshape(1).astype(jnp.int32)
    def before(i):
        return i + 8 if i // 8 % 2 == 1 else i - 8

    ins = [vectors, leaf_basis, transfer_leaf]
    ins += [points.transpose(1, 0, 2), skel_leaf.transpose(1, 0, 2)]
    ins += [near_list, far_leaf]
    ship, keep, send = call(
        prepare_kernel,
        (f32(LEAF + PACK, 128), f32(64, 128), f32(80, 128)),
        [idx, *ins],
        n_smem=1,
        n_hbm=len(ins),
        scratch=[pltpu.VMEM(a.shape, a.dtype) for a in ins] + [pltpu.SemaphoreType.DMA((len(ins),))],
        flops=2 * 6 * 640 * 128 * 128,
        nbytes=1 << 20,
        vmem=60,
    )
    got = swap(send, 1)
    def near(slots, blocks, total, after):
        return call(
            functools.partial(near_kernel, slots),
            f32(1024, 128),
            [idx, got, own] + blocks + [total],
            n_smem=1,
            after=after,
            scratch=near_scratch(),
            flops=2 * len(slots) * NEAR_FLOPS,
        )

    bx, by, be = [swap(ship, m) for m in (2, 4, 8)]
    bo = permute(ship, before)
    rise, epair = call(rise_kernel, (f32(160, 128), f32(64, 128)), [keep, got, transfer_pair, transfer_quad], flops=2 * 6 * 64 * 128 * 128)
    rise_x = swap(rise, 2)
    total, own = call(
        own_kernel,
        (f32(1024, 128), f32(LEAF + PACK, 128)),
        [idx, got, ship],
        n_smem=1,
        n_hbm=1,
        after=[rise],
        scratch=near_scratch() + [pltpu.SemaphoreType.DMA],
        flops=2 * NEAR_FLOPS,
    )
    half = call(quad_kernel, f32(256, 128), [rise, rise_x, epair], after=[total])
    way = call(way_kernel, f32(LEAF + PACK, 128), [idx, bx, by], n_smem=1, after=[half])
    bd = permute(way, lambda i: i ^ 4 if i % 2 == 0 else i ^ 2)

    half_got = swap(half, 1)
    shared, ctx = call(
        top_kernel,
        (f32(128, 128), f32(256, 128)),
        [idx, half, half_got],
        n_smem=1,
        after=[way],
        scratch=[pltpu.VMEM((128, 128), jnp.float32), pltpu.VMEM((128, 128), jnp.float32)],
        flops=2 * 6 * 128**3,
    )
    direct = n == 4 * PLANE
    received = [swap(shared, PLANE * m) for m in (3, 2, 1)][::-1] if direct else []
    block = f32(LEAF + PACK, 128)
    sx, sy = call(cross_kernel, (block,) * 2, [idx, be, bo], n_smem=1, after=[shared])
    cx, cy = swap(sx, 2), swap(sy, 4)
    cd = permute(bd, lambda i: i + 8 if i // 2 % 4 < 2 else i - 8)
    total = near((1, 2), [bx, by], total, [sx])
    total = near((4, 5), [be, bo], total, [])
    planes = call(stack_kernel, f32(512, 128), [shared, *received], after=[total]) if direct else shared
    if direct:
        skels = [skel_quad.transpose(1, 0, 2), skel_top.transpose(1, 0, 2)]
        quad_own, quad_send = call(
            upper_kernel,
            (f32(256, 128), f32(256, 128)),
            [idx, far_quad, far_top, planes, *skels],
            n_smem=3,
            after=[total],
            scratch=far_scratch(256, 4) + [pltpu.VMEM((512, 128), jnp.float32)],
            flops=2 * 6 * 12 * 128**3,
        )
        quad_got = swap(quad_send, 4)
    else:
        quad_own = upper_anywhere(device, shared, ctx, far_quad, far_top, skel_quad, skel_top)
        quad_got = jnp.zeros_like(quad_own)
    far_pair_t, skel_pair_t = far_pair.T, skel_pair.transpose(1, 0, 2)
    total = near((3, 6, 7), [bd, cx, cy], total, [quad_own])
    total = near((8,), [cd], total, [])
    keep, share = call(
        close_kernel,
        (f32(768, 128), f32(768, 128)),
        [idx, far_pair_t, got, own, skel_pair_t, total, ctx, quad_own, quad_got]
        + [bx, by, bd, be, bo, cx, cy, cd],
        n_smem=2,
        scratch=[pltpu.VMEM((384, 128), jnp.float32)] + far_scratch(256, 9),
        flops=2 * 3 * 28 * 128**3,
    )
    return call(
        final_kernel,
        f32(1, 512, 128),
        [keep, swap(share, 1), transfer_leaf, leaf_basis],
        flops=2 * 6 * 640 * 128 * 128,
    )


def solution(mesh):
    placed = (
        P("leaf", None, None),
        P("leaf", None, None),
        P("leaf", None, None),
        P("leaf", None, None),
        P("leaf", None),
        P("leaf", None),
        P("leaf", None, None),
        P(),
        P(),
        P(),
        P("leaf", None),
        P("leaf", None),
        P(),
        P(),
        P(),
    )
    return jax.shard_map(
        per_device, mesh=mesh, in_specs=placed, out_specs=P("leaf", None, None), check_vma=False
    )
```

time: 56.9 us -> 51.5 us (0.905)
  the two profiles are of different devices: /device:TPU:15 before, /device:TPU:0 now
where the time goes in v3:
time: 51.5 us; the launch traced here: 51.2 us
  starting transfers between devices  20.8 us (40%)
  Pallas kernels  20.3 us (39%)
  waiting for transfers between devices  6.74 us (13%)
  local copies, waits for them, and re-layouts  3.08 us (6%)
    ppermute x16, starting transfers between devices, permute(): lax.ppermute(value, AXIS, [(i, j) for i, j in pairs if 0 <= j < n and i !...  20.8 us
    pallas_call x15, Pallas kernels, call(): pl.pallas_call(ordered if after else body, out_shape=outs, in_specs=[SMEM...  20.3 us
    ppermute x16, waiting for transfers between devices, permute(): lax.ppermute(value, AXIS, [(i, j) for i, j in pairs if 0 <= j < n and i !...  6.74 us
    unnamed x24, local copies, waits for them, and re-layouts  3.08 us
  transfers between devices with their start and end apart: 16, of which 6 were waited for; matrix products, arithmetic and copies ran while one was open for 0% of the time, Pallas kernels for 27%

profile of v3, /device:TPU:0, one launch (start us, length us, event | category | flops | bytes accessed | tf_op | source)
XLA Modules:
  0.0 51.2 jit_solution(2427324061126217836)
XLA Ops:
  0.0 0.0 copy-start.2
  0.0 2.6 %shard_map.145 = (f32[784,128]{1,0:T(8,128)}, f32[64,128]{1,0:T(8,128)}, f32[80,128]{1,0:T(8,128)}) custom-call(s32[1]{0:T(128)} %bitcast.idx.refs_0_, f32[1,512,128]{2,1,0:T(8,128)} %refs_0_.1, f32[1,512,128]{2,1,0:T(8,128)} %basis.1, f32[1,128,128]{2,1,0:T(8,128)} %move.1, f32[3,1,512]{2,1,0:T(1,128)} %bitcast.11, f32[3,1,128]{2,1,0:T(1,128)} %bitcast.12, ...), custom_call_target="tpu_custom_call" | custom-call | flops 125829120 | bytes 1048576 | tf_op jit(solution)/shard_map/pallas_call | solution.py:37
  2.6 3.0 %collective-permute-start.2 = (f32[784,128]{1,0:T(8,128)}, f32[784,128]{1,0:T(8,128)S(1)}, u32[]{:S(2)}, u32[]{:S(2)}) collective-permute-start(f32[784,128]{1,0:T(8,128)} %get-tuple-element.21.refs_2_), channel_id=1, source_target_pairs={{0,4},{1,5},{2,6},{3,7},{4,0},{5,1},{6,2},{7,3},{8,12},{9,13},{10,... | collective-permute-start | bytes 1204232 | tf_op jit(solution)/shard_map/ppermute | solution.py:376
  5.6 1.5 %collective-permute-start.1 = (f32[784,128]{1,0:T(8,128)}, f32[784,128]{1,0:T(8,128)S(1)}, u32[]{:S(2)}, u32[]{:S(2)}) collective-permute-start(f32[784,128]{1,0:T(8,128)} %get-tuple-element.21.refs_2_), channel_id=1, source_target_pairs={{0,2},{1,3},{2,0},{3,1},{4,6},{5,7},{6,4},{7,5},{8,10},{9,11},{10,... | collective-permute-start | bytes 1204232 | tf_op jit(solution)/shard_map/ppermute | solution.py:376
  7.1 0.7 %collective-permute-start.7 = (f32[784,128]{1,0:T(8,128)}, f32[784,128]{1,0:T(8,128)S(1)}, u32[]{:S(2)}, u32[]{:S(2)}) collective-permute-start(f32[784,128]{1,0:T(8,128)} %get-tuple-element.21.refs_2_), channel_id=1, source_target_pairs={{8,16},{9,17},{10,18},{11,19},{12,20},{13,21},{14,22},{15,23},{16,... | collective-permute-start | bytes 1204232 | tf_op jit(solution)/shard_map/ppermute | solution.py:376
  7.8 4.4 %collective-permute-start.6 = (f32[784,128]{1,0:T(8,128)}, f32[784,128]{1,0:T(8,128)S(1)}, u32[]{:S(2)}, u32[]{:S(2)}) collective-permute-start(f32[784,128]{1,0:T(8,128)} %get-tuple-element.21.refs_2_), channel_id=1, source_target_pairs={{0,8},{1,9},{2,10},{3,11},{4,12},{5,13},{6,14},{7,15},{8,0},{9,1},... | collective-permute-start | bytes 1204232 | tf_op jit(solution)/shard_map/ppermute | solution.py:376
  12.2 0.0 collective-permute-start
  12.2 1.4 %collective-permute-done.got.refs_1_ = f32[80,128]{1,0:T(8,128)S(1)} collective-permute-done((f32[80,128]{1,0:T(8,128)}, f32[80,128]{1,0:T(8,128)S(1)}, u32[]{:S(2)}, u32[]{:S(2)}) %collective-permute-start) | collective-permute-done | bytes 40992 | tf_op jit(solution)/shard_map/ppermute | solution.py:376
  13.6 0.0 copy-done.2
  13.6 0.0 copy-done.5
  13.7 0.8 %copy-done.3 = f32[64,128]{1,0:T(8,128)S(1)} copy-done((f32[64,128]{1,0:T(8,128)S(1)}, f32[64,128]{1,0:T(8,128)}, u32[]{:S(2)}) %copy-start.3) | copy-done | bytes 32792
  14.4 0.3 shard_map.146
  14.7 0.6 %collective-permute-start.3 = (f32[160,128]{1,0:T(8,128)S(1)}, f32[160,128]{1,0:T(8,128)S(1)}, u32[]{:S(2)}, u32[]{:S(2)}) collective-permute-start(f32[160,128]{1,0:T(8,128)S(1)} %get-tuple-element.23.refs_3_.refs_0_), channel_id=1, source_target_pairs={{0,2},{1,3},{2,0},{3,1},{4,6},{5,7},{6,4},{7,5},{8,10},{9,11},{10,... | collective-permute-start | bytes 245768 | tf_op jit(solution)/shard_map/ppermute | solution.py:376
  15.3 1.0 %copy-done.7 = f32[784,128]{1,0:T(8,128)S(1)} copy-done((f32[784,128]{1,0:T(8,128)S(1)}, f32[784,128]{1,0:T(8,128)}, u32[]{:S(2)}) %copy-start.7) | copy-done | bytes 401432
  16.3 1.7 %shard_map.147 = (f32[1024,128]{1,0:T(8,128)S(1)}, f32[784,128]{1,0:T(8,128)S(1)}) custom-call(s32[1]{0:T(128)} %bitcast.idx.refs_0_, f32[80,128]{1,0:T(8,128)S(1)} %collective-permute-done.got.refs_1_, f32[784,128]{1,0:T(8,128)S(1)} %copy-done.7, f32[160,128]{1,0:T(8,128)S(1)} %get-tuple-element.23.refs_3_.refs_0_), custom_call_target="tpu_custom_call" | custom-call | flops 805306368 | tf_op jit(solution)/shard_map/pallas_call | solution.py:37
  17.9 1.3 %collective-permute-done.3.refs_1_ = f32[160,128]{1,0:T(8,128)S(1)} collective-permute-done((f32[160,128]{1,0:T(8,128)S(1)}, f32[160,128]{1,0:T(8,128)S(1)}, u32[]{:S(2)}, u32[]{:S(2)}) %collective-permute-start.3) | collective-permute-done | bytes 81952 | tf_op jit(solution)/shard_map/ppermute | solution.py:376
  19.3 0.0 collective-permute-done.2.refs_2_.refs_4_.refs_1_
  19.3 0.0 collective-permute-done.1.refs_1_.refs_3_.refs_0_
  19.3 0.1 shard_map.149.refs_3_
  19.3 0.6 %collective-permute-start.4 = (f32[784,128]{1,0:T(8,128)S(1)}, f32[784,128]{1,0:T(8,128)S(1)}, u32[]{:S(2)}, u32[]{:S(2)}) collective-permute-start(f32[784,128]{1,0:T(8,128)S(1)} %shard_map.149.refs_3_), channel_id=1, source_target_pairs={{0,4},{1,3},{2,6},{3,1},{4,0},{5,7},{6,2},{7,5},{8,12},{9,11},{10,... | collective-permute-start | bytes 1204232 | tf_op jit(solution)/shard_map/ppermute | solution.py:376
  19.9 0.0 collective-permute-start.8
  19.9 1.3 %collective-permute-done.8.refs_2_ = f32[256,128]{1,0:T(8,128)S(1)} collective-permute-done((f32[256,128]{1,0:T(8,128)S(1)}, f32[256,128]{1,0:T(8,128)S(1)}, u32[]{:S(2)}, u32[]{:S(2)}) %collective-permute-start.8) | collective-permute-done | bytes 131104 | tf_op jit(solution)/shard_map/ppermute | solution.py:376
  21.3 0.3 shard_map.150
  21.6 0.0 collective-permute-done.7.refs_2_.refs_1_.refs_4_
  21.6 0.0 collective-permute-done.6.refs_1_.refs_0_.refs_3_
  21.6 0.1 shard_map.151
  21.7 1.6 %collective-permute-start.10 = (f32[784,128]{1,0:T(8,128)S(1)}, f32[784,128]{1,0:T(8,128)S(1)}, u32[]{:S(2)}, u32[]{:S(2)}) collective-permute-start(f32[784,128]{1,0:T(8,128)S(1)} %get-tuple-element.29), channel_id=1, source_target_pairs={{0,4},{1,5},{2,6},{3,7},{4,0},{5,1},{6,2},{7,3},{8,12},{9,13},{10,... | collective-permute-start | bytes 1204232 | tf_op jit(solution)/shard_map/ppermute | solution.py:376
  23.3 0.6 %collective-permute-start.9 = (f32[784,128]{1,0:T(8,128)S(1)}, f32[784,128]{1,0:T(8,128)S(1)}, u32[]{:S(2)}, u32[]{:S(2)}) collective-permute-start(f32[784,128]{1,0:T(8,128)S(1)} %get-tuple-element.28.refs_6_), channel_id=1, source_target_pairs={{0,2},{1,3},{2,0},{3,1},{4,6},{5,7},{6,4},{7,5},{8,10},{9,11},{10,... | collective-permute-start | bytes 1204232 | tf_op jit(solution)/shard_map/ppermute | solution.py:376
  23.8 3.6 %collective-permute-start.13 = (f32[128,128]{1,0:T(8,128)S(1)}, f32[128,128]{1,0:T(8,128)S(1)}, u32[]{:S(2)}, u32[]{:S(2)}) collective-permute-start(f32[128,128]{1,0:T(8,128)S(1)} %get-tuple-element.27.refs_3_.refs_0_), channel_id=1, source_target_pairs={{0,24},{1,25},{2,26},{3,27},{4,28},{5,29},{6,30},{7,31},{8,16},{9,... | collective-permute-start | bytes 196616 | tf_op jit(solution)/shard_map/ppermute | solution.py:376
  27.4 0.0 collective-permute-start.12
  27.4 2.4 %shard_map.152.refs_2_ = f32[1024,128]{1,0:T(8,128)S(1)} custom-call(s32[1]{0:T(128)} %bitcast.idx.refs_0_, f32[80,128]{1,0:T(8,128)S(1)} %collective-permute-done.got.refs_1_, f32[784,128]{1,0:T(8,128)S(1)} %get-tuple-element.24.refs_2_.own, f32[784,128]{1,0:T(8,128)S(1)} %collective-permute-done.1.refs_1_.refs_3_.refs_0_, ...), custom_call_target="tpu_custom_call" | custom-call | flops 1610612736 | tf_op jit(solution)/shard_map/pallas_call | solution.py:37
  29.8 0.8 %collective-permute-done.13.refs_3_ = f32[128,128]{1,0:T(8,128)S(1)} collective-permute-done((f32[128,128]{1,0:T(8,128)S(1)}, f32[128,128]{1,0:T(8,128)S(1)}, u32[]{:S(2)}, u32[]{:S(2)}) %collective-permute-start.13) | collective-permute-done | bytes 65568 | tf_op jit(solution)/shard_map/ppermute | solution.py:376
  30.7 1.3 %collective-permute-start.11 = (f32[128,128]{1,0:T(8,128)S(1)}, f32[128,128]{1,0:T(8,128)S(1)}, u32[]{:S(2)}, u32[]{:S(2)}) collective-permute-start(f32[128,128]{1,0:T(8,128)S(1)} %get-tuple-element.27.refs_3_.refs_0_), channel_id=1, source_target_pairs={{0,8},{1,9},{2,10},{3,11},{4,12},{5,13},{6,14},{7,15},{8,0},{9,1},... | collective-permute-start | bytes 196616 | tf_op jit(solution)/shard_map/ppermute | solution.py:376
  32.0 0.0 collective-permute-done.4.refs_3_.refs_2_
  32.0 2.8 %collective-permute-start.5 = (f32[784,128]{1,0:T(8,128)S(1)}, f32[784,128]{1,0:T(8,128)S(1)}, u32[]{:S(2)}, u32[]{:S(2)}) collective-permute-start(f32[784,128]{1,0:T(8,128)S(1)} %collective-permute-done.4.refs_3_.refs_2_), channel_id=1, source_target_pairs={{0,8},{1,9},{2,10},{3,11},{8,16},{9,17},{10,18},{11,19},{12,4},{13... | collective-permute-start | bytes 1204232 | tf_op jit(solution)/shard_map/ppermute | solution.py:376
  34.8 2.4 %shard_map.153.refs_4_.refs_6_ = f32[1024,128]{1,0:T(8,128)S(1)} custom-call(s32[1]{0:T(128)} %bitcast.idx.refs_0_, f32[80,128]{1,0:T(8,128)S(1)} %collective-permute-done.got.refs_1_, f32[784,128]{1,0:T(8,128)S(1)} %get-tuple-element.24.refs_2_.own, f32[784,128]{1,0:T(8,128)S(1)} %collective-permute-done.6.refs_1_.refs_0_.refs_3_, ...), custom_call_target="tpu_custom_call" | custom-call | flops 1610612736 | tf_op jit(solution)/shard_map/pallas_call | solution.py:37
  37.2 0.0 copy-start.8
  37.2 0.0 copy-start.9
  37.2 0.0 copy-start.10
  37.2 0.0 collective-permute-done.12.refs_2_
  37.2 0.0 collective-permute-done.11.refs_1_
  37.3 0.0 copy-start.11
  37.3 0.6 %copy-done.8 = f32[8,3,128]{2,0,1:T(8,128)S(1)} copy-done((f32[8,3,128]{2,0,1:T(8,128)S(1)}, f32[8,3,128]{2,0,1:T(8,128)}, u32[]{:S(2)}) %copy-start.8) | copy-done | bytes 12312
  37.9 0.0 copy-done.9
  37.9 0.0 copy-done.10
  37.9 0.0 copy-done.11
  38.0 1.7 %shard_map.155 = (f32[256,128]{1,0:T(8,128)S(1)}, f32[256,128]{1,0:T(8,128)S(1)}) custom-call(s32[1]{0:T(128)} %bitcast.idx.refs_0_, s32[8,8]{1,0:T(8,128)S(1)} %copy-done.10, s32[4,8]{1,0:T(4,128)S(1)} %copy-done.11, f32[512,128]{1,0:T(8,128)S(1)} %shard_map.154.refs_3_, f32[3,8,128]{2,1,0:T(8,128)S(1)} %bitcast.9, f32[3,4,128]{2,1,0:T(4,128)S(1)} %bitcast.10, ...), custom_call_target="tpu_custom_call" | custom-call | flops 301989888 | tf_op jit(solution)/shard_map/pallas_call | solution.py:37
  39.6 0.1 collective-permute-start.14
  39.7 0.0 collective-permute-done.10.refs_5_.refs_6_
  39.7 0.0 collective-permute-done.9.refs_4_.refs_5_
  39.7 3.4 %shard_map.156.refs_1_ = f32[1024,128]{1,0:T(8,128)S(1)} custom-call(s32[1]{0:T(128)} %bitcast.idx.refs_0_, f32[80,128]{1,0:T(8,128)S(1)} %collective-permute-done.got.refs_1_, f32[784,128]{1,0:T(8,128)S(1)} %get-tuple-element.24.refs_2_.own, f32[784,128]{1,0:T(8,128)S(1)} %collective-permute-done.4.refs_3_.refs_2_, ...), custom_call_target="tpu_custom_call" | custom-call | flops 2415919104 | tf_op jit(solution)/shard_map/pallas_call | solution.py:37
  43.1 0.0 copy-start.4
  43.1 0.0 collective-permute-done.5.refs_0_.refs_7_
  43.1 1.4 %shard_map.157.total = f32[1024,128]{1,0:T(8,128)S(1)} custom-call(s32[1]{0:T(128)} %bitcast.idx.refs_0_, f32[80,128]{1,0:T(8,128)S(1)} %collective-permute-done.got.refs_1_, f32[784,128]{1,0:T(8,128)S(1)} %get-tuple-element.24.refs_2_.own, f32[784,128]{1,0:T(8,128)S(1)} %collective-permute-done.5.refs_0_.refs_7_, f32[1024,128]{1,0:T(8,128)S(1)} %shard_map.156.refs_1_), custom_call_target="tpu_custom_call" | custom-call | flops 805306368 | tf_op jit(solution)/shard_map/pallas_call | solution.py:37
  44.6 0.0 copy-start.6
  44.6 0.1 collective-permute-done.14.quad_got
  44.7 0.0 copy-done.4
  44.7 0.6 %copy-done.6 = s32[16,8]{0,1:T(8,128)S(1)} copy-done((s32[16,8]{0,1:T(8,128)S(1)}, s32[16,8]{0,1:T(8,128)}, u32[]{:S(2)}) %copy-start.6) | copy-done | bytes 536
  45.3 2.8 %shard_map.158 = (f32[768,128]{1,0:T(8,128)S(1)}, f32[768,128]{1,0:T(8,128)S(1)}) custom-call(s32[1]{0:T(128)} %bitcast.idx.refs_0_, s32[8,16]{1,0:T(8,128)S(1)} %bitcast.8, f32[80,128]{1,0:T(8,128)S(1)} %collective-permute-done.got.refs_1_, f32[784,128]{1,0:T(8,128)S(1)} %get-tuple-element.24.refs_2_.own, f32[3,16,128]{2,1,0:T(8,128)S(1)} %bitcast.7, ...), custom_call_target="tpu_custom_call" | custom-call | flops 352321536 | tf_op jit(solution)/shard_map/pallas_call | solution.py:37
  48.0 0.1 collective-permute-start.15
  48.1 1.7 %collective-permute-done.15.got = f32[768,128]{1,0:T(8,128)S(1)} collective-permute-done((f32[768,128]{1,0:T(8,128)S(1)}, f32[768,128]{1,0:T(8,128)S(1)}, u32[]{:S(2)}, u32[]{:S(2)}) %collective-permute-start.15) | collective-permute-done | bytes 393248 | tf_op jit(solution)/shard_map/ppermute | solution.py:376
  49.8 0.0 copy-done
  49.8 0.0 copy-done.1
  49.8 1.4 %shard_map.159 = f32[1,512,128]{2,1,0:T(8,128)} custom-call(f32[768,128]{1,0:T(8,128)S(1)} %get-tuple-element.33.keep, f32[768,128]{1,0:T(8,128)S(1)} %collective-permute-done.15.got, f32[1,128,128]{2,1,0:T(8,128)S(1)} %copy-done.1, f32[1,512,128]{2,1,0:T(8,128)S(1)} %copy-done), custom_call_target="tpu_custom_call" | custom-call | flops 125829120 | tf_op jit(solution)/shard_map/pallas_call | solution.py:37
  (7 shorter events, 0.0 us)
Async XLA Ops:
  0.0 13.6 %copy-start.2 = (f32[64,128]{1,0:T(8,128)S(1)}, f32[64,128]{1,0:T(8,128)}, u32[]{:S(2)}) copy-start(f32[64,128]{1,0:T(8,128)} %epair.1) | copy-start | bytes 98308
  0.0 13.6 %copy-start.5 = (f32[32,128]{1,0:T(8,128)S(1)}, f32[32,128]{1,0:T(8,128)}, u32[]{:S(2)}) copy-start(f32[32,128]{1,0:T(8,128)} %equad.1) | copy-start | bytes 49156
  2.6 16.7 %collective-permute-start.2 = (f32[784,128]{1,0:T(8,128)}, f32[784,128]{1,0:T(8,128)S(1)}, u32[]{:S(2)}, u32[]{:S(2)}) collective-permute-start(f32[784,128]{1,0:T(8,128)} %get-tuple-element.21.refs_2_), channel_id=1, source_target_pairs={{0,4},{1,5},{2,6},{3,7},{4,0},{5,1},{6,2},{7,3},{8,12},{9,13},{10,... | collective-permute-start | bytes 1204232 | tf_op jit(solution)/shard_map/ppermute | solution.py:376
  5.6 13.7 %collective-permute-start.1 = (f32[784,128]{1,0:T(8,128)}, f32[784,128]{1,0:T(8,128)S(1)}, u32[]{:S(2)}, u32[]{:S(2)}) collective-permute-start(f32[784,128]{1,0:T(8,128)} %get-tuple-element.21.refs_2_), channel_id=1, source_target_pairs={{0,2},{1,3},{2,0},{3,1},{4,6},{5,7},{6,4},{7,5},{8,10},{9,11},{10,... | collective-permute-start | bytes 1204232 | tf_op jit(solution)/shard_map/ppermute | solution.py:376
  7.1 14.5 %collective-permute-start.7 = (f32[784,128]{1,0:T(8,128)}, f32[784,128]{1,0:T(8,128)S(1)}, u32[]{:S(2)}, u32[]{:S(2)}) collective-permute-start(f32[784,128]{1,0:T(8,128)} %get-tuple-element.21.refs_2_), channel_id=1, source_target_pairs={{8,16},{9,17},{10,18},{11,19},{12,20},{13,21},{14,22},{15,23},{16,... | collective-permute-start | bytes 1204232 | tf_op jit(solution)/shard_map/ppermute | solution.py:376
  7.8 13.8 %collective-permute-start.6 = (f32[784,128]{1,0:T(8,128)}, f32[784,128]{1,0:T(8,128)S(1)}, u32[]{:S(2)}, u32[]{:S(2)}) collective-permute-start(f32[784,128]{1,0:T(8,128)} %get-tuple-element.21.refs_2_), channel_id=1, source_target_pairs={{0,8},{1,9},{2,10},{3,11},{4,12},{5,13},{6,14},{7,15},{8,0},{9,1},... | collective-permute-start | bytes 1204232 | tf_op jit(solution)/shard_map/ppermute | solution.py:376
  12.2 1.4 %collective-permute-start = (f32[80,128]{1,0:T(8,128)}, f32[80,128]{1,0:T(8,128)S(1)}, u32[]{:S(2)}, u32[]{:S(2)}) collective-permute-start(f32[80,128]{1,0:T(8,128)} %get-tuple-element.20), channel_id=1, source_target_pairs={{0,1},{1,0},{2,3},{3,2},{4,5},{5,4},{6,7},{7,6},{8,9},{9,8},{10,11... | collective-permute-start | bytes 122888 | tf_op jit(solution)/shard_map/ppermute | solution.py:376
  13.6 0.8 %copy-start.3 = (f32[64,128]{1,0:T(8,128)S(1)}, f32[64,128]{1,0:T(8,128)}, u32[]{:S(2)}) copy-start(f32[64,128]{1,0:T(8,128)} %get-tuple-element.22.keep) | copy-start | bytes 98308
  14.7 4.6 %collective-permute-start.3 = (f32[160,128]{1,0:T(8,128)S(1)}, f32[160,128]{1,0:T(8,128)S(1)}, u32[]{:S(2)}, u32[]{:S(2)}) collective-permute-start(f32[160,128]{1,0:T(8,128)S(1)} %get-tuple-element.23.refs_3_.refs_0_), channel_id=1, source_target_pairs={{0,2},{1,3},{2,0},{3,1},{4,6},{5,7},{6,4},{7,5},{8,10},{9,11},{10,... | collective-permute-start | bytes 245768 | tf_op jit(solution)/shard_map/ppermute | solution.py:376
  15.3 1.0 %copy-start.7 = (f32[784,128]{1,0:T(8,128)S(1)}, f32[784,128]{1,0:T(8,128)}, u32[]{:S(2)}) copy-start(f32[784,128]{1,0:T(8,128)} %get-tuple-element.21.refs_2_) | copy-start | bytes 1204228
  19.3 12.6 %collective-permute-start.4 = (f32[784,128]{1,0:T(8,128)S(1)}, f32[784,128]{1,0:T(8,128)S(1)}, u32[]{:S(2)}, u32[]{:S(2)}) collective-permute-start(f32[784,128]{1,0:T(8,128)S(1)} %shard_map.149.refs_3_), channel_id=1, source_target_pairs={{0,4},{1,3},{2,6},{3,1},{4,0},{5,7},{6,2},{7,5},{8,12},{9,11},{10,... | collective-permute-start | bytes 1204232 | tf_op jit(solution)/shard_map/ppermute | solution.py:376
  19.9 1.3 %collective-permute-start.8 = (f32[256,128]{1,0:T(8,128)S(1)}, f32[256,128]{1,0:T(8,128)S(1)}, u32[]{:S(2)}, u32[]{:S(2)}) collective-permute-start(f32[256,128]{1,0:T(8,128)S(1)} %shard_map.148.refs_3_.refs_1_), channel_id=1, source_target_pairs={{0,1},{1,0},{2,3},{3,2},{4,5},{5,4},{6,7},{7,6},{8,9},{9,8},{10,11... | collective-permute-start | bytes 393224 | tf_op jit(solution)/shard_map/ppermute | solution.py:376
  21.7 18.0 %collective-permute-start.10 = (f32[784,128]{1,0:T(8,128)S(1)}, f32[784,128]{1,0:T(8,128)S(1)}, u32[]{:S(2)}, u32[]{:S(2)}) collective-permute-start(f32[784,128]{1,0:T(8,128)S(1)} %get-tuple-element.29), channel_id=1, source_target_pairs={{0,4},{1,5},{2,6},{3,7},{4,0},{5,1},{6,2},{7,3},{8,12},{9,13},{10,... | collective-permute-start | bytes 1204232 | tf_op jit(solution)/shard_map/ppermute | solution.py:376
  23.3 16.4 %collective-permute-start.9 = (f32[784,128]{1,0:T(8,128)S(1)}, f32[784,128]{1,0:T(8,128)S(1)}, u32[]{:S(2)}, u32[]{:S(2)}) collective-permute-start(f32[784,128]{1,0:T(8,128)S(1)} %get-tuple-element.28.refs_6_), channel_id=1, source_target_pairs={{0,2},{1,3},{2,0},{3,1},{4,6},{5,7},{6,4},{7,5},{8,10},{9,11},{10,... | collective-permute-start | bytes 1204232 | tf_op jit(solution)/shard_map/ppermute | solution.py:376
  23.8 6.8 %collective-permute-start.13 = (f32[128,128]{1,0:T(8,128)S(1)}, f32[128,128]{1,0:T(8,128)S(1)}, u32[]{:S(2)}, u32[]{:S(2)}) collective-permute-start(f32[128,128]{1,0:T(8,128)S(1)} %get-tuple-element.27.refs_3_.refs_0_), channel_id=1, source_target_pairs={{0,24},{1,25},{2,26},{3,27},{4,28},{5,29},{6,30},{7,31},{8,16},{9,... | collective-permute-start | bytes 196616 | tf_op jit(solution)/shard_map/ppermute | solution.py:376
  27.4 9.8 %collective-permute-start.12 = (f32[128,128]{1,0:T(8,128)S(1)}, f32[128,128]{1,0:T(8,128)S(1)}, u32[]{:S(2)}, u32[]{:S(2)}) collective-permute-start(f32[128,128]{1,0:T(8,128)S(1)} %get-tuple-element.27.refs_3_.refs_0_), channel_id=1, source_target_pairs={{0,16},{1,17},{2,18},{3,19},{4,20},{5,21},{6,22},{7,23},{8,24},{9,... | collective-permute-start | bytes 196616 | tf_op jit(solution)/shard_map/ppermute | solution.py:376
  30.7 6.6 %collective-permute-start.11 = (f32[128,128]{1,0:T(8,128)S(1)}, f32[128,128]{1,0:T(8,128)S(1)}, u32[]{:S(2)}, u32[]{:S(2)}) collective-permute-start(f32[128,128]{1,0:T(8,128)S(1)} %get-tuple-element.27.refs_3_.refs_0_), channel_id=1, source_target_pairs={{0,8},{1,9},{2,10},{3,11},{4,12},{5,13},{6,14},{7,15},{8,0},{9,1},... | collective-permute-start | bytes 196616 | tf_op jit(solution)/shard_map/ppermute | solution.py:376
  32.0 11.2 %collective-permute-start.5 = (f32[784,128]{1,0:T(8,128)S(1)}, f32[784,128]{1,0:T(8,128)S(1)}, u32[]{:S(2)}, u32[]{:S(2)}) collective-permute-start(f32[784,128]{1,0:T(8,128)S(1)} %collective-permute-done.4.refs_3_.refs_2_), channel_id=1, source_target_pairs={{0,8},{1,9},{2,10},{3,11},{8,16},{9,17},{10,18},{11,19},{12,4},{13... | collective-permute-start | bytes 1204232 | tf_op jit(solution)/shard_map/ppermute | solution.py:376
  37.2 0.7 %copy-start.8 = (f32[8,3,128]{2,0,1:T(8,128)S(1)}, f32[8,3,128]{2,0,1:T(8,128)}, u32[]{:S(2)}) copy-start(f32[8,3,128]{2,0,1:T(8,128)} %param.23) | copy-start | bytes 36868
  37.2 0.7 %copy-start.9 = (f32[4,3,128]{2,0,1:T(4,128)S(1)}, f32[4,3,128]{2,0,1:T(4,128)}, u32[]{:S(2)}) copy-start(f32[4,3,128]{2,0,1:T(4,128)} %param.24) | copy-start | bytes 18436
  37.2 0.7 %copy-start.10 = (s32[8,8]{1,0:T(8,128)S(1)}, s32[8,8]{1,0:T(8,128)}, u32[]{:S(2)}) copy-start(s32[8,8]{1,0:T(8,128)} %refs_1_.3) | copy-start | bytes 772
  37.3 0.7 %copy-start.11 = (s32[4,8]{1,0:T(4,128)S(1)}, s32[4,8]{1,0:T(4,128)}, u32[]{:S(2)}) copy-start(s32[4,8]{1,0:T(4,128)} %refs_2_.3) | copy-start | bytes 388
  39.6 5.0 %collective-permute-start.14 = (f32[256,128]{1,0:T(8,128)S(1)}, f32[256,128]{1,0:T(8,128)S(1)}, u32[]{:S(2)}, u32[]{:S(2)}) collective-permute-start(f32[256,128]{1,0:T(8,128)S(1)} %get-tuple-element.32), channel_id=1, source_target_pairs={{0,4},{1,5},{2,6},{3,7},{4,0},{5,1},{6,2},{7,3},{8,12},{9,13},{10,... | collective-permute-start | bytes 393224 | tf_op jit(solution)/shard_map/ppermute | solution.py:376
  43.1 1.6 %copy-start.4 = (f32[16,3,128]{2,0,1:T(8,128)S(1)}, f32[16,3,128]{2,0,1:T(8,128)}, u32[]{:S(2)}) copy-start(f32[16,3,128]{2,0,1:T(8,128)} %param.22) | copy-start | bytes 73732
  44.6 0.7 %copy-start.6 = (s32[16,8]{0,1:T(8,128)S(1)}, s32[16,8]{0,1:T(8,128)}, u32[]{:S(2)}) copy-start(s32[16,8]{0,1:T(8,128)} %param.27) | copy-start | bytes 1540
  45.3 4.5 %copy-start = (f32[1,512,128]{2,1,0:T(8,128)S(1)}, f32[1,512,128]{2,1,0:T(8,128)}, u32[]{:S(2)}) copy-start(f32[1,512,128]{2,1,0:T(8,128)} %basis.1) | copy-start | bytes 786436
  45.3 4.5 %copy-start.1 = (f32[1,128,128]{2,1,0:T(8,128)S(1)}, f32[1,128,128]{2,1,0:T(8,128)}, u32[]{:S(2)}) copy-start(f32[1,128,128]{2,1,0:T(8,128)} %move.1) | copy-start | bytes 196612
  48.0 1.8 %collective-permute-start.15 = (f32[768,128]{1,0:T(8,128)S(1)}, f32[768,128]{1,0:T(8,128)S(1)}, u32[]{:S(2)}, u32[]{:S(2)}) collective-permute-start(f32[768,128]{1,0:T(8,128)S(1)} %get-tuple-element.34), channel_id=1, source_target_pairs={{0,1},{1,0},{2,3},{3,2},{4,5},{5,4},{6,7},{7,6},{8,9},{9,8},{10,11... | collective-permute-start | bytes 1179656 | tf_op jit(solution)/shard_map/ppermute | solution.py:376

commit v4 on v3

--- a/solution.py
+++ b/solution.py
@@ -72,6 +72,15 @@
     both = jnp.dot(high, values, preferred_element_type=jnp.float32)
     rest = jnp.dot(low, values[:, 0:128], preferred_element_type=jnp.float32)
     return both[:, 0:128] + (both[:, 128:256] + rest)
+
+
+def three_dot(a, b, contract=1):
+    (ah, al), (bh, bl) = split(a), split(b)
+
+    def one(x, y):
+        return lax.dot_general(x, y, (((contract,), (0,)), ((), ())), preferred_element_type=jnp.float32)
+
+    return one(ah, bh) + (one(ah, bl) + one(al, bh))
 
 
 def columns(rows):
@@ -152,8 +161,8 @@
     lists = [near_list[...].astype(jnp.float32), far_list[...].astype(jnp.float32), rest]
     pieces.append(jnp.concatenate(lists, axis=1))
     meta = jnp.concatenate(pieces, axis=0)
-    coef = dot_t(basis[0], vec[0])
-    up = dot_t(move[0], coef)
+    coef = three_dot(basis[0], vec[0], 0)
+    up = three_dot(move[0], coef, 0)
     ship[0:LEAF, :] = vec[0]
     ship[LEAF : LEAF + PACK, :] = jnp.concatenate([meta, coef, up], axis=0)
     low, high = up[:64], up[64:]
@@ -263,11 +272,24 @@
         out[...] = jnp.where(((place ^ m) < place) == plane_odd, even[...], odd[...])
 
 
+def fetch_kernel(*refs):
+    half = len(refs) // 2
+    for a, b in zip(refs[:half], refs[half:]):
+        b[...] = a[...]
+
+
 def way_kernel(idx, bx, by, out):
     out[...] = jnp.where(idx[0] % 2 == 0, bx[...], by[...])
 
 
-def close_kernel(idx, far_pair, got, own, skel_pair, total, ctx, quad_own, quad_got, *refs):
+def last_kernel(slots, idx, got, own, block, total_in, mine, share, total, *scratch):
+    total[...] = total_in[...]
+    add_near(idx[0], slots, [(block, block, LEAF)], ((own, LEAF), (got, 64)), total, scratch)
+    mine[...] = total[0:512, :]
+    share[...] = total[512:1024, :]
+
+
+def close_kernel(idx, far_pair, got, own, skel_pair, ctx, quad_own, quad_got, *refs):
     blocks = [(b, b, LEAF) for b in (own,) + refs[:8]]
     keep, share, low, *scratch = refs[8:]
     low[...] = jnp.zeros_like(low)
@@ -275,11 +297,9 @@
     local_top = quad_own[128:256, :] + quad_got[128:256, :]
     local_quad = quad_own[0:128, :] + quad_got[0:128, :] + dot(ctx[0:128, :], local_top)
     low[256:384, :] += dot(ctx[128:256, :], local_quad)
-    keep[0:512, :] = total[0:512, :]
-    keep[512:640, :] = low[0:128, :]
-    keep[640:768, :] = low[256:384, :]
-    share[0:512, :] = total[512:1024, :]
-    share[512:768, :] = low[128:384, :]
+    keep[0:128, :] = low[0:128, :]
+    keep[128:256, :] = low[256:384, :]
+    share[...] = low[128:384, :]
 
 
 def rise_kernel(keep, got, epair, equad, out, moved):
@@ -313,14 +333,15 @@
     send[64:128, :] = top[pl.ds(half, 64), :]
 
 
-def upper_kernel(idx, far_quad, far_top, planes, skel_quad, skel_top, mine, send, high, low, values, rows):
+def upper_kernel(idx, far_quad, far_top, two, others, skel_quad, skel_top, mine, send, high, low, values, rows):
     device = idx[0]
     half = pl.multiple_of((device % 2) * 64, 64)
     plane = device // 8
     quad = device // 4
     rows[...] = jnp.zeros_like(rows)
     for j in range(4):
-        rows[pl.ds(128 * j + half, 64), :] = planes[128 * j + 64 : 128 * (j + 1), :]
+        at = 128 * (j % 2)
+        rows[pl.ds(128 * j + half, 64), :] = (two, others)[j // 2][at + 64 : at + 128, :]
     put_values(values, slice(0, 512), rows[...])
     bits = window_bits(lambda e: far_top[plane, e], FAR_SLOTS, 0)
     cols = own_columns(skeleton(skel_top, plane))
@@ -333,7 +354,8 @@
     mine[128:256, :] = top
     send[128:256, :] = top
     for j in range(4):
-        rows[pl.ds(128 * j + half, 64), :] = planes[128 * j : 128 * j + 64, :]
+        at = 128 * (j % 2)
+        rows[pl.ds(128 * j + half, 64), :] = (two, others)[j // 2][at : at + 64, :]
     put_values(values, slice(0, 512), rows[...])
     for s in range(2):
         target = quad ^ s
@@ -349,10 +371,10 @@
     send[0:128, :] = far[128:256]
 
 
-def final_kernel(keep, got, move, basis, out):
-    local_pair = keep[640:768, :] + got[640:768, :]
-    local = keep[512:640, :] + got[512:640, :] + dot(move[0], local_pair)
-    out[0] = keep[0:512, :] + got[0:512, :] + dot(basis[0], local)
+def final_kernel(near, near_got, low, low_got, move, basis, out):
+    local_pair = low[128:256, :] + low_got[128:256, :]
+    local = low[0:128, :] + low_got[0:128, :] + dot(move[0], local_pair)
+    out[0] = near[...] + near_got[...] + three_dot(basis[0], local)
 
 
 def near_scratch():
@@ -467,7 +489,10 @@
         scratch=near_scratch() + [pltpu.SemaphoreType.DMA],
         flops=2 * NEAR_FLOPS,
     )
-    half = call(quad_kernel, f32(256, 128), [rise, rise_x, epair], after=[total])
+    lists = [far_pair.T, far_quad, far_top] + [a.transpose(1, 0, 2) for a in (skel_pair, skel_quad, skel_top)]
+    fetched = call(fetch_kernel, tuple(jax.ShapeDtypeStruct(a.shape, a.dtype) for a in lists), lists, after=[total])
+    far_pair_t, far_quad_v, far_top_v, skel_pair_t, *skels = fetched
+    half = call(quad_kernel, f32(256, 128), [rise, rise_x, epair], after=[fetched[0]])
     way = call(way_kernel, f32(LEAF + PACK, 128), [idx, bx, by], n_smem=1, after=[half])
     bd = permute(way, lambda i: i ^ 4 if i % 2 == 0 else i ^ 2)
 
@@ -482,20 +507,21 @@
         flops=2 * 6 * 128**3,
     )
     direct = n == 4 * PLANE
-    received = [swap(shared, PLANE * m) for m in (3, 2, 1)][::-1] if direct else []
     block = f32(LEAF + PACK, 128)
-    sx, sy = call(cross_kernel, (block,) * 2, [idx, be, bo], n_smem=1, after=[shared])
+    total = near((1, 2), [bx, by], total, [shared])
+    if direct:
+        two = call(stack_kernel, f32(256, 128), [shared, swap(shared, PLANE)], after=[total])
+    else:
+        two = total
+    sx, sy = call(cross_kernel, (block,) * 2, [idx, be, bo], n_smem=1, after=[two])
     cx, cy = swap(sx, 2), swap(sy, 4)
     cd = permute(bd, lambda i: i + 8 if i // 2 % 4 < 2 else i - 8)
-    total = near((1, 2), [bx, by], total, [sx])
-    total = near((4, 5), [be, bo], total, [])
-    planes = call(stack_kernel, f32(512, 128), [shared, *received], after=[total]) if direct else shared
+    total = near((4, 5), [be, bo], total, [sx])
     if direct:
-        skels = [skel_quad.transpose(1, 0, 2), skel_top.transpose(1, 0, 2)]
         quad_own, quad_send = call(
             upper_kernel,
             (f32(256, 128), f32(256, 128)),
-            [idx, far_quad, far_top, planes, *skels],
+            [idx, far_quad_v, far_top_v, two, swap(two, 2 * PLANE), *skels],
             n_smem=3,
             after=[total],
             scratch=far_scratch(256, 4) + [pltpu.VMEM((512, 128), jnp.float32)],
@@ -505,22 +531,30 @@
     else:
         quad_own = upper_anywhere(device, shared, ctx, far_quad, far_top, skel_quad, skel_top)
         quad_got = jnp.zeros_like(quad_own)
-    far_pair_t, skel_pair_t = far_pair.T, skel_pair.transpose(1, 0, 2)
     total = near((3, 6, 7), [bd, cx, cy], total, [quad_own])
-    total = near((8,), [cd], total, [])
-    keep, share = call(
+    mine, share = call(
+        functools.partial(last_kernel, (8,)),
+        (f32(512, 128), f32(512, 128)),
+        [idx, got, own, cd, total],
+        n_smem=1,
+        scratch=[pltpu.VMEM((1024, 128), jnp.float32)] + near_scratch(),
+        flops=2 * NEAR_FLOPS,
+    )
+    near_got = swap(share, 1)
+    low, low_share = call(
         close_kernel,
-        (f32(768, 128), f32(768, 128)),
-        [idx, far_pair_t, got, own, skel_pair_t, total, ctx, quad_own, quad_got]
+        (f32(256, 128), f32(256, 128)),
+        [idx, far_pair_t, got, own, skel_pair_t, ctx, quad_own, quad_got]
         + [bx, by, bd, be, bo, cx, cy, cd],
         n_smem=2,
+        after=[share],
         scratch=[pltpu.VMEM((384, 128), jnp.float32)] + far_scratch(256, 9),
         flops=2 * 3 * 28 * 128**3,
     )
     return call(
         final_kernel,
         f32(1, 512, 128),
-        [keep, swap(share, 1), transfer_leaf, leaf_basis],
+        [mine, near_got, low, swap(low_share, 1), transfer_leaf, leaf_basis],
         flops=2 * 6 * 640 * 128 * 128,
     )
 

time: 51.5 us -> 49.2 us (0.955)
  the two profiles are of different devices: /device:TPU:0 before, /device:TPU:17 now
where the time goes in v4:
time: 49.2 us; the launch traced here: 48.9 us
  Pallas kernels  20 us (41%)
  starting transfers between devices  19.3 us (39%)
  waiting for transfers between devices  6.92 us (14%)
  local copies, waits for them, and re-layouts  2.42 us (5%)
    pallas_call x16, Pallas kernels, call(): pl.pallas_call(ordered if after else body, out_shape=outs, in_specs=[SMEM...  20 us
    ppermute x16, starting transfers between devices, permute(): lax.ppermute(value, AXIS, [(i, j) for i, j in pairs if 0 <= j < n and i !...  19.3 us
    ppermute x16, waiting for transfers between devices, permute(): lax.ppermute(value, AXIS, [(i, j) for i, j in pairs if 0 <= j < n and i !...  6.92 us
    unnamed x24, local copies, waits for them, and re-layouts  2.42 us
  transfers between devices with their start and end apart: 16, of which 3 were waited for; matrix products, arithmetic and copies ran while one was open for 0% of the time, Pallas kernels for 34%

profile of v4, /device:TPU:17, one launch (start us, length us, event | category | flops | bytes accessed | tf_op | source)
XLA Modules:
  0.0 48.9 jit_solution(14097759411731390196)
XLA Ops:
  0.0 0.0 copy-start.5
  0.0 2.4 %shard_map.145 = (f32[784,128]{1,0:T(8,128)}, f32[64,128]{1,0:T(8,128)}, f32[80,128]{1,0:T(8,128)}) custom-call(s32[1]{0:T(128)} %bitcast.idx.refs_0_, f32[1,512,128]{2,1,0:T(8,128)} %refs_0_.1, f32[1,512,128]{2,1,0:T(8,128)} %basis.1, f32[1,128,128]{2,1,0:T(8,128)} %move.1, f32[3,1,512]{2,1,0:T(1,128)} %bitcast.11, f32[3,1,128]{2,1,0:T(1,128)} %bitcast.12, ...), custom_call_target="tpu_custom_call" | custom-call | flops 125829120 | bytes 1048576 | tf_op jit(solution)/shard_map/pallas_call | solution.py:37
  2.4 1.3 %collective-permute-start.1 = (f32[784,128]{1,0:T(8,128)}, f32[784,128]{1,0:T(8,128)S(1)}, u32[]{:S(2)}, u32[]{:S(2)}) collective-permute-start(f32[784,128]{1,0:T(8,128)} %get-tuple-element.29.refs_2_), channel_id=1, source_target_pairs={{0,2},{1,3},{2,0},{3,1},{4,6},{5,7},{6,4},{7,5},{8,10},{9,11},{10,... | collective-permute-start | bytes 1204232 | tf_op jit(solution)/shard_map/ppermute | solution.py:398
  3.7 1.2 %collective-permute-start.2 = (f32[784,128]{1,0:T(8,128)}, f32[784,128]{1,0:T(8,128)S(1)}, u32[]{:S(2)}, u32[]{:S(2)}) collective-permute-start(f32[784,128]{1,0:T(8,128)} %get-tuple-element.29.refs_2_), channel_id=1, source_target_pairs={{0,4},{1,5},{2,6},{3,7},{4,0},{5,1},{6,2},{7,3},{8,12},{9,13},{10,... | collective-permute-start | bytes 1204232 | tf_op jit(solution)/shard_map/ppermute | solution.py:398
  4.9 1.2 %collective-permute-start = (f32[80,128]{1,0:T(8,128)}, f32[80,128]{1,0:T(8,128)S(1)}, u32[]{:S(2)}, u32[]{:S(2)}) collective-permute-start(f32[80,128]{1,0:T(8,128)} %get-tuple-element.28), channel_id=1, source_target_pairs={{0,1},{1,0},{2,3},{3,2},{4,5},{5,4},{6,7},{7,6},{8,9},{9,8},{10,11... | collective-permute-start | bytes 122888 | tf_op jit(solution)/shard_map/ppermute | solution.py:398
  6.1 1.3 %collective-permute-start.6 = (f32[784,128]{1,0:T(8,128)}, f32[784,128]{1,0:T(8,128)S(1)}, u32[]{:S(2)}, u32[]{:S(2)}) collective-permute-start(f32[784,128]{1,0:T(8,128)} %get-tuple-element.29.refs_2_), channel_id=1, source_target_pairs={{0,8},{1,9},{2,10},{3,11},{4,12},{5,13},{6,14},{7,15},{8,0},{9,1},... | collective-permute-start | bytes 1204232 | tf_op jit(solution)/shard_map/ppermute | solution.py:398
  7.4 1.9 %collective-permute-start.7 = (f32[784,128]{1,0:T(8,128)}, f32[784,128]{1,0:T(8,128)S(1)}, u32[]{:S(2)}, u32[]{:S(2)}) collective-permute-start(f32[784,128]{1,0:T(8,128)} %get-tuple-element.29.refs_2_), channel_id=1, source_target_pairs={{8,16},{9,17},{10,18},{11,19},{12,20},{13,21},{14,22},{15,23},{16,... | collective-permute-start | bytes 1204232 | tf_op jit(solution)/shard_map/ppermute | solution.py:398
  9.3 0.0 collective-permute-done.got.refs_1_.refs_2_
  9.4 0.0 copy-done.2
  9.4 0.0 copy-done.5
  9.4 0.0 copy-start.3
  9.4 0.7 %copy-done.3 = f32[64,128]{1,0:T(8,128)S(1)} copy-done((f32[64,128]{1,0:T(8,128)S(1)}, f32[64,128]{1,0:T(8,128)}, u32[]{:S(2)}) %copy-start.3) | copy-done | bytes 32792
  10.1 0.3 shard_map.146
  10.4 0.3 collective-permute-start.3
  10.7 0.0 copy-start.11
  10.7 1.0 %copy-done.11 = f32[784,128]{1,0:T(8,128)S(1)} copy-done((f32[784,128]{1,0:T(8,128)S(1)}, f32[784,128]{1,0:T(8,128)}, u32[]{:S(2)}) %copy-start.11) | copy-done | bytes 401432
  11.7 0.0 copy-start.4
  11.7 0.0 copy-start.6
  11.7 1.7 %shard_map.147 = (f32[1024,128]{1,0:T(8,128)S(1)}, f32[784,128]{1,0:T(8,128)S(1)}) custom-call(s32[1]{0:T(128)} %bitcast.idx.refs_0_, f32[80,128]{1,0:T(8,128)S(1)} %collective-permute-done.got.refs_1_.refs_2_, f32[784,128]{1,0:T(8,128)S(1)} %copy-done.11, f32[160,128]{1,0:T(8,128)S(1)} %get-tuple-element.31.refs_3_.refs_0_), custom_call_target="tpu_custom_call" | custom-call | flops 805306368 | tf_op jit(solution)/shard_map/pallas_call | solution.py:37
  13.4 0.0 copy-start.7
  13.4 0.0 copy-start.10
  13.4 0.0 copy-done.4
  13.4 0.0 copy-done.6
  13.4 0.0 copy-done.8
  13.5 0.0 copy-done.9
  13.5 0.6 %copy-done.7 = f32[4,3,128]{2,0,1:T(4,128)S(1)} copy-done((f32[4,3,128]{2,0,1:T(4,128)S(1)}, f32[4,3,128]{2,0,1:T(4,128)}, u32[]{:S(2)}) %copy-start.7) | copy-done | bytes 6168
  14.1 0.0 copy-done.10
  14.1 0.9 %collective-permute-done.3.refs_1_ = f32[160,128]{1,0:T(8,128)S(1)} collective-permute-done((f32[160,128]{1,0:T(8,128)S(1)}, f32[160,128]{1,0:T(8,128)S(1)}, u32[]{:S(2)}, u32[]{:S(2)}) %collective-permute-start.3) | collective-permute-done | bytes 81952 | tf_op jit(solution)/shard_map/ppermute | solution.py:398
  15.0 1.2 %collective-permute-start.8 = (f32[256,128]{1,0:T(8,128)S(1)}, f32[256,128]{1,0:T(8,128)S(1)}, u32[]{:S(2)}, u32[]{:S(2)}) collective-permute-start(f32[256,128]{1,0:T(8,128)S(1)} %shard_map.149.refs_3_.refs_1_), channel_id=1, source_target_pairs={{0,1},{1,0},{2,3},{3,2},{4,5},{5,4},{6,7},{7,6},{8,9},{9,8},{10,11... | collective-permute-start | bytes 393224 | tf_op jit(solution)/shard_map/ppermute | solution.py:398
  16.2 0.0 collective-permute-done.1.refs_1_.refs_3_.refs_8_
  16.2 0.0 collective-permute-done.2.refs_2_.refs_4_.refs_9_
  16.2 0.1 shard_map.150.refs_3_
  16.3 1.3 %collective-permute-start.4 = (f32[784,128]{1,0:T(8,128)S(1)}, f32[784,128]{1,0:T(8,128)S(1)}, u32[]{:S(2)}, u32[]{:S(2)}) collective-permute-start(f32[784,128]{1,0:T(8,128)S(1)} %shard_map.150.refs_3_), channel_id=1, source_target_pairs={{0,4},{1,3},{2,6},{3,1},{4,0},{5,7},{6,2},{7,5},{8,12},{9,11},{10,... | collective-permute-start | bytes 1204232 | tf_op jit(solution)/shard_map/ppermute | solution.py:398
  17.5 0.0 collective-permute-done.8.refs_2_
  17.5 0.3 shard_map.151
  17.8 1.4 %collective-permute-start.9 = (f32[128,128]{1,0:T(8,128)S(1)}, f32[128,128]{1,0:T(8,128)S(1)}, u32[]{:S(2)}, u32[]{:S(2)}) collective-permute-start(f32[128,128]{1,0:T(8,128)S(1)} %get-tuple-element.36.refs_6_.refs_0_), channel_id=1, source_target_pairs={{0,8},{1,9},{2,10},{3,11},{4,12},{5,13},{6,14},{7,15},{8,0},{9,1},... | collective-permute-start | bytes 196616 | tf_op jit(solution)/shard_map/ppermute | solution.py:398
  19.2 2.4 %shard_map.152.refs_2_.refs_5_ = f32[1024,128]{1,0:T(8,128)S(1)} custom-call(s32[1]{0:T(128)} %bitcast.idx.refs_0_, f32[80,128]{1,0:T(8,128)S(1)} %collective-permute-done.got.refs_1_.refs_2_, f32[784,128]{1,0:T(8,128)S(1)} %get-tuple-element.32.refs_2_.own.refs_3_, f32[784,128]{1,0:T(8,128)S(1)} %collective-permute-done.1.refs_1_.refs_3_.refs_8_, ...), custom_call_target="tpu_custom_call" | custom-call | flops 1610612736 | tf_op jit(solution)/shard_map/pallas_call | solution.py:37
  21.6 0.0 collective-permute-done.9.refs_1_
  21.6 0.0 collective-permute-done.6.refs_1_.refs_3_.refs_11_
  21.6 0.0 collective-permute-done.7.refs_2_.refs_4_.refs_12_
  21.6 0.1 shard_map.154
  21.7 0.9 %collective-permute-start.10 = (f32[784,128]{1,0:T(8,128)S(1)}, f32[784,128]{1,0:T(8,128)S(1)}, u32[]{:S(2)}, u32[]{:S(2)}) collective-permute-start(f32[784,128]{1,0:T(8,128)S(1)} %get-tuple-element.37.refs_6_), channel_id=1, source_target_pairs={{0,2},{1,3},{2,0},{3,1},{4,6},{5,7},{6,4},{7,5},{8,10},{9,11},{10,... | collective-permute-start | bytes 1204232 | tf_op jit(solution)/shard_map/ppermute | solution.py:398
  22.7 1.2 %collective-permute-start.11 = (f32[784,128]{1,0:T(8,128)S(1)}, f32[784,128]{1,0:T(8,128)S(1)}, u32[]{:S(2)}, u32[]{:S(2)}) collective-permute-start(f32[784,128]{1,0:T(8,128)S(1)} %get-tuple-element.38), channel_id=1, source_target_pairs={{0,4},{1,5},{2,6},{3,7},{4,0},{5,1},{6,2},{7,3},{8,12},{9,13},{10,... | collective-permute-start | bytes 1204232 | tf_op jit(solution)/shard_map/ppermute | solution.py:398
  23.9 0.1 collective-permute-start.12
  24.0 0.0 collective-permute-done.4.refs_3_.refs_10_
  24.0 3.1 %collective-permute-start.5 = (f32[784,128]{1,0:T(8,128)S(1)}, f32[784,128]{1,0:T(8,128)S(1)}, u32[]{:S(2)}, u32[]{:S(2)}) collective-permute-start(f32[784,128]{1,0:T(8,128)S(1)} %collective-permute-done.4.refs_3_.refs_10_), channel_id=1, source_target_pairs={{0,8},{1,9},{2,10},{3,11},{8,16},{9,17},{10,18},{11,19},{12,4},{13... | collective-permute-start | bytes 1204232 | tf_op jit(solution)/shard_map/ppermute | solution.py:398
  27.1 2.4 %shard_map.155.refs_7_.refs_6_ = f32[1024,128]{1,0:T(8,128)S(1)} custom-call(s32[1]{0:T(128)} %bitcast.idx.refs_0_, f32[80,128]{1,0:T(8,128)S(1)} %collective-permute-done.got.refs_1_.refs_2_, f32[784,128]{1,0:T(8,128)S(1)} %get-tuple-element.32.refs_2_.own.refs_3_, f32[784,128]{1,0:T(8,128)S(1)} %collective-permute-done.6.refs_1_.refs_3_.refs_11_, ...), custom_call_target="tpu_custom_call" | custom-call | flops 1610612736 | tf_op jit(solution)/shard_map/pallas_call | solution.py:37
  29.5 0.0 collective-permute-done.12.refs_4_
  29.5 1.7 %shard_map.156 = (f32[256,128]{1,0:T(8,128)S(1)}, f32[256,128]{1,0:T(8,128)S(1)}) custom-call(s32[1]{0:T(128)} %bitcast.idx.refs_0_, s32[8,8]{1,0:T(8,128)S(1)} %get-tuple-element.39.refs_1_, s32[4,8]{1,0:T(4,128)S(1)} %get-tuple-element.40.refs_2_, f32[256,128]{1,0:T(8,128)S(1)} %shard_map.153.refs_3_, f32[256,128]{1,0:T(8,128)S(1)} %collective-permute-done.12.refs_4_, ...), custom_call_target="tpu_custom_call" | custom-call | flops 301989888 | tf_op jit(solution)/shard_map/pallas_call | solution.py:37
  31.2 1.4 %collective-permute-start.14 = (f32[256,128]{1,0:T(8,128)S(1)}, f32[256,128]{1,0:T(8,128)S(1)}, u32[]{:S(2)}, u32[]{:S(2)}) collective-permute-start(f32[256,128]{1,0:T(8,128)S(1)} %get-tuple-element.48), channel_id=1, source_target_pairs={{0,4},{1,5},{2,6},{3,7},{4,0},{5,1},{6,2},{7,3},{8,12},{9,13},{10,... | collective-permute-start | bytes 393224 | tf_op jit(solution)/shard_map/ppermute | solution.py:398
  32.6 0.0 collective-permute-done.10.refs_4_.refs_13_
  32.6 0.0 collective-permute-done.11.refs_5_.refs_14_
  32.6 3.4 %shard_map.157.total_in = f32[1024,128]{1,0:T(8,128)S(1)} custom-call(s32[1]{0:T(128)} %bitcast.idx.refs_0_, f32[80,128]{1,0:T(8,128)S(1)} %collective-permute-done.got.refs_1_.refs_2_, f32[784,128]{1,0:T(8,128)S(1)} %get-tuple-element.32.refs_2_.own.refs_3_, f32[784,128]{1,0:T(8,128)S(1)} %collective-permute-done.4.refs_3_.refs_10_, ...), custom_call_target="tpu_custom_call" | custom-call | flops 2415919104 | tf_op jit(solution)/shard_map/pallas_call | solution.py:37
  36.0 4.7 %collective-permute-done.5.block.refs_15_ = f32[784,128]{1,0:T(8,128)S(1)} collective-permute-done((f32[784,128]{1,0:T(8,128)S(1)}, f32[784,128]{1,0:T(8,128)S(1)}, u32[]{:S(2)}, u32[]{:S(2)}) %collective-permute-start.5) | collective-permute-done | bytes 401440 | tf_op jit(solution)/shard_map/ppermute | solution.py:398
  40.7 1.4 %shard_map.158 = (f32[512,128]{1,0:T(8,128)S(1)}, f32[512,128]{1,0:T(8,128)S(1)}) custom-call(s32[1]{0:T(128)} %bitcast.idx.refs_0_, f32[80,128]{1,0:T(8,128)S(1)} %collective-permute-done.got.refs_1_.refs_2_, f32[784,128]{1,0:T(8,128)S(1)} %get-tuple-element.32.refs_2_.own.refs_3_, f32[784,128]{1,0:T(8,128)S(1)} %collective-permute-done.5.block.refs_15_, ...), custom_call_target="tpu_custom_call" | custom-call | flops 805306368 | tf_op jit(solution)/shard_map/pallas_call | solution.py:37
  42.1 1.3 %collective-permute-start.13 = (f32[512,128]{1,0:T(8,128)S(1)}, f32[512,128]{1,0:T(8,128)S(1)}, u32[]{:S(2)}, u32[]{:S(2)}) collective-permute-start(f32[512,128]{1,0:T(8,128)S(1)} %get-tuple-element.45.refs_16_), channel_id=1, source_target_pairs={{0,1},{1,0},{2,3},{3,2},{4,5},{5,4},{6,7},{7,6},{8,9},{9,8},{10,11... | collective-permute-start | bytes 786440 | tf_op jit(solution)/shard_map/ppermute | solution.py:398
  43.4 0.0 collective-permute-done.14.refs_7_
  43.5 2.8 %shard_map.159 = (f32[256,128]{1,0:T(8,128)S(1)}, f32[256,128]{1,0:T(8,128)S(1)}) custom-call(s32[1]{0:T(128)} %bitcast.idx.refs_0_, s32[8,16]{1,0:T(8,128)S(1)} %get-tuple-element.35.refs_3_.refs_1_, f32[80,128]{1,0:T(8,128)S(1)} %collective-permute-done.got.refs_1_.refs_2_, f32[784,128]{1,0:T(8,128)S(1)} %get-tuple-element.32.refs_2_.own.refs_3_, ...), custom_call_target="tpu_custom_call" | custom-call | flops 352321536 | tf_op jit(solution)/shard_map/pallas_call | solution.py:37
  46.2 0.1 collective-permute-start.15
  46.3 1.3 %collective-permute-done.15.low_got = f32[256,128]{1,0:T(8,128)S(1)} collective-permute-done((f32[256,128]{1,0:T(8,128)S(1)}, f32[256,128]{1,0:T(8,128)S(1)}, u32[]{:S(2)}, u32[]{:S(2)}) %collective-permute-start.15) | collective-permute-done | bytes 131104 | tf_op jit(solution)/shard_map/ppermute | solution.py:398
  47.6 0.0 collective-permute-done.13.near_got
  47.6 0.0 copy-done
  47.6 0.0 copy-done.1
  47.6 1.2 %shard_map.160 = f32[1,512,128]{2,1,0:T(8,128)} custom-call(f32[512,128]{1,0:T(8,128)S(1)} %get-tuple-element.44.near, f32[512,128]{1,0:T(8,128)S(1)} %collective-permute-done.13.near_got, f32[256,128]{1,0:T(8,128)S(1)} %get-tuple-element.49.low, f32[256,128]{1,0:T(8,128)S(1)} %collective-permute-done.15.low_got, f32[1,128,128]{2,1,0:T(8,128)S(1)} %copy-done.1, ...), custom_call_target="tpu_custom_call" | custom-call | flops 125829120 | tf_op jit(solution)/shard_map/pallas_call | solution.py:37
  (8 shorter events, 0.0 us)
Async XLA Ops:
  0.0 9.4 %copy-start.2 = (f32[64,128]{1,0:T(8,128)S(1)}, f32[64,128]{1,0:T(8,128)}, u32[]{:S(2)}) copy-start(f32[64,128]{1,0:T(8,128)} %epair.1) | copy-start | bytes 98308
  0.0 9.4 %copy-start.5 = (f32[32,128]{1,0:T(8,128)S(1)}, f32[32,128]{1,0:T(8,128)}, u32[]{:S(2)}) copy-start(f32[32,128]{1,0:T(8,128)} %equad.1) | copy-start | bytes 49156
  2.4 13.8 %collective-permute-start.1 = (f32[784,128]{1,0:T(8,128)}, f32[784,128]{1,0:T(8,128)S(1)}, u32[]{:S(2)}, u32[]{:S(2)}) collective-permute-start(f32[784,128]{1,0:T(8,128)} %get-tuple-element.29.refs_2_), channel_id=1, source_target_pairs={{0,2},{1,3},{2,0},{3,1},{4,6},{5,7},{6,4},{7,5},{8,10},{9,11},{10,... | collective-permute-start | bytes 1204232 | tf_op jit(solution)/shard_map/ppermute | solution.py:398
  3.7 12.5 %collective-permute-start.2 = (f32[784,128]{1,0:T(8,128)}, f32[784,128]{1,0:T(8,128)S(1)}, u32[]{:S(2)}, u32[]{:S(2)}) collective-permute-start(f32[784,128]{1,0:T(8,128)} %get-tuple-element.29.refs_2_), channel_id=1, source_target_pairs={{0,4},{1,5},{2,6},{3,7},{4,0},{5,1},{6,2},{7,3},{8,12},{9,13},{10,... | collective-permute-start | bytes 1204232 | tf_op jit(solution)/shard_map/ppermute | solution.py:398
  4.9 4.5 %collective-permute-start = (f32[80,128]{1,0:T(8,128)}, f32[80,128]{1,0:T(8,128)S(1)}, u32[]{:S(2)}, u32[]{:S(2)}) collective-permute-start(f32[80,128]{1,0:T(8,128)} %get-tuple-element.28), channel_id=1, source_target_pairs={{0,1},{1,0},{2,3},{3,2},{4,5},{5,4},{6,7},{7,6},{8,9},{9,8},{10,11... | collective-permute-start | bytes 122888 | tf_op jit(solution)/shard_map/ppermute | solution.py:398
  6.1 15.5 %collective-permute-start.6 = (f32[784,128]{1,0:T(8,128)}, f32[784,128]{1,0:T(8,128)S(1)}, u32[]{:S(2)}, u32[]{:S(2)}) collective-permute-start(f32[784,128]{1,0:T(8,128)} %get-tuple-element.29.refs_2_), channel_id=1, source_target_pairs={{0,8},{1,9},{2,10},{3,11},{4,12},{5,13},{6,14},{7,15},{8,0},{9,1},... | collective-permute-start | bytes 1204232 | tf_op jit(solution)/shard_map/ppermute | solution.py:398
  7.4 14.2 %collective-permute-start.7 = (f32[784,128]{1,0:T(8,128)}, f32[784,128]{1,0:T(8,128)S(1)}, u32[]{:S(2)}, u32[]{:S(2)}) collective-permute-start(f32[784,128]{1,0:T(8,128)} %get-tuple-element.29.refs_2_), channel_id=1, source_target_pairs={{8,16},{9,17},{10,18},{11,19},{12,20},{13,21},{14,22},{15,23},{16,... | collective-permute-start | bytes 1204232 | tf_op jit(solution)/shard_map/ppermute | solution.py:398
  9.4 0.8 %copy-start.3 = (f32[64,128]{1,0:T(8,128)S(1)}, f32[64,128]{1,0:T(8,128)}, u32[]{:S(2)}) copy-start(f32[64,128]{1,0:T(8,128)} %get-tuple-element.30.keep) | copy-start | bytes 98308
  10.4 4.6 %collective-permute-start.3 = (f32[160,128]{1,0:T(8,128)S(1)}, f32[160,128]{1,0:T(8,128)S(1)}, u32[]{:S(2)}, u32[]{:S(2)}) collective-permute-start(f32[160,128]{1,0:T(8,128)S(1)} %get-tuple-element.31.refs_3_.refs_0_), channel_id=1, source_target_pairs={{0,2},{1,3},{2,0},{3,1},{4,6},{5,7},{6,4},{7,5},{8,10},{9,11},{10,... | collective-permute-start | bytes 245768 | tf_op jit(solution)/shard_map/ppermute | solution.py:398
  10.7 1.0 %copy-start.11 = (f32[784,128]{1,0:T(8,128)S(1)}, f32[784,128]{1,0:T(8,128)}, u32[]{:S(2)}) copy-start(f32[784,128]{1,0:T(8,128)} %get-tuple-element.29.refs_2_) | copy-start | bytes 1204228
  11.7 1.7 %copy-start.4 = (f32[16,3,128]{2,0,1:T(8,128)S(1)}, f32[16,3,128]{2,0,1:T(8,128)}, u32[]{:S(2)}) copy-start(f32[16,3,128]{2,0,1:T(8,128)} %param.22) | copy-start | bytes 73732
  11.7 1.7 %copy-start.6 = (f32[8,3,128]{2,0,1:T(8,128)S(1)}, f32[8,3,128]{2,0,1:T(8,128)}, u32[]{:S(2)}) copy-start(f32[8,3,128]{2,0,1:T(8,128)} %param.23) | copy-start | bytes 36868
  11.7 1.7 %copy-start.8 = (s32[16,8]{0,1:T(8,128)S(1)}, s32[16,8]{0,1:T(8,128)}, u32[]{:S(2)}) copy-start(s32[16,8]{0,1:T(8,128)} %param.27) | copy-start | bytes 1540
  11.7 1.7 %copy-start.9 = (s32[8,8]{1,0:T(8,128)S(1)}, s32[8,8]{1,0:T(8,128)}, u32[]{:S(2)}) copy-start(s32[8,8]{1,0:T(8,128)} %refs_1_.3) | copy-start | bytes 772
  13.4 0.7 %copy-start.7 = (f32[4,3,128]{2,0,1:T(4,128)S(1)}, f32[4,3,128]{2,0,1:T(4,128)}, u32[]{:S(2)}) copy-start(f32[4,3,128]{2,0,1:T(4,128)} %param.24) | copy-start | bytes 18436
  13.4 0.7 %copy-start.10 = (s32[4,8]{1,0:T(4,128)S(1)}, s32[4,8]{1,0:T(4,128)}, u32[]{:S(2)}) copy-start(s32[4,8]{1,0:T(4,128)} %refs_2_.3) | copy-start | bytes 388
  15.0 2.5 %collective-permute-start.8 = (f32[256,128]{1,0:T(8,128)S(1)}, f32[256,128]{1,0:T(8,128)S(1)}, u32[]{:S(2)}, u32[]{:S(2)}) collective-permute-start(f32[256,128]{1,0:T(8,128)S(1)} %shard_map.149.refs_3_.refs_1_), channel_id=1, source_target_pairs={{0,1},{1,0},{2,3},{3,2},{4,5},{5,4},{6,7},{7,6},{8,9},{9,8},{10,11... | collective-permute-start | bytes 393224 | tf_op jit(solution)/shard_map/ppermute | solution.py:398
  16.3 7.7 %collective-permute-start.4 = (f32[784,128]{1,0:T(8,128)S(1)}, f32[784,128]{1,0:T(8,128)S(1)}, u32[]{:S(2)}, u32[]{:S(2)}) collective-permute-start(f32[784,128]{1,0:T(8,128)S(1)} %shard_map.150.refs_3_), channel_id=1, source_target_pairs={{0,4},{1,3},{2,6},{3,1},{4,0},{5,7},{6,2},{7,5},{8,12},{9,11},{10,... | collective-permute-start | bytes 1204232 | tf_op jit(solution)/shard_map/ppermute | solution.py:398
  17.8 3.7 %collective-permute-start.9 = (f32[128,128]{1,0:T(8,128)S(1)}, f32[128,128]{1,0:T(8,128)S(1)}, u32[]{:S(2)}, u32[]{:S(2)}) collective-permute-start(f32[128,128]{1,0:T(8,128)S(1)} %get-tuple-element.36.refs_6_.refs_0_), channel_id=1, source_target_pairs={{0,8},{1,9},{2,10},{3,11},{4,12},{5,13},{6,14},{7,15},{8,0},{9,1},... | collective-permute-start | bytes 196616 | tf_op jit(solution)/shard_map/ppermute | solution.py:398
  21.7 10.8 %collective-permute-start.10 = (f32[784,128]{1,0:T(8,128)S(1)}, f32[784,128]{1,0:T(8,128)S(1)}, u32[]{:S(2)}, u32[]{:S(2)}) collective-permute-start(f32[784,128]{1,0:T(8,128)S(1)} %get-tuple-element.37.refs_6_), channel_id=1, source_target_pairs={{0,2},{1,3},{2,0},{3,1},{4,6},{5,7},{6,4},{7,5},{8,10},{9,11},{10,... | collective-permute-start | bytes 1204232 | tf_op jit(solution)/shard_map/ppermute | solution.py:398
  22.7 9.9 %collective-permute-start.11 = (f32[784,128]{1,0:T(8,128)S(1)}, f32[784,128]{1,0:T(8,128)S(1)}, u32[]{:S(2)}, u32[]{:S(2)}) collective-permute-start(f32[784,128]{1,0:T(8,128)S(1)} %get-tuple-element.38), channel_id=1, source_target_pairs={{0,4},{1,5},{2,6},{3,7},{4,0},{5,1},{6,2},{7,3},{8,12},{9,13},{10,... | collective-permute-start | bytes 1204232 | tf_op jit(solution)/shard_map/ppermute | solution.py:398
  23.9 5.5 %collective-permute-start.12 = (f32[256,128]{1,0:T(8,128)S(1)}, f32[256,128]{1,0:T(8,128)S(1)}, u32[]{:S(2)}, u32[]{:S(2)}) collective-permute-start(f32[256,128]{1,0:T(8,128)S(1)} %shard_map.153.refs_3_), channel_id=1, source_target_pairs={{0,16},{1,17},{2,18},{3,19},{4,20},{5,21},{6,22},{7,23},{8,24},{9,... | collective-permute-start | bytes 393224 | tf_op jit(solution)/shard_map/ppermute | solution.py:398
  24.0 16.7 %collective-permute-start.5 = (f32[784,128]{1,0:T(8,128)S(1)}, f32[784,128]{1,0:T(8,128)S(1)}, u32[]{:S(2)}, u32[]{:S(2)}) collective-permute-start(f32[784,128]{1,0:T(8,128)S(1)} %collective-permute-done.4.refs_3_.refs_10_), channel_id=1, source_target_pairs={{0,8},{1,9},{2,10},{3,11},{8,16},{9,17},{10,18},{11,19},{12,4},{13... | collective-permute-start | bytes 1204232 | tf_op jit(solution)/shard_map/ppermute | solution.py:398
  31.2 12.3 %collective-permute-start.14 = (f32[256,128]{1,0:T(8,128)S(1)}, f32[256,128]{1,0:T(8,128)S(1)}, u32[]{:S(2)}, u32[]{:S(2)}) collective-permute-start(f32[256,128]{1,0:T(8,128)S(1)} %get-tuple-element.48), channel_id=1, source_target_pairs={{0,4},{1,5},{2,6},{3,7},{4,0},{5,1},{6,2},{7,3},{8,12},{9,13},{10,... | collective-permute-start | bytes 393224 | tf_op jit(solution)/shard_map/ppermute | solution.py:398
  42.1 5.5 %collective-permute-start.13 = (f32[512,128]{1,0:T(8,128)S(1)}, f32[512,128]{1,0:T(8,128)S(1)}, u32[]{:S(2)}, u32[]{:S(2)}) collective-permute-start(f32[512,128]{1,0:T(8,128)S(1)} %get-tuple-element.45.refs_16_), channel_id=1, source_target_pairs={{0,1},{1,0},{2,3},{3,2},{4,5},{5,4},{6,7},{7,6},{8,9},{9,8},{10,11... | collective-permute-start | bytes 786440 | tf_op jit(solution)/shard_map/ppermute | solution.py:398
  43.4 4.2 %copy-start = (f32[1,512,128]{2,1,0:T(8,128)S(1)}, f32[1,512,128]{2,1,0:T(8,128)}, u32[]{:S(2)}) copy-start(f32[1,512,128]{2,1,0:T(8,128)} %basis.1) | copy-start | bytes 786436
  43.5 4.2 %copy-start.1 = (f32[1,128,128]{2,1,0:T(8,128)S(1)}, f32[1,128,128]{2,1,0:T(8,128)}, u32[]{:S(2)}) copy-start(f32[1,128,128]{2,1,0:T(8,128)} %move.1) | copy-start | bytes 196612
  46.2 1.4 %collective-permute-start.15 = (f32[256,128]{1,0:T(8,128)S(1)}, f32[256,128]{1,0:T(8,128)S(1)}, u32[]{:S(2)}, u32[]{:S(2)}) collective-permute-start(f32[256,128]{1,0:T(8,128)S(1)} %get-tuple-element.50), channel_id=1, source_target_pairs={{0,1},{1,0},{2,3},{3,2},{4,5},{5,4},{6,7},{7,6},{8,9},{9,8},{10,11... | collective-permute-start | bytes 393224 | tf_op jit(solution)/shard_map/ppermute | solution.py:398

commit v5 on v4

--- a/solution.py
+++ b/solution.py
@@ -289,11 +289,16 @@
     share[...] = total[512:1024, :]
 
 
-def close_kernel(idx, far_pair, got, own, skel_pair, ctx, quad_own, quad_got, *refs):
-    blocks = [(b, b, LEAF) for b in (own,) + refs[:8]]
-    keep, share, low, *scratch = refs[8:]
+def far_kernel(idx, far_pair, got, own, skel_pair, *refs):
+    blocks = [(b, b, LEAF) for b in (own,) + refs[:7]]
+    low, *scratch = refs[7:]
     low[...] = jnp.zeros_like(low)
-    add_far(idx[0], range(9), blocks, ((own, LEAF), (got, 64)), far_pair, skel_pair, low, scratch)
+    add_far(idx[0], range(8), blocks, ((own, LEAF), (got, 64)), far_pair, skel_pair, low, scratch)
+
+
+def close_kernel(idx, far_pair, got, own, skel_pair, ctx, quad_own, quad_got, low_in, cd, keep, share, low, *scratch):
+    low[...] = low_in[...]
+    add_far(idx[0], (8,), [(cd, cd, LEAF)], ((own, LEAF), (got, 64)), far_pair, skel_pair, low, scratch)
     local_top = quad_own[128:256, :] + quad_got[128:256, :]
     local_quad = quad_own[0:128, :] + quad_got[0:128, :] + dot(ctx[0:128, :], local_top)
     low[256:384, :] += dot(ctx[128:256, :], local_quad)
@@ -515,8 +520,9 @@
         two = total
     sx, sy = call(cross_kernel, (block,) * 2, [idx, be, bo], n_smem=1, after=[two])
     cx, cy = swap(sx, 2), swap(sy, 4)
-    cd = permute(bd, lambda i: i + 8 if i // 2 % 4 < 2 else i - 8)
     total = near((4, 5), [be, bo], total, [sx])
+    bd_later = call(fetch_kernel, (block,), [bd], after=[total])[0]
+    cd = permute(bd_later, lambda i: i + 8 if i // 2 % 4 < 2 else i - 8)
     if direct:
         quad_own, quad_send = call(
             upper_kernel,
@@ -532,11 +538,21 @@
         quad_own = upper_anywhere(device, shared, ctx, far_quad, far_top, skel_quad, skel_top)
         quad_got = jnp.zeros_like(quad_own)
     total = near((3, 6, 7), [bd, cx, cy], total, [quad_own])
+    far = call(
+        far_kernel,
+        f32(384, 128),
+        [idx, far_pair_t, got, own, skel_pair_t, bx, by, bd, be, bo, cx, cy],
+        n_smem=2,
+        after=[total],
+        scratch=far_scratch(256, 8),
+        flops=2 * 3 * 25 * 128**3,
+    )
     mine, share = call(
         functools.partial(last_kernel, (8,)),
         (f32(512, 128), f32(512, 128)),
         [idx, got, own, cd, total],
         n_smem=1,
+        after=[far],
         scratch=[pltpu.VMEM((1024, 128), jnp.float32)] + near_scratch(),
         flops=2 * NEAR_FLOPS,
     )
@@ -544,11 +560,10 @@
     low, low_share = call(
         close_kernel,
         (f32(256, 128), f32(256, 128)),
-        [idx, far_pair_t, got, own, skel_pair_t, ctx, quad_own, quad_got]
-        + [bx, by, bd, be, bo, cx, cy, cd],
+        [idx, far_pair_t, got, own, skel_pair_t, ctx, quad_own, quad_got, far, cd],
         n_smem=2,
         after=[share],
-        scratch=[pltpu.VMEM((384, 128), jnp.float32)] + far_scratch(256, 9),
+        scratch=[pltpu.VMEM((384, 128), jnp.float32)] + far_scratch(256, 1),
         flops=2 * 3 * 28 * 128**3,
     )
     return call(

time: 49.2 us -> 48.6 us (0.988)
  the two profiles are of different devices: /device:TPU:17 before, /device:TPU:0 now
where the time goes in v5:
time: 48.6 us; the launch traced here: 48.3 us
  Pallas kernels  21.1 us (43%)
  starting transfers between devices  20.9 us (43%)
  waiting for transfers between devices  3.47 us (7%)
  local copies, waits for them, and re-layouts  2.43 us (5%)
    pallas_call x18, Pallas kernels, call(): pl.pallas_call(ordered if after else body, out_shape=outs, in_specs=[SMEM...  21.1 us
    ppermute x16, starting transfers between devices, permute(): lax.ppermute(value, AXIS, [(i, j) for i, j in pairs if 0 <= j < n and i !...  20.9 us
    ppermute x16, waiting for transfers between devices, permute(): lax.ppermute(value, AXIS, [(i, j) for i, j in pairs if 0 <= j < n and i !...  3.47 us
    unnamed x24, local copies, waits for them, and re-layouts  2.43 us
  transfers between devices with their start and end apart: 16, of which 2 were waited for; matrix products, arithmetic and copies ran while one was open for 0% of the time, Pallas kernels for 36%

profile of v5, /device:TPU:0, one launch (start us, length us, event | category | flops | bytes accessed | tf_op | source)
XLA Modules:
  0.0 48.3 jit_solution(1990075607464383097)
XLA Ops:
  0.0 0.0 copy-start.2
  0.0 2.4 %shard_map.145 = (f32[784,128]{1,0:T(8,128)}, f32[64,128]{1,0:T(8,128)}, f32[80,128]{1,0:T(8,128)}) custom-call(s32[1]{0:T(128)} %bitcast.idx.refs_0_, f32[1,512,128]{2,1,0:T(8,128)} %refs_0_.1, f32[1,512,128]{2,1,0:T(8,128)} %basis.1, f32[1,128,128]{2,1,0:T(8,128)} %move.1, f32[3,1,512]{2,1,0:T(1,128)} %bitcast.11, f32[3,1,128]{2,1,0:T(1,128)} %bitcast.12, ...), custom_call_target="tpu_custom_call" | custom-call | flops 125829120 | bytes 1048576 | tf_op jit(solution)/shard_map/pallas_call | solution.py:37
  2.4 3.0 %collective-permute-start.1 = (f32[784,128]{1,0:T(8,128)}, f32[784,128]{1,0:T(8,128)S(1)}, u32[]{:S(2)}, u32[]{:S(2)}) collective-permute-start(f32[784,128]{1,0:T(8,128)} %get-tuple-element.29.refs_2_), channel_id=1, source_target_pairs={{0,2},{1,3},{2,0},{3,1},{4,6},{5,7},{6,4},{7,5},{8,10},{9,11},{10,... | collective-permute-start | bytes 1204232 | tf_op jit(solution)/shard_map/ppermute | solution.py:403
  5.4 1.5 %collective-permute-start.2 = (f32[784,128]{1,0:T(8,128)}, f32[784,128]{1,0:T(8,128)S(1)}, u32[]{:S(2)}, u32[]{:S(2)}) collective-permute-start(f32[784,128]{1,0:T(8,128)} %get-tuple-element.29.refs_2_), channel_id=1, source_target_pairs={{0,4},{1,5},{2,6},{3,7},{4,0},{5,1},{6,2},{7,3},{8,12},{9,13},{10,... | collective-permute-start | bytes 1204232 | tf_op jit(solution)/shard_map/ppermute | solution.py:403
  6.9 0.0 collective-permute-start
  6.9 1.6 %collective-permute-start.5 = (f32[784,128]{1,0:T(8,128)}, f32[784,128]{1,0:T(8,128)S(1)}, u32[]{:S(2)}, u32[]{:S(2)}) collective-permute-start(f32[784,128]{1,0:T(8,128)} %get-tuple-element.29.refs_2_), channel_id=1, source_target_pairs={{0,8},{1,9},{2,10},{3,11},{4,12},{5,13},{6,14},{7,15},{8,0},{9,1},... | collective-permute-start | bytes 1204232 | tf_op jit(solution)/shard_map/ppermute | solution.py:403
  8.5 0.7 %collective-permute-start.6 = (f32[784,128]{1,0:T(8,128)}, f32[784,128]{1,0:T(8,128)S(1)}, u32[]{:S(2)}, u32[]{:S(2)}) collective-permute-start(f32[784,128]{1,0:T(8,128)} %get-tuple-element.29.refs_2_), channel_id=1, source_target_pairs={{8,16},{9,17},{10,18},{11,19},{12,20},{13,21},{14,22},{15,23},{16,... | collective-permute-start | bytes 1204232 | tf_op jit(solution)/shard_map/ppermute | solution.py:403
  9.2 0.0 collective-permute-done.got.refs_1_.refs_2_
  9.2 0.0 copy-done.2
  9.2 0.0 copy-done.5
  9.2 0.0 copy-start.3
  9.2 0.7 %copy-done.3 = f32[64,128]{1,0:T(8,128)S(1)} copy-done((f32[64,128]{1,0:T(8,128)S(1)}, f32[64,128]{1,0:T(8,128)}, u32[]{:S(2)}) %copy-start.3) | copy-done | bytes 32792
  10.0 0.3 shard_map.146
  10.2 0.6 %collective-permute-start.3 = (f32[160,128]{1,0:T(8,128)S(1)}, f32[160,128]{1,0:T(8,128)S(1)}, u32[]{:S(2)}, u32[]{:S(2)}) collective-permute-start(f32[160,128]{1,0:T(8,128)S(1)} %get-tuple-element.31.refs_3_.refs_0_), channel_id=1, source_target_pairs={{0,2},{1,3},{2,0},{3,1},{4,6},{5,7},{6,4},{7,5},{8,10},{9,11},{10,... | collective-permute-start | bytes 245768 | tf_op jit(solution)/shard_map/ppermute | solution.py:403
  10.8 1.0 %copy-done.11 = f32[784,128]{1,0:T(8,128)S(1)} copy-done((f32[784,128]{1,0:T(8,128)S(1)}, f32[784,128]{1,0:T(8,128)}, u32[]{:S(2)}) %copy-start.11) | copy-done | bytes 401432
  11.8 1.7 %shard_map.147 = (f32[1024,128]{1,0:T(8,128)S(1)}, f32[784,128]{1,0:T(8,128)S(1)}) custom-call(s32[1]{0:T(128)} %bitcast.idx.refs_0_, f32[80,128]{1,0:T(8,128)S(1)} %collective-permute-done.got.refs_1_.refs_2_, f32[784,128]{1,0:T(8,128)S(1)} %copy-done.11, f32[160,128]{1,0:T(8,128)S(1)} %get-tuple-element.31.refs_3_.refs_0_), custom_call_target="tpu_custom_call" | custom-call | flops 805306368 | tf_op jit(solution)/shard_map/pallas_call | solution.py:37
  13.5 0.0 copy-start.7
  13.5 0.0 copy-start.10
  13.5 0.0 copy-done.4
  13.5 0.0 copy-done.6
  13.6 0.0 copy-done.8
  13.6 0.0 copy-done.9
  13.6 0.6 %copy-done.7 = f32[4,3,128]{2,0,1:T(4,128)S(1)} copy-done((f32[4,3,128]{2,0,1:T(4,128)S(1)}, f32[4,3,128]{2,0,1:T(4,128)}, u32[]{:S(2)}) %copy-start.7) | copy-done | bytes 6168
  14.2 0.0 copy-done.10
  14.2 2.4 %collective-permute-done.3.refs_1_ = f32[160,128]{1,0:T(8,128)S(1)} collective-permute-done((f32[160,128]{1,0:T(8,128)S(1)}, f32[160,128]{1,0:T(8,128)S(1)}, u32[]{:S(2)}, u32[]{:S(2)}) %collective-permute-start.3) | collective-permute-done | bytes 81952 | tf_op jit(solution)/shard_map/ppermute | solution.py:403
  16.7 0.1 collective-permute-start.7
  16.7 0.0 collective-permute-done.1.refs_1_.refs_3_.refs_5_
  16.7 0.0 collective-permute-done.2.refs_2_.refs_4_.refs_6_
  16.8 0.1 shard_map.150.refs_3_
  16.8 1.8 %collective-permute-start.4 = (f32[784,128]{1,0:T(8,128)S(1)}, f32[784,128]{1,0:T(8,128)S(1)}, u32[]{:S(2)}, u32[]{:S(2)}) collective-permute-start(f32[784,128]{1,0:T(8,128)S(1)} %shard_map.150.refs_3_), channel_id=1, source_target_pairs={{0,4},{1,3},{2,6},{3,1},{4,0},{5,7},{6,2},{7,5},{8,12},{9,11},{10,... | collective-permute-start | bytes 1204232 | tf_op jit(solution)/shard_map/ppermute | solution.py:403
  18.6 0.0 collective-permute-done.7.refs_2_
  18.6 0.3 shard_map.151
  18.9 1.9 %collective-permute-start.8 = (f32[128,128]{1,0:T(8,128)S(1)}, f32[128,128]{1,0:T(8,128)S(1)}, u32[]{:S(2)}, u32[]{:S(2)}) collective-permute-start(f32[128,128]{1,0:T(8,128)S(1)} %get-tuple-element.36.refs_6_.refs_0_), channel_id=1, source_target_pairs={{0,8},{1,9},{2,10},{3,11},{4,12},{5,13},{6,14},{7,15},{8,0},{9,1},... | collective-permute-start | bytes 196616 | tf_op jit(solution)/shard_map/ppermute | solution.py:403
  20.9 2.4 %shard_map.152.refs_2_.refs_5_ = f32[1024,128]{1,0:T(8,128)S(1)} custom-call(s32[1]{0:T(128)} %bitcast.idx.refs_0_, f32[80,128]{1,0:T(8,128)S(1)} %collective-permute-done.got.refs_1_.refs_2_, f32[784,128]{1,0:T(8,128)S(1)} %get-tuple-element.32.refs_2_.refs_3_, f32[784,128]{1,0:T(8,128)S(1)} %collective-permute-done.1.refs_1_.refs_3_.refs_5_, ...), custom_call_target="tpu_custom_call" | custom-call | flops 1610612736 | tf_op jit(solution)/shard_map/pallas_call | solution.py:37
  23.3 0.0 collective-permute-done.8.refs_1_
  23.3 0.0 collective-permute-done.5.refs_1_.refs_3_.refs_8_
  23.3 0.0 collective-permute-done.6.refs_2_.refs_4_.refs_9_
  23.3 0.1 shard_map.154
  23.5 1.5 %collective-permute-start.10 = (f32[784,128]{1,0:T(8,128)S(1)}, f32[784,128]{1,0:T(8,128)S(1)}, u32[]{:S(2)}, u32[]{:S(2)}) collective-permute-start(f32[784,128]{1,0:T(8,128)S(1)} %get-tuple-element.37.refs_6_), channel_id=1, source_target_pairs={{0,2},{1,3},{2,0},{3,1},{4,6},{5,7},{6,4},{7,5},{8,10},{9,11},{10,... | collective-permute-start | bytes 1204232 | tf_op jit(solution)/shard_map/ppermute | solution.py:403
  25.0 1.2 %collective-permute-start.11 = (f32[784,128]{1,0:T(8,128)S(1)}, f32[784,128]{1,0:T(8,128)S(1)}, u32[]{:S(2)}, u32[]{:S(2)}) collective-permute-start(f32[784,128]{1,0:T(8,128)S(1)} %get-tuple-element.38), channel_id=1, source_target_pairs={{0,4},{1,5},{2,6},{3,7},{4,0},{5,1},{6,2},{7,3},{8,12},{9,13},{10,... | collective-permute-start | bytes 1204232 | tf_op jit(solution)/shard_map/ppermute | solution.py:403
  26.2 2.6 %collective-permute-start.12 = (f32[256,128]{1,0:T(8,128)S(1)}, f32[256,128]{1,0:T(8,128)S(1)}, u32[]{:S(2)}, u32[]{:S(2)}) collective-permute-start(f32[256,128]{1,0:T(8,128)S(1)} %shard_map.153.refs_3_), channel_id=1, source_target_pairs={{0,16},{1,17},{2,18},{3,19},{4,20},{5,21},{6,22},{7,23},{8,24},{9,... | collective-permute-start | bytes 393224 | tf_op jit(solution)/shard_map/ppermute | solution.py:403
  28.8 2.4 %shard_map.155.refs_1_.refs_7_.refs_6_ = f32[1024,128]{1,0:T(8,128)S(1)} custom-call(s32[1]{0:T(128)} %bitcast.idx.refs_0_, f32[80,128]{1,0:T(8,128)S(1)} %collective-permute-done.got.refs_1_.refs_2_, f32[784,128]{1,0:T(8,128)S(1)} %get-tuple-element.32.refs_2_.refs_3_, f32[784,128]{1,0:T(8,128)S(1)} %collective-permute-done.5.refs_1_.refs_3_.refs_8_, ...), custom_call_target="tpu_custom_call" | custom-call | flops 1610612736 | tf_op jit(solution)/shard_map/pallas_call | solution.py:37
  31.1 0.0 collective-permute-done.4.refs_0_.refs_3_.refs_7_
  31.2 3.7 %collective-permute-start.9 = (f32[784,128]{1,0:T(8,128)S(1)}, f32[784,128]{1,0:T(8,128)S(1)}, u32[]{:S(2)}, u32[]{:S(2)}) collective-permute-start(f32[784,128]{1,0:T(8,128)S(1)} %shard_map.156), channel_id=1, source_target_pairs={{0,8},{1,9},{2,10},{3,11},{8,16},{9,17},{10,18},{11,19},{12,4},{13... | collective-permute-start | bytes 1204232 | tf_op jit(solution)/shard_map/ppermute | solution.py:403
  34.9 0.0 collective-permute-done.12.refs_4_
  34.9 1.7 %shard_map.157 = (f32[256,128]{1,0:T(8,128)S(1)}, f32[256,128]{1,0:T(8,128)S(1)}) custom-call(s32[1]{0:T(128)} %bitcast.idx.refs_0_, s32[8,8]{1,0:T(8,128)S(1)} %get-tuple-element.39.refs_1_, s32[4,8]{1,0:T(4,128)S(1)} %get-tuple-element.40.refs_2_, f32[256,128]{1,0:T(8,128)S(1)} %shard_map.153.refs_3_, f32[256,128]{1,0:T(8,128)S(1)} %collective-permute-done.12.refs_4_, ...), custom_call_target="tpu_custom_call" | custom-call | flops 301989888 | tf_op jit(solution)/shard_map/pallas_call | solution.py:37
  36.6 0.1 collective-permute-start.14
  36.7 0.0 collective-permute-done.10.refs_4_.refs_10_
  36.7 0.0 collective-permute-done.11.refs_5_.refs_11_
  36.7 3.4 %shard_map.158.refs_12_.refs_4_ = f32[1024,128]{1,0:T(8,128)S(1)} custom-call(s32[1]{0:T(128)} %bitcast.idx.refs_0_, f32[80,128]{1,0:T(8,128)S(1)} %collective-permute-done.got.refs_1_.refs_2_, f32[784,128]{1,0:T(8,128)S(1)} %get-tuple-element.32.refs_2_.refs_3_, f32[784,128]{1,0:T(8,128)S(1)} %collective-permute-done.4.refs_0_.refs_3_.refs_7_, ...), custom_call_target="tpu_custom_call" | custom-call | flops 2415919104 | tf_op jit(solution)/shard_map/pallas_call | solution.py:37
  40.1 2.3 %shard_map.159.refs_5_.refs_8_ = f32[384,128]{1,0:T(8,128)S(1)} custom-call(s32[1]{0:T(128)} %bitcast.idx.refs_0_, s32[8,16]{1,0:T(8,128)S(1)} %get-tuple-element.35.refs_3_.refs_1_, f32[80,128]{1,0:T(8,128)S(1)} %collective-permute-done.got.refs_1_.refs_2_, f32[784,128]{1,0:T(8,128)S(1)} %get-tuple-element.32.refs_2_.refs_3_, ...), custom_call_target="tpu_custom_call" | custom-call | flops 314572800 | tf_op jit(solution)/shard_map/pallas_call | solution.py:37
  42.5 0.0 collective-permute-done.9.refs_3_.refs_9_
  42.5 1.4 %shard_map.160 = (f32[512,128]{1,0:T(8,128)S(1)}, f32[512,128]{1,0:T(8,128)S(1)}) custom-call(s32[1]{0:T(128)} %bitcast.idx.refs_0_, f32[80,128]{1,0:T(8,128)S(1)} %collective-permute-done.got.refs_1_.refs_2_, f32[784,128]{1,0:T(8,128)S(1)} %get-tuple-element.32.refs_2_.refs_3_, f32[784,128]{1,0:T(8,128)S(1)} %collective-permute-done.9.refs_3_.refs_9_, ...), custom_call_target="tpu_custom_call" | custom-call | flops 805306368 | tf_op jit(solution)/shard_map/pallas_call | solution.py:37
  43.9 0.1 collective-permute-start.13
  44.0 0.0 collective-permute-done.14.refs_7_
  44.0 0.0 copy-start
  44.0 0.0 copy-start.1
  44.0 1.5 %shard_map.161 = (f32[256,128]{1,0:T(8,128)S(1)}, f32[256,128]{1,0:T(8,128)S(1)}) custom-call(s32[1]{0:T(128)} %bitcast.idx.refs_0_, s32[8,16]{1,0:T(8,128)S(1)} %get-tuple-element.35.refs_3_.refs_1_, f32[80,128]{1,0:T(8,128)S(1)} %collective-permute-done.got.refs_1_.refs_2_, f32[784,128]{1,0:T(8,128)S(1)} %get-tuple-element.32.refs_2_.refs_3_, ...), custom_call_target="tpu_custom_call" | custom-call | flops 352321536 | tf_op jit(solution)/shard_map/pallas_call | solution.py:37
  45.5 0.5 %collective-permute-start.15 = (f32[256,128]{1,0:T(8,128)S(1)}, f32[256,128]{1,0:T(8,128)S(1)}, u32[]{:S(2)}, u32[]{:S(2)}) collective-permute-start(f32[256,128]{1,0:T(8,128)S(1)} %get-tuple-element.50), channel_id=1, source_target_pairs={{0,1},{1,0},{2,3},{3,2},{4,5},{5,4},{6,7},{7,6},{8,9},{9,8},{10,11... | collective-permute-start | bytes 393224 | tf_op jit(solution)/shard_map/ppermute | solution.py:403
  46.0 1.0 %collective-permute-done.15.low_got = f32[256,128]{1,0:T(8,128)S(1)} collective-permute-done((f32[256,128]{1,0:T(8,128)S(1)}, f32[256,128]{1,0:T(8,128)S(1)}, u32[]{:S(2)}, u32[]{:S(2)}) %collective-permute-start.15) | collective-permute-done | bytes 131104 | tf_op jit(solution)/shard_map/ppermute | solution.py:403
  47.0 0.0 collective-permute-done.13.near_got
  47.0 0.0 copy-done
  47.0 0.0 copy-done.1
  47.0 1.2 %shard_map.162 = f32[1,512,128]{2,1,0:T(8,128)} custom-call(f32[512,128]{1,0:T(8,128)S(1)} %get-tuple-element.45.near, f32[512,128]{1,0:T(8,128)S(1)} %collective-permute-done.13.near_got, f32[256,128]{1,0:T(8,128)S(1)} %get-tuple-element.49.low, f32[256,128]{1,0:T(8,128)S(1)} %collective-permute-done.15.low_got, f32[1,128,128]{2,1,0:T(8,128)S(1)} %copy-done.1, ...), custom_call_target="tpu_custom_call" | custom-call | flops 125829120 | tf_op jit(solution)/shard_map/pallas_call | solution.py:37
  (10 shorter events, 0.1 us)
Async XLA Ops:
  0.0 9.2 %copy-start.2 = (f32[64,128]{1,0:T(8,128)S(1)}, f32[64,128]{1,0:T(8,128)}, u32[]{:S(2)}) copy-start(f32[64,128]{1,0:T(8,128)} %epair.1) | copy-start | bytes 98308
  0.0 9.2 %copy-start.5 = (f32[32,128]{1,0:T(8,128)S(1)}, f32[32,128]{1,0:T(8,128)}, u32[]{:S(2)}) copy-start(f32[32,128]{1,0:T(8,128)} %equad.1) | copy-start | bytes 49156
  2.4 14.4 %collective-permute-start.1 = (f32[784,128]{1,0:T(8,128)}, f32[784,128]{1,0:T(8,128)S(1)}, u32[]{:S(2)}, u32[]{:S(2)}) collective-permute-start(f32[784,128]{1,0:T(8,128)} %get-tuple-element.29.refs_2_), channel_id=1, source_target_pairs={{0,2},{1,3},{2,0},{3,1},{4,6},{5,7},{6,4},{7,5},{8,10},{9,11},{10,... | collective-permute-start | bytes 1204232 | tf_op jit(solution)/shard_map/ppermute | solution.py:403
  5.4 11.4 %collective-permute-start.2 = (f32[784,128]{1,0:T(8,128)}, f32[784,128]{1,0:T(8,128)S(1)}, u32[]{:S(2)}, u32[]{:S(2)}) collective-permute-start(f32[784,128]{1,0:T(8,128)} %get-tuple-element.29.refs_2_), channel_id=1, source_target_pairs={{0,4},{1,5},{2,6},{3,7},{4,0},{5,1},{6,2},{7,3},{8,12},{9,13},{10,... | collective-permute-start | bytes 1204232 | tf_op jit(solution)/shard_map/ppermute | solution.py:403
  6.9 2.3 %collective-permute-start = (f32[80,128]{1,0:T(8,128)}, f32[80,128]{1,0:T(8,128)S(1)}, u32[]{:S(2)}, u32[]{:S(2)}) collective-permute-start(f32[80,128]{1,0:T(8,128)} %get-tuple-element.28), channel_id=1, source_target_pairs={{0,1},{1,0},{2,3},{3,2},{4,5},{5,4},{6,7},{7,6},{8,9},{9,8},{10,11... | collective-permute-start | bytes 122888 | tf_op jit(solution)/shard_map/ppermute | solution.py:403
  6.9 16.4 %collective-permute-start.5 = (f32[784,128]{1,0:T(8,128)}, f32[784,128]{1,0:T(8,128)S(1)}, u32[]{:S(2)}, u32[]{:S(2)}) collective-permute-start(f32[784,128]{1,0:T(8,128)} %get-tuple-element.29.refs_2_), channel_id=1, source_target_pairs={{0,8},{1,9},{2,10},{3,11},{4,12},{5,13},{6,14},{7,15},{8,0},{9,1},... | collective-permute-start | bytes 1204232 | tf_op jit(solution)/shard_map/ppermute | solution.py:403
  8.5 14.8 %collective-permute-start.6 = (f32[784,128]{1,0:T(8,128)}, f32[784,128]{1,0:T(8,128)S(1)}, u32[]{:S(2)}, u32[]{:S(2)}) collective-permute-start(f32[784,128]{1,0:T(8,128)} %get-tuple-element.29.refs_2_), channel_id=1, source_target_pairs={{8,16},{9,17},{10,18},{11,19},{12,20},{13,21},{14,22},{15,23},{16,... | collective-permute-start | bytes 1204232 | tf_op jit(solution)/shard_map/ppermute | solution.py:403
  9.2 0.8 %copy-start.3 = (f32[64,128]{1,0:T(8,128)S(1)}, f32[64,128]{1,0:T(8,128)}, u32[]{:S(2)}) copy-start(f32[64,128]{1,0:T(8,128)} %get-tuple-element.30.keep) | copy-start | bytes 98308
  10.2 6.4 %collective-permute-start.3 = (f32[160,128]{1,0:T(8,128)S(1)}, f32[160,128]{1,0:T(8,128)S(1)}, u32[]{:S(2)}, u32[]{:S(2)}) collective-permute-start(f32[160,128]{1,0:T(8,128)S(1)} %get-tuple-element.31.refs_3_.refs_0_), channel_id=1, source_target_pairs={{0,2},{1,3},{2,0},{3,1},{4,6},{5,7},{6,4},{7,5},{8,10},{9,11},{10,... | collective-permute-start | bytes 245768 | tf_op jit(solution)/shard_map/ppermute | solution.py:403
  10.8 1.0 %copy-start.11 = (f32[784,128]{1,0:T(8,128)S(1)}, f32[784,128]{1,0:T(8,128)}, u32[]{:S(2)}) copy-start(f32[784,128]{1,0:T(8,128)} %get-tuple-element.29.refs_2_) | copy-start | bytes 1204228
  11.8 1.7 %copy-start.4 = (f32[16,3,128]{2,0,1:T(8,128)S(1)}, f32[16,3,128]{2,0,1:T(8,128)}, u32[]{:S(2)}) copy-start(f32[16,3,128]{2,0,1:T(8,128)} %param.22) | copy-start | bytes 73732
  11.8 1.7 %copy-start.6 = (f32[8,3,128]{2,0,1:T(8,128)S(1)}, f32[8,3,128]{2,0,1:T(8,128)}, u32[]{:S(2)}) copy-start(f32[8,3,128]{2,0,1:T(8,128)} %param.23) | copy-start | bytes 36868
  11.8 1.7 %copy-start.8 = (s32[16,8]{0,1:T(8,128)S(1)}, s32[16,8]{0,1:T(8,128)}, u32[]{:S(2)}) copy-start(s32[16,8]{0,1:T(8,128)} %param.27) | copy-start | bytes 1540
  11.8 1.7 %copy-start.9 = (s32[8,8]{1,0:T(8,128)S(1)}, s32[8,8]{1,0:T(8,128)}, u32[]{:S(2)}) copy-start(s32[8,8]{1,0:T(8,128)} %refs_1_.3) | copy-start | bytes 772
  13.5 0.7 %copy-start.7 = (f32[4,3,128]{2,0,1:T(4,128)S(1)}, f32[4,3,128]{2,0,1:T(4,128)}, u32[]{:S(2)}) copy-start(f32[4,3,128]{2,0,1:T(4,128)} %param.24) | copy-start | bytes 18436
  13.5 0.7 %copy-start.10 = (s32[4,8]{1,0:T(4,128)S(1)}, s32[4,8]{1,0:T(4,128)}, u32[]{:S(2)}) copy-start(s32[4,8]{1,0:T(4,128)} %refs_2_.3) | copy-start | bytes 388
  16.7 2.0 %collective-permute-start.7 = (f32[256,128]{1,0:T(8,128)S(1)}, f32[256,128]{1,0:T(8,128)S(1)}, u32[]{:S(2)}, u32[]{:S(2)}) collective-permute-start(f32[256,128]{1,0:T(8,128)S(1)} %shard_map.149.refs_3_.refs_1_), channel_id=1, source_target_pairs={{0,1},{1,0},{2,3},{3,2},{4,5},{5,4},{6,7},{7,6},{8,9},{9,8},{10,11... | collective-permute-start | bytes 393224 | tf_op jit(solution)/shard_map/ppermute | solution.py:403
  16.8 14.3 %collective-permute-start.4 = (f32[784,128]{1,0:T(8,128)S(1)}, f32[784,128]{1,0:T(8,128)S(1)}, u32[]{:S(2)}, u32[]{:S(2)}) collective-permute-start(f32[784,128]{1,0:T(8,128)S(1)} %shard_map.150.refs_3_), channel_id=1, source_target_pairs={{0,4},{1,3},{2,6},{3,1},{4,0},{5,7},{6,2},{7,5},{8,12},{9,11},{10,... | collective-permute-start | bytes 1204232 | tf_op jit(solution)/shard_map/ppermute | solution.py:403
  18.9 4.4 %collective-permute-start.8 = (f32[128,128]{1,0:T(8,128)S(1)}, f32[128,128]{1,0:T(8,128)S(1)}, u32[]{:S(2)}, u32[]{:S(2)}) collective-permute-start(f32[128,128]{1,0:T(8,128)S(1)} %get-tuple-element.36.refs_6_.refs_0_), channel_id=1, source_target_pairs={{0,8},{1,9},{2,10},{3,11},{4,12},{5,13},{6,14},{7,15},{8,0},{9,1},... | collective-permute-start | bytes 196616 | tf_op jit(solution)/shard_map/ppermute | solution.py:403
  23.5 13.2 %collective-permute-start.10 = (f32[784,128]{1,0:T(8,128)S(1)}, f32[784,128]{1,0:T(8,128)S(1)}, u32[]{:S(2)}, u32[]{:S(2)}) collective-permute-start(f32[784,128]{1,0:T(8,128)S(1)} %get-tuple-element.37.refs_6_), channel_id=1, source_target_pairs={{0,2},{1,3},{2,0},{3,1},{4,6},{5,7},{6,4},{7,5},{8,10},{9,11},{10,... | collective-permute-start | bytes 1204232 | tf_op jit(solution)/shard_map/ppermute | solution.py:403
  25.0 11.7 %collective-permute-start.11 = (f32[784,128]{1,0:T(8,128)S(1)}, f32[784,128]{1,0:T(8,128)S(1)}, u32[]{:S(2)}, u32[]{:S(2)}) collective-permute-start(f32[784,128]{1,0:T(8,128)S(1)} %get-tuple-element.38), channel_id=1, source_target_pairs={{0,4},{1,5},{2,6},{3,7},{4,0},{5,1},{6,2},{7,3},{8,12},{9,13},{10,... | collective-permute-start | bytes 1204232 | tf_op jit(solution)/shard_map/ppermute | solution.py:403
  26.2 8.7 %collective-permute-start.12 = (f32[256,128]{1,0:T(8,128)S(1)}, f32[256,128]{1,0:T(8,128)S(1)}, u32[]{:S(2)}, u32[]{:S(2)}) collective-permute-start(f32[256,128]{1,0:T(8,128)S(1)} %shard_map.153.refs_3_), channel_id=1, source_target_pairs={{0,16},{1,17},{2,18},{3,19},{4,20},{5,21},{6,22},{7,23},{8,24},{9,... | collective-permute-start | bytes 393224 | tf_op jit(solution)/shard_map/ppermute | solution.py:403
  31.2 11.3 %collective-permute-start.9 = (f32[784,128]{1,0:T(8,128)S(1)}, f32[784,128]{1,0:T(8,128)S(1)}, u32[]{:S(2)}, u32[]{:S(2)}) collective-permute-start(f32[784,128]{1,0:T(8,128)S(1)} %shard_map.156), channel_id=1, source_target_pairs={{0,8},{1,9},{2,10},{3,11},{8,16},{9,17},{10,18},{11,19},{12,4},{13... | collective-permute-start | bytes 1204232 | tf_op jit(solution)/shard_map/ppermute | solution.py:403
  36.6 7.4 %collective-permute-start.14 = (f32[256,128]{1,0:T(8,128)S(1)}, f32[256,128]{1,0:T(8,128)S(1)}, u32[]{:S(2)}, u32[]{:S(2)}) collective-permute-start(f32[256,128]{1,0:T(8,128)S(1)} %get-tuple-element.48), channel_id=1, source_target_pairs={{0,4},{1,5},{2,6},{3,7},{4,0},{5,1},{6,2},{7,3},{8,12},{9,13},{10,... | collective-permute-start | bytes 393224 | tf_op jit(solution)/shard_map/ppermute | solution.py:403
  43.9 3.1 %collective-permute-start.13 = (f32[512,128]{1,0:T(8,128)S(1)}, f32[512,128]{1,0:T(8,128)S(1)}, u32[]{:S(2)}, u32[]{:S(2)}) collective-permute-start(f32[512,128]{1,0:T(8,128)S(1)} %get-tuple-element.46.refs_10_), channel_id=1, source_target_pairs={{0,1},{1,0},{2,3},{3,2},{4,5},{5,4},{6,7},{7,6},{8,9},{9,8},{10,11... | collective-permute-start | bytes 786440 | tf_op jit(solution)/shard_map/ppermute | solution.py:403
  44.0 3.1 %copy-start = (f32[1,512,128]{2,1,0:T(8,128)S(1)}, f32[1,512,128]{2,1,0:T(8,128)}, u32[]{:S(2)}) copy-start(f32[1,512,128]{2,1,0:T(8,128)} %basis.1) | copy-start | bytes 786436
  44.0 3.0 %copy-start.1 = (f32[1,128,128]{2,1,0:T(8,128)S(1)}, f32[1,128,128]{2,1,0:T(8,128)}, u32[]{:S(2)}) copy-start(f32[1,128,128]{2,1,0:T(8,128)} %move.1) | copy-start | bytes 196612
  45.5 1.5 %collective-permute-start.15 = (f32[256,128]{1,0:T(8,128)S(1)}, f32[256,128]{1,0:T(8,128)S(1)}, u32[]{:S(2)}, u32[]{:S(2)}) collective-permute-start(f32[256,128]{1,0:T(8,128)S(1)} %get-tuple-element.50), channel_id=1, source_target_pairs={{0,1},{1,0},{2,3},{3,2},{4,5},{5,4},{6,7},{7,6},{8,9},{9,8},{10,11... | collective-permute-start | bytes 393224 | tf_op jit(solution)/shard_map/ppermute | solution.py:403

commit v6 on v5

--- a/solution.py
+++ b/solution.py
@@ -300,8 +300,8 @@
     low[...] = low_in[...]
     add_far(idx[0], (8,), [(cd, cd, LEAF)], ((own, LEAF), (got, 64)), far_pair, skel_pair, low, scratch)
     local_top = quad_own[128:256, :] + quad_got[128:256, :]
-    local_quad = quad_own[0:128, :] + quad_got[0:128, :] + dot(ctx[0:128, :], local_top)
-    low[256:384, :] += dot(ctx[128:256, :], local_quad)
+    local_quad = quad_own[0:128, :] + quad_got[0:128, :] + three_dot(ctx[0:128, :], local_top)
+    low[256:384, :] += three_dot(ctx[128:256, :], local_quad)
     keep[0:128, :] = low[0:128, :]
     keep[128:256, :] = low[256:384, :]
     share[...] = low[128:384, :]
@@ -309,7 +309,7 @@
 
 def rise_kernel(keep, got, epair, equad, out, moved):
     moved[...] = epair[...]
-    out[0:128, :] = dot_t(epair[...], keep[...] + got[0:64, :])
+    out[0:128, :] = three_dot(epair[...], keep[...] + got[0:64, :], 0)
     out[128:160, :] = equad[...]
 
 
@@ -333,7 +333,7 @@
     ctx[pl.ds(128 + half, 64), :] = mine[192:256, :]
     ctx[pl.ds(192 - half, 64), :] = theirs[192:256, :]
     quad[...] = mine[0:128, :] + theirs[0:128, :]
-    top[...] = dot_t(ctx[0:128, :], quad[...])
+    top[...] = three_dot(ctx[0:128, :], quad[...], 0)
     send[0:64, :] = quad[pl.ds(half, 64), :]
     send[64:128, :] = top[pl.ds(half, 64), :]
 
@@ -378,7 +378,7 @@
 
 def final_kernel(near, near_got, low, low_got, move, basis, out):
     local_pair = low[128:256, :] + low_got[128:256, :]
-    local = low[0:128, :] + low_got[0:128, :] + dot(move[0], local_pair)
+    local = low[0:128, :] + low_got[0:128, :] + three_dot(move[0], local_pair)
     out[0] = near[...] + near_got[...] + three_dot(basis[0], local)
 
 

time: 48.6 us -> 48.3 us (level)
  transfers between devices with their start and end apart: 16 -> 16, of which waited for: 2 -> 3; matrix products, arithmetic and copies ran while one was open for 0% -> 0% of each run, Pallas kernels for 36% -> 36%
where the time goes in v6:
time: 48.3 us; the launch traced here: 48 us
  Pallas kernels  20.9 us (43%)
  starting transfers between devices  20.9 us (43%)
  waiting for transfers between devices  3.56 us (7%)
  local copies, waits for them, and re-layouts  2.43 us (5%)
    pallas_call x18, Pallas kernels, call(): pl.pallas_call(ordered if after else body, out_shape=outs, in_specs=[SMEM...  20.9 us
    ppermute x16, starting transfers between devices, permute(): lax.ppermute(value, AXIS, [(i, j) for i, j in pairs if 0 <= j < n and i !...  20.9 us
    ppermute x16, waiting for transfers between devices, permute(): lax.ppermute(value, AXIS, [(i, j) for i, j in pairs if 0 <= j < n and i !...  3.56 us
    unnamed x24, local copies, waits for them, and re-layouts  2.43 us
  transfers between devices with their start and end apart: 16, of which 3 were waited for; matrix products, arithmetic and copies ran while one was open for 0% of the time, Pallas kernels for 36%

profile of v6, /device:TPU:0, one launch (start us, length us, event | category | flops | bytes accessed | tf_op | source)
XLA Modules:
  0.0 48.0 jit_solution(12705928192656235514)
XLA Ops:
  0.0 0.0 copy-start.2
  0.0 2.4 %shard_map.145 = (f32[784,128]{1,0:T(8,128)}, f32[64,128]{1,0:T(8,128)}, f32[80,128]{1,0:T(8,128)}) custom-call(s32[1]{0:T(128)} %bitcast.idx.refs_0_, f32[1,512,128]{2,1,0:T(8,128)} %refs_0_.1, f32[1,512,128]{2,1,0:T(8,128)} %basis.1, f32[1,128,128]{2,1,0:T(8,128)} %move.1, f32[3,1,512]{2,1,0:T(1,128)} %bitcast.11, f32[3,1,128]{2,1,0:T(1,128)} %bitcast.12, ...), custom_call_target="tpu_custom_call" | custom-call | flops 125829120 | bytes 1048576 | tf_op jit(solution)/shard_map/pallas_call | solution.py:37
  2.4 3.0 %collective-permute-start.1 = (f32[784,128]{1,0:T(8,128)}, f32[784,128]{1,0:T(8,128)S(1)}, u32[]{:S(2)}, u32[]{:S(2)}) collective-permute-start(f32[784,128]{1,0:T(8,128)} %get-tuple-element.29.refs_2_), channel_id=1, source_target_pairs={{0,2},{1,3},{2,0},{3,1},{4,6},{5,7},{6,4},{7,5},{8,10},{9,11},{10,... | collective-permute-start | bytes 1204232 | tf_op jit(solution)/shard_map/ppermute | solution.py:403
  5.4 1.5 %collective-permute-start.2 = (f32[784,128]{1,0:T(8,128)}, f32[784,128]{1,0:T(8,128)S(1)}, u32[]{:S(2)}, u32[]{:S(2)}) collective-permute-start(f32[784,128]{1,0:T(8,128)} %get-tuple-element.29.refs_2_), channel_id=1, source_target_pairs={{0,4},{1,5},{2,6},{3,7},{4,0},{5,1},{6,2},{7,3},{8,12},{9,13},{10,... | collective-permute-start | bytes 1204232 | tf_op jit(solution)/shard_map/ppermute | solution.py:403
  6.9 0.0 collective-permute-start
  6.9 1.6 %collective-permute-start.5 = (f32[784,128]{1,0:T(8,128)}, f32[784,128]{1,0:T(8,128)S(1)}, u32[]{:S(2)}, u32[]{:S(2)}) collective-permute-start(f32[784,128]{1,0:T(8,128)} %get-tuple-element.29.refs_2_), channel_id=1, source_target_pairs={{0,8},{1,9},{2,10},{3,11},{4,12},{5,13},{6,14},{7,15},{8,0},{9,1},... | collective-permute-start | bytes 1204232 | tf_op jit(solution)/shard_map/ppermute | solution.py:403
  8.5 0.7 %collective-permute-start.6 = (f32[784,128]{1,0:T(8,128)}, f32[784,128]{1,0:T(8,128)S(1)}, u32[]{:S(2)}, u32[]{:S(2)}) collective-permute-start(f32[784,128]{1,0:T(8,128)} %get-tuple-element.29.refs_2_), channel_id=1, source_target_pairs={{8,16},{9,17},{10,18},{11,19},{12,20},{13,21},{14,22},{15,23},{16,... | collective-permute-start | bytes 1204232 | tf_op jit(solution)/shard_map/ppermute | solution.py:403
  9.2 0.0 collective-permute-done.got.refs_1_.refs_2_
  9.2 0.0 copy-done.2
  9.2 0.0 copy-done.5
  9.2 0.0 copy-start.3
  9.2 0.7 %copy-done.3 = f32[64,128]{1,0:T(8,128)S(1)} copy-done((f32[64,128]{1,0:T(8,128)S(1)}, f32[64,128]{1,0:T(8,128)}, u32[]{:S(2)}) %copy-start.3) | copy-done | bytes 32792
  10.0 0.2 shard_map.146
  10.2 0.6 %collective-permute-start.3 = (f32[160,128]{1,0:T(8,128)S(1)}, f32[160,128]{1,0:T(8,128)S(1)}, u32[]{:S(2)}, u32[]{:S(2)}) collective-permute-start(f32[160,128]{1,0:T(8,128)S(1)} %get-tuple-element.31.refs_3_.refs_0_), channel_id=1, source_target_pairs={{0,2},{1,3},{2,0},{3,1},{4,6},{5,7},{6,4},{7,5},{8,10},{9,11},{10,... | collective-permute-start | bytes 245768 | tf_op jit(solution)/shard_map/ppermute | solution.py:403
  10.8 1.0 %copy-done.11 = f32[784,128]{1,0:T(8,128)S(1)} copy-done((f32[784,128]{1,0:T(8,128)S(1)}, f32[784,128]{1,0:T(8,128)}, u32[]{:S(2)}) %copy-start.11) | copy-done | bytes 401432
  11.8 1.7 %shard_map.147 = (f32[1024,128]{1,0:T(8,128)S(1)}, f32[784,128]{1,0:T(8,128)S(1)}) custom-call(s32[1]{0:T(128)} %bitcast.idx.refs_0_, f32[80,128]{1,0:T(8,128)S(1)} %collective-permute-done.got.refs_1_.refs_2_, f32[784,128]{1,0:T(8,128)S(1)} %copy-done.11, f32[160,128]{1,0:T(8,128)S(1)} %get-tuple-element.31.refs_3_.refs_0_), custom_call_target="tpu_custom_call" | custom-call | flops 805306368 | tf_op jit(solution)/shard_map/pallas_call | solution.py:37
  13.5 0.0 copy-start.7
  13.5 0.0 copy-start.10
  13.5 0.0 copy-done.4
  13.5 0.0 copy-done.6
  13.5 0.0 copy-done.8
  13.5 0.0 copy-done.9
  13.5 0.6 %copy-done.7 = f32[4,3,128]{2,0,1:T(4,128)S(1)} copy-done((f32[4,3,128]{2,0,1:T(4,128)S(1)}, f32[4,3,128]{2,0,1:T(4,128)}, u32[]{:S(2)}) %copy-start.7) | copy-done | bytes 6168
  14.1 0.0 copy-done.10
  14.2 2.5 %collective-permute-done.3.refs_1_ = f32[160,128]{1,0:T(8,128)S(1)} collective-permute-done((f32[160,128]{1,0:T(8,128)S(1)}, f32[160,128]{1,0:T(8,128)S(1)}, u32[]{:S(2)}, u32[]{:S(2)}) %collective-permute-start.3) | collective-permute-done | bytes 81952 | tf_op jit(solution)/shard_map/ppermute | solution.py:403
  16.7 0.1 collective-permute-start.7
  16.7 0.0 collective-permute-done.1.refs_1_.refs_3_.refs_5_
  16.7 0.0 collective-permute-done.2.refs_2_.refs_4_.refs_6_
  16.8 0.1 shard_map.150.refs_3_
  16.8 1.8 %collective-permute-start.4 = (f32[784,128]{1,0:T(8,128)S(1)}, f32[784,128]{1,0:T(8,128)S(1)}, u32[]{:S(2)}, u32[]{:S(2)}) collective-permute-start(f32[784,128]{1,0:T(8,128)S(1)} %shard_map.150.refs_3_), channel_id=1, source_target_pairs={{0,4},{1,3},{2,6},{3,1},{4,0},{5,7},{6,2},{7,5},{8,12},{9,11},{10,... | collective-permute-start | bytes 1204232 | tf_op jit(solution)/shard_map/ppermute | solution.py:403
  18.6 0.0 collective-permute-done.7.refs_2_
  18.6 0.2 shard_map.151
  18.9 1.9 %collective-permute-start.8 = (f32[128,128]{1,0:T(8,128)S(1)}, f32[128,128]{1,0:T(8,128)S(1)}, u32[]{:S(2)}, u32[]{:S(2)}) collective-permute-start(f32[128,128]{1,0:T(8,128)S(1)} %get-tuple-element.36.refs_6_.refs_0_), channel_id=1, source_target_pairs={{0,8},{1,9},{2,10},{3,11},{4,12},{5,13},{6,14},{7,15},{8,0},{9,1},... | collective-permute-start | bytes 196616 | tf_op jit(solution)/shard_map/ppermute | solution.py:403
  20.8 2.4 %shard_map.152.refs_2_.refs_5_ = f32[1024,128]{1,0:T(8,128)S(1)} custom-call(s32[1]{0:T(128)} %bitcast.idx.refs_0_, f32[80,128]{1,0:T(8,128)S(1)} %collective-permute-done.got.refs_1_.refs_2_, f32[784,128]{1,0:T(8,128)S(1)} %get-tuple-element.32.refs_2_.refs_3_, f32[784,128]{1,0:T(8,128)S(1)} %collective-permute-done.1.refs_1_.refs_3_.refs_5_, ...), custom_call_target="tpu_custom_call" | custom-call | flops 1610612736 | tf_op jit(solution)/shard_map/pallas_call | solution.py:37
  23.1 0.1 collective-permute-done.8.refs_1_
  23.2 0.0 collective-permute-done.5.refs_1_.refs_3_.refs_8_
  23.2 0.0 collective-permute-done.6.refs_2_.refs_4_.refs_9_
  23.3 0.1 shard_map.154
  23.4 1.6 %collective-permute-start.10 = (f32[784,128]{1,0:T(8,128)S(1)}, f32[784,128]{1,0:T(8,128)S(1)}, u32[]{:S(2)}, u32[]{:S(2)}) collective-permute-start(f32[784,128]{1,0:T(8,128)S(1)} %get-tuple-element.37.refs_6_), channel_id=1, source_target_pairs={{0,2},{1,3},{2,0},{3,1},{4,6},{5,7},{6,4},{7,5},{8,10},{9,11},{10,... | collective-permute-start | bytes 1204232 | tf_op jit(solution)/shard_map/ppermute | solution.py:403
  24.9 1.2 %collective-permute-start.11 = (f32[784,128]{1,0:T(8,128)S(1)}, f32[784,128]{1,0:T(8,128)S(1)}, u32[]{:S(2)}, u32[]{:S(2)}) collective-permute-start(f32[784,128]{1,0:T(8,128)S(1)} %get-tuple-element.38), channel_id=1, source_target_pairs={{0,4},{1,5},{2,6},{3,7},{4,0},{5,1},{6,2},{7,3},{8,12},{9,13},{10,... | collective-permute-start | bytes 1204232 | tf_op jit(solution)/shard_map/ppermute | solution.py:403
  26.1 2.6 %collective-permute-start.12 = (f32[256,128]{1,0:T(8,128)S(1)}, f32[256,128]{1,0:T(8,128)S(1)}, u32[]{:S(2)}, u32[]{:S(2)}) collective-permute-start(f32[256,128]{1,0:T(8,128)S(1)} %shard_map.153.refs_3_), channel_id=1, source_target_pairs={{0,16},{1,17},{2,18},{3,19},{4,20},{5,21},{6,22},{7,23},{8,24},{9,... | collective-permute-start | bytes 393224 | tf_op jit(solution)/shard_map/ppermute | solution.py:403
  28.7 2.4 %shard_map.155.refs_1_.refs_7_.refs_6_ = f32[1024,128]{1,0:T(8,128)S(1)} custom-call(s32[1]{0:T(128)} %bitcast.idx.refs_0_, f32[80,128]{1,0:T(8,128)S(1)} %collective-permute-done.got.refs_1_.refs_2_, f32[784,128]{1,0:T(8,128)S(1)} %get-tuple-element.32.refs_2_.refs_3_, f32[784,128]{1,0:T(8,128)S(1)} %collective-permute-done.5.refs_1_.refs_3_.refs_8_, ...), custom_call_target="tpu_custom_call" | custom-call | flops 1610612736 | tf_op jit(solution)/shard_map/pallas_call | solution.py:37
  31.1 0.0 collective-permute-done.4.refs_0_.refs_3_.refs_7_
  31.1 3.7 %collective-permute-start.9 = (f32[784,128]{1,0:T(8,128)S(1)}, f32[784,128]{1,0:T(8,128)S(1)}, u32[]{:S(2)}, u32[]{:S(2)}) collective-permute-start(f32[784,128]{1,0:T(8,128)S(1)} %shard_map.156), channel_id=1, source_target_pairs={{0,8},{1,9},{2,10},{3,11},{8,16},{9,17},{10,18},{11,19},{12,4},{13... | collective-permute-start | bytes 1204232 | tf_op jit(solution)/shard_map/ppermute | solution.py:403
  34.8 0.0 collective-permute-done.12.refs_4_
  34.8 1.7 %shard_map.157 = (f32[256,128]{1,0:T(8,128)S(1)}, f32[256,128]{1,0:T(8,128)S(1)}) custom-call(s32[1]{0:T(128)} %bitcast.idx.refs_0_, s32[8,8]{1,0:T(8,128)S(1)} %get-tuple-element.39.refs_1_, s32[4,8]{1,0:T(4,128)S(1)} %get-tuple-element.40.refs_2_, f32[256,128]{1,0:T(8,128)S(1)} %shard_map.153.refs_3_, f32[256,128]{1,0:T(8,128)S(1)} %collective-permute-done.12.refs_4_, ...), custom_call_target="tpu_custom_call" | custom-call | flops 301989888 | tf_op jit(solution)/shard_map/pallas_call | solution.py:37
  36.5 0.1 collective-permute-start.14
  36.6 0.0 collective-permute-done.10.refs_4_.refs_10_
  36.6 0.0 collective-permute-done.11.refs_5_.refs_11_
  36.6 3.4 %shard_map.158.refs_12_.refs_4_ = f32[1024,128]{1,0:T(8,128)S(1)} custom-call(s32[1]{0:T(128)} %bitcast.idx.refs_0_, f32[80,128]{1,0:T(8,128)S(1)} %collective-permute-done.got.refs_1_.refs_2_, f32[784,128]{1,0:T(8,128)S(1)} %get-tuple-element.32.refs_2_.refs_3_, f32[784,128]{1,0:T(8,128)S(1)} %collective-permute-done.4.refs_0_.refs_3_.refs_7_, ...), custom_call_target="tpu_custom_call" | custom-call | flops 2415919104 | tf_op jit(solution)/shard_map/pallas_call | solution.py:37
  40.0 2.3 %shard_map.159.refs_5_.refs_8_ = f32[384,128]{1,0:T(8,128)S(1)} custom-call(s32[1]{0:T(128)} %bitcast.idx.refs_0_, s32[8,16]{1,0:T(8,128)S(1)} %get-tuple-element.35.refs_3_.refs_1_, f32[80,128]{1,0:T(8,128)S(1)} %collective-permute-done.got.refs_1_.refs_2_, f32[784,128]{1,0:T(8,128)S(1)} %get-tuple-element.32.refs_2_.refs_3_, ...), custom_call_target="tpu_custom_call" | custom-call | flops 314572800 | tf_op jit(solution)/shard_map/pallas_call | solution.py:37
  42.4 0.0 collective-permute-done.9.refs_3_.refs_9_
  42.4 1.4 %shard_map.160 = (f32[512,128]{1,0:T(8,128)S(1)}, f32[512,128]{1,0:T(8,128)S(1)}) custom-call(s32[1]{0:T(128)} %bitcast.idx.refs_0_, f32[80,128]{1,0:T(8,128)S(1)} %collective-permute-done.got.refs_1_.refs_2_, f32[784,128]{1,0:T(8,128)S(1)} %get-tuple-element.32.refs_2_.refs_3_, f32[784,128]{1,0:T(8,128)S(1)} %collective-permute-done.9.refs_3_.refs_9_, ...), custom_call_target="tpu_custom_call" | custom-call | flops 805306368 | tf_op jit(solution)/shard_map/pallas_call | solution.py:37
  43.8 0.1 collective-permute-start.13
  43.9 0.0 collective-permute-done.14.refs_7_
  43.9 0.0 copy-start
  43.9 0.0 copy-start.1
  43.9 1.4 %shard_map.161 = (f32[256,128]{1,0:T(8,128)S(1)}, f32[256,128]{1,0:T(8,128)S(1)}) custom-call(s32[1]{0:T(128)} %bitcast.idx.refs_0_, s32[8,16]{1,0:T(8,128)S(1)} %get-tuple-element.35.refs_3_.refs_1_, f32[80,128]{1,0:T(8,128)S(1)} %collective-permute-done.got.refs_1_.refs_2_, f32[784,128]{1,0:T(8,128)S(1)} %get-tuple-element.32.refs_2_.refs_3_, ...), custom_call_target="tpu_custom_call" | custom-call | flops 352321536 | tf_op jit(solution)/shard_map/pallas_call | solution.py:37
  45.3 0.5 %collective-permute-start.15 = (f32[256,128]{1,0:T(8,128)S(1)}, f32[256,128]{1,0:T(8,128)S(1)}, u32[]{:S(2)}, u32[]{:S(2)}) collective-permute-start(f32[256,128]{1,0:T(8,128)S(1)} %get-tuple-element.50), channel_id=1, source_target_pairs={{0,1},{1,0},{2,3},{3,2},{4,5},{5,4},{6,7},{7,6},{8,9},{9,8},{10,11... | collective-permute-start | bytes 393224 | tf_op jit(solution)/shard_map/ppermute | solution.py:403
  45.9 1.0 %collective-permute-done.15.low_got = f32[256,128]{1,0:T(8,128)S(1)} collective-permute-done((f32[256,128]{1,0:T(8,128)S(1)}, f32[256,128]{1,0:T(8,128)S(1)}, u32[]{:S(2)}, u32[]{:S(2)}) %collective-permute-start.15) | collective-permute-done | bytes 131104 | tf_op jit(solution)/shard_map/ppermute | solution.py:403
  46.9 0.0 collective-permute-done.13.near_got
  46.9 0.0 copy-done
  46.9 0.0 copy-done.1
  46.9 1.2 %shard_map.162 = f32[1,512,128]{2,1,0:T(8,128)} custom-call(f32[512,128]{1,0:T(8,128)S(1)} %get-tuple-element.45.near, f32[512,128]{1,0:T(8,128)S(1)} %collective-permute-done.13.near_got, f32[256,128]{1,0:T(8,128)S(1)} %get-tuple-element.49.low, f32[256,128]{1,0:T(8,128)S(1)} %collective-permute-done.15.low_got, f32[1,128,128]{2,1,0:T(8,128)S(1)} %copy-done.1, ...), custom_call_target="tpu_custom_call" | custom-call | flops 125829120 | tf_op jit(solution)/shard_map/pallas_call | solution.py:37
  (10 shorter events, 0.1 us)
Async XLA Ops:
  0.0 9.2 %copy-start.2 = (f32[64,128]{1,0:T(8,128)S(1)}, f32[64,128]{1,0:T(8,128)}, u32[]{:S(2)}) copy-start(f32[64,128]{1,0:T(8,128)} %epair.1) | copy-start | bytes 98308
  0.0 9.2 %copy-start.5 = (f32[32,128]{1,0:T(8,128)S(1)}, f32[32,128]{1,0:T(8,128)}, u32[]{:S(2)}) copy-start(f32[32,128]{1,0:T(8,128)} %equad.1) | copy-start | bytes 49156
  2.4 14.4 %collective-permute-start.1 = (f32[784,128]{1,0:T(8,128)}, f32[784,128]{1,0:T(8,128)S(1)}, u32[]{:S(2)}, u32[]{:S(2)}) collective-permute-start(f32[784,128]{1,0:T(8,128)} %get-tuple-element.29.refs_2_), channel_id=1, source_target_pairs={{0,2},{1,3},{2,0},{3,1},{4,6},{5,7},{6,4},{7,5},{8,10},{9,11},{10,... | collective-permute-start | bytes 1204232 | tf_op jit(solution)/shard_map/ppermute | solution.py:403
  5.4 11.4 %collective-permute-start.2 = (f32[784,128]{1,0:T(8,128)}, f32[784,128]{1,0:T(8,128)S(1)}, u32[]{:S(2)}, u32[]{:S(2)}) collective-permute-start(f32[784,128]{1,0:T(8,128)} %get-tuple-element.29.refs_2_), channel_id=1, source_target_pairs={{0,4},{1,5},{2,6},{3,7},{4,0},{5,1},{6,2},{7,3},{8,12},{9,13},{10,... | collective-permute-start | bytes 1204232 | tf_op jit(solution)/shard_map/ppermute | solution.py:403
  6.9 2.3 %collective-permute-start = (f32[80,128]{1,0:T(8,128)}, f32[80,128]{1,0:T(8,128)S(1)}, u32[]{:S(2)}, u32[]{:S(2)}) collective-permute-start(f32[80,128]{1,0:T(8,128)} %get-tuple-element.28), channel_id=1, source_target_pairs={{0,1},{1,0},{2,3},{3,2},{4,5},{5,4},{6,7},{7,6},{8,9},{9,8},{10,11... | collective-permute-start | bytes 122888 | tf_op jit(solution)/shard_map/ppermute | solution.py:403
  6.9 16.3 %collective-permute-start.5 = (f32[784,128]{1,0:T(8,128)}, f32[784,128]{1,0:T(8,128)S(1)}, u32[]{:S(2)}, u32[]{:S(2)}) collective-permute-start(f32[784,128]{1,0:T(8,128)} %get-tuple-element.29.refs_2_), channel_id=1, source_target_pairs={{0,8},{1,9},{2,10},{3,11},{4,12},{5,13},{6,14},{7,15},{8,0},{9,1},... | collective-permute-start | bytes 1204232 | tf_op jit(solution)/shard_map/ppermute | solution.py:403
  8.5 14.8 %collective-permute-start.6 = (f32[784,128]{1,0:T(8,128)}, f32[784,128]{1,0:T(8,128)S(1)}, u32[]{:S(2)}, u32[]{:S(2)}) collective-permute-start(f32[784,128]{1,0:T(8,128)} %get-tuple-element.29.refs_2_), channel_id=1, source_target_pairs={{8,16},{9,17},{10,18},{11,19},{12,20},{13,21},{14,22},{15,23},{16,... | collective-permute-start | bytes 1204232 | tf_op jit(solution)/shard_map/ppermute | solution.py:403
  9.2 0.8 %copy-start.3 = (f32[64,128]{1,0:T(8,128)S(1)}, f32[64,128]{1,0:T(8,128)}, u32[]{:S(2)}) copy-start(f32[64,128]{1,0:T(8,128)} %get-tuple-element.30.keep) | copy-start | bytes 98308
  10.2 6.5 %collective-permute-start.3 = (f32[160,128]{1,0:T(8,128)S(1)}, f32[160,128]{1,0:T(8,128)S(1)}, u32[]{:S(2)}, u32[]{:S(2)}) collective-permute-start(f32[160,128]{1,0:T(8,128)S(1)} %get-tuple-element.31.refs_3_.refs_0_), channel_id=1, source_target_pairs={{0,2},{1,3},{2,0},{3,1},{4,6},{5,7},{6,4},{7,5},{8,10},{9,11},{10,... | collective-permute-start | bytes 245768 | tf_op jit(solution)/shard_map/ppermute | solution.py:403
  10.8 1.0 %copy-start.11 = (f32[784,128]{1,0:T(8,128)S(1)}, f32[784,128]{1,0:T(8,128)}, u32[]{:S(2)}) copy-start(f32[784,128]{1,0:T(8,128)} %get-tuple-element.29.refs_2_) | copy-start | bytes 1204228
  11.8 1.7 %copy-start.4 = (f32[16,3,128]{2,0,1:T(8,128)S(1)}, f32[16,3,128]{2,0,1:T(8,128)}, u32[]{:S(2)}) copy-start(f32[16,3,128]{2,0,1:T(8,128)} %param.22) | copy-start | bytes 73732
  11.8 1.7 %copy-start.6 = (f32[8,3,128]{2,0,1:T(8,128)S(1)}, f32[8,3,128]{2,0,1:T(8,128)}, u32[]{:S(2)}) copy-start(f32[8,3,128]{2,0,1:T(8,128)} %param.23) | copy-start | bytes 36868
  11.8 1.7 %copy-start.8 = (s32[16,8]{0,1:T(8,128)S(1)}, s32[16,8]{0,1:T(8,128)}, u32[]{:S(2)}) copy-start(s32[16,8]{0,1:T(8,128)} %param.27) | copy-start | bytes 1540
  11.8 1.7 %copy-start.9 = (s32[8,8]{1,0:T(8,128)S(1)}, s32[8,8]{1,0:T(8,128)}, u32[]{:S(2)}) copy-start(s32[8,8]{1,0:T(8,128)} %refs_1_.3) | copy-start | bytes 772
  13.5 0.7 %copy-start.7 = (f32[4,3,128]{2,0,1:T(4,128)S(1)}, f32[4,3,128]{2,0,1:T(4,128)}, u32[]{:S(2)}) copy-start(f32[4,3,128]{2,0,1:T(4,128)} %param.24) | copy-start | bytes 18436
  13.5 0.7 %copy-start.10 = (s32[4,8]{1,0:T(4,128)S(1)}, s32[4,8]{1,0:T(4,128)}, u32[]{:S(2)}) copy-start(s32[4,8]{1,0:T(4,128)} %refs_2_.3) | copy-start | bytes 388
  16.7 2.0 %collective-permute-start.7 = (f32[256,128]{1,0:T(8,128)S(1)}, f32[256,128]{1,0:T(8,128)S(1)}, u32[]{:S(2)}, u32[]{:S(2)}) collective-permute-start(f32[256,128]{1,0:T(8,128)S(1)} %shard_map.149.refs_3_.refs_1_), channel_id=1, source_target_pairs={{0,1},{1,0},{2,3},{3,2},{4,5},{5,4},{6,7},{7,6},{8,9},{9,8},{10,11... | collective-permute-start | bytes 393224 | tf_op jit(solution)/shard_map/ppermute | solution.py:403
  16.8 14.3 %collective-permute-start.4 = (f32[784,128]{1,0:T(8,128)S(1)}, f32[784,128]{1,0:T(8,128)S(1)}, u32[]{:S(2)}, u32[]{:S(2)}) collective-permute-start(f32[784,128]{1,0:T(8,128)S(1)} %shard_map.150.refs_3_), channel_id=1, source_target_pairs={{0,4},{1,3},{2,6},{3,1},{4,0},{5,7},{6,2},{7,5},{8,12},{9,11},{10,... | collective-permute-start | bytes 1204232 | tf_op jit(solution)/shard_map/ppermute | solution.py:403
  18.9 4.3 %collective-permute-start.8 = (f32[128,128]{1,0:T(8,128)S(1)}, f32[128,128]{1,0:T(8,128)S(1)}, u32[]{:S(2)}, u32[]{:S(2)}) collective-permute-start(f32[128,128]{1,0:T(8,128)S(1)} %get-tuple-element.36.refs_6_.refs_0_), channel_id=1, source_target_pairs={{0,8},{1,9},{2,10},{3,11},{4,12},{5,13},{6,14},{7,15},{8,0},{9,1},... | collective-permute-start | bytes 196616 | tf_op jit(solution)/shard_map/ppermute | solution.py:403
  23.4 13.2 %collective-permute-start.10 = (f32[784,128]{1,0:T(8,128)S(1)}, f32[784,128]{1,0:T(8,128)S(1)}, u32[]{:S(2)}, u32[]{:S(2)}) collective-permute-start(f32[784,128]{1,0:T(8,128)S(1)} %get-tuple-element.37.refs_6_), channel_id=1, source_target_pairs={{0,2},{1,3},{2,0},{3,1},{4,6},{5,7},{6,4},{7,5},{8,10},{9,11},{10,... | collective-permute-start | bytes 1204232 | tf_op jit(solution)/shard_map/ppermute | solution.py:403
  24.9 11.7 %collective-permute-start.11 = (f32[784,128]{1,0:T(8,128)S(1)}, f32[784,128]{1,0:T(8,128)S(1)}, u32[]{:S(2)}, u32[]{:S(2)}) collective-permute-start(f32[784,128]{1,0:T(8,128)S(1)} %get-tuple-element.38), channel_id=1, source_target_pairs={{0,4},{1,5},{2,6},{3,7},{4,0},{5,1},{6,2},{7,3},{8,12},{9,13},{10,... | collective-permute-start | bytes 1204232 | tf_op jit(solution)/shard_map/ppermute | solution.py:403
  26.1 8.7 %collective-permute-start.12 = (f32[256,128]{1,0:T(8,128)S(1)}, f32[256,128]{1,0:T(8,128)S(1)}, u32[]{:S(2)}, u32[]{:S(2)}) collective-permute-start(f32[256,128]{1,0:T(8,128)S(1)} %shard_map.153.refs_3_), channel_id=1, source_target_pairs={{0,16},{1,17},{2,18},{3,19},{4,20},{5,21},{6,22},{7,23},{8,24},{9,... | collective-permute-start | bytes 393224 | tf_op jit(solution)/shard_map/ppermute | solution.py:403
  31.1 11.3 %collective-permute-start.9 = (f32[784,128]{1,0:T(8,128)S(1)}, f32[784,128]{1,0:T(8,128)S(1)}, u32[]{:S(2)}, u32[]{:S(2)}) collective-permute-start(f32[784,128]{1,0:T(8,128)S(1)} %shard_map.156), channel_id=1, source_target_pairs={{0,8},{1,9},{2,10},{3,11},{8,16},{9,17},{10,18},{11,19},{12,4},{13... | collective-permute-start | bytes 1204232 | tf_op jit(solution)/shard_map/ppermute | solution.py:403
  36.5 7.4 %collective-permute-start.14 = (f32[256,128]{1,0:T(8,128)S(1)}, f32[256,128]{1,0:T(8,128)S(1)}, u32[]{:S(2)}, u32[]{:S(2)}) collective-permute-start(f32[256,128]{1,0:T(8,128)S(1)} %get-tuple-element.48), channel_id=1, source_target_pairs={{0,4},{1,5},{2,6},{3,7},{4,0},{5,1},{6,2},{7,3},{8,12},{9,13},{10,... | collective-permute-start | bytes 393224 | tf_op jit(solution)/shard_map/ppermute | solution.py:403
  43.8 3.0 %collective-permute-start.13 = (f32[512,128]{1,0:T(8,128)S(1)}, f32[512,128]{1,0:T(8,128)S(1)}, u32[]{:S(2)}, u32[]{:S(2)}) collective-permute-start(f32[512,128]{1,0:T(8,128)S(1)} %get-tuple-element.46.refs_10_), channel_id=1, source_target_pairs={{0,1},{1,0},{2,3},{3,2},{4,5},{5,4},{6,7},{7,6},{8,9},{9,8},{10,11... | collective-permute-start | bytes 786440 | tf_op jit(solution)/shard_map/ppermute | solution.py:403
  43.9 3.0 %copy-start = (f32[1,512,128]{2,1,0:T(8,128)S(1)}, f32[1,512,128]{2,1,0:T(8,128)}, u32[]{:S(2)}) copy-start(f32[1,512,128]{2,1,0:T(8,128)} %basis.1) | copy-start | bytes 786436
  43.9 2.9 %copy-start.1 = (f32[1,128,128]{2,1,0:T(8,128)S(1)}, f32[1,128,128]{2,1,0:T(8,128)}, u32[]{:S(2)}) copy-start(f32[1,128,128]{2,1,0:T(8,128)} %move.1) | copy-start | bytes 196612
  45.3 1.5 %collective-permute-start.15 = (f32[256,128]{1,0:T(8,128)S(1)}, f32[256,128]{1,0:T(8,128)S(1)}, u32[]{:S(2)}, u32[]{:S(2)}) collective-permute-start(f32[256,128]{1,0:T(8,128)S(1)} %get-tuple-element.50), channel_id=1, source_target_pairs={{0,1},{1,0},{2,3},{3,2},{4,5},{5,4},{6,7},{7,6},{8,9},{9,8},{10,11... | collective-permute-start | bytes 393224 | tf_op jit(solution)/shard_map/ppermute | solution.py:403
